TPU v7x, 32 devices: a whole 2x2x4 slice. The times are simulated.
32 devices in a mesh: wide: 8 (over z, x), narrow: 4 (over y, core).
Axes of the slice: x: 2, y: 2, z: 4, core: 2. Of those that a mesh axis runs over, the one named last changes fastest.
Arguments:
- tokens: bfloat16 [24576, 1024], P(('wide', 'narrow')), may hold values from -6 to 6
- cotangent: bfloat16 [24576, 1024], P(('wide', 'narrow')), may hold values from -6 to 6
- lengths: int32 [8], P('wide'), may hold values from 2305 to 3072, as said below
- owners: int32 [192], replicated, may hold values from 0 to 31, as said below
- w_qkv: float32 [4, 256, 3072], P(None, ('wide', 'narrow')), may hold values from -0.125 to 0.125
- w_out: float32 [4, 256, 1024], P(None, ('wide', 'narrow')), may hold values from -2.5 to 2.5
- w_up: float32 [4, 256, 4096], P(None, ('wide', 'narrow')), may hold values from -0.1875 to 0.1875
- w_down: float32 [16, 256, 1024], P(None, ('wide', 'narrow')), may hold values from -0.09375 to 0.09375
- norm_gains: float32 [2, 1024], P(None, ('wide', 'narrow')), may hold values from 0.5 to 3.5
- gain_first: float32 [2, 1024], P(None, ('wide', 'narrow')), may hold values from -0.01171875 to 0.01171875
- gain_second: float32 [2, 1024], P(None, ('wide', 'narrow')), may hold values from 7.151393e-07 to 2.8605573e-06
- moment_first: float32 [192, 256, 256], P(('wide', 'narrow')), may hold values from -0.00390625 to 0.00390625
- moment_second: float32 [192, 256, 256], P(('wide', 'narrow')), may hold values from 7.945993e-08 to 3.1783972e-07
- left_stat: float32 [192, 256, 256], P(('wide', 'narrow')), as said below
- right_stat: float32 [192, 256, 256], P(('wide', 'narrow')), as said below
- left_basis: float32 [192, 256, 256], P(('wide', 'narrow')), may hold values from -1 to 1, as said below
- right_basis: float32 [192, 256, 256], P(('wide', 'narrow')), may hold values from -1 to 1, as said below
Outputs:
- block_out: bfloat16 [24576, 1024], P(('wide', 'narrow'))
- grad_tokens: bfloat16 [24576, 1024], P(('wide', 'narrow'))
- grad_norm: float32 [], replicated
- new_qkv: float32 [4, 256, 3072], P(None, ('wide', 'narrow'))
- new_out: float32 [4, 256, 1024], P(None, ('wide', 'narrow'))
- new_up: float32 [4, 256, 4096], P(None, ('wide', 'narrow'))
- new_down: float32 [16, 256, 1024], P(None, ('wide', 'narrow'))
- gain_values: float32 [2, 1024], P(None, ('wide', 'narrow'))
- gain_first_new: float32 [2, 1024], P(None, ('wide', 'narrow'))
- gain_second_new: float32 [2, 1024], P(None, ('wide', 'narrow'))
- moment_first_new: float32 [192, 256, 256], P(('wide', 'narrow'))
- moment_second_new: float32 [192, 256, 256], P(('wide', 'narrow'))
- left_stat_new: float32 [192, 256, 256], P(('wide', 'narrow'))
- right_stat_new: float32 [192, 256, 256], P(('wide', 'narrow'))
- left_basis_new: float32 [192, 256, 256], P(('wide', 'narrow'))
- right_basis_new: float32 [192, 256, 256], P(('wide', 'narrow'))
Inputs may be any that keep to these rules, and one draw needn't show every extreme that they name: `lengths`: some scene has all 3072 tokens valid. `owners`: no device owns more than 6 blocks, and some device owns exactly 6. `left_stat`: each slot's statistics are symmetric positive definite. `right_stat`: each slot's statistics are symmetric positive definite. `left_basis`: each slot's basis is orthogonal. `right_basis`: each slot's basis is orthogonal.
All inputs are finite; a program needn't handle non-finite values.
Results may differ from a plain program's by a relative error of at most 0.017.
The roundings to bfloat16 on the way count: a program that leaves them out, or rounds other values in their place, can miss the bound.
Values may be sent and summed in bfloat16 or wider, within the bound.
A program may use at most 256 MiB of HBM per device.

v0:
```python
from functools import partial

import jax
import jax.numpy as jnp
from jax import lax
from jax.sharding import PartitionSpec as P

FF = 4096
HEADS = 16
HEAD = 64
BLOCK = 256
STEP = 10


eps_norm = 1e-05
eps_adam = 1e-08
decay_rate = 0.5
clip_bound = 1.0
weight_decay = 0.01
gain_rate = 1.0
neg_large = -1e30
highest = lax.Precision.HIGHEST


def shortened(shard):
    return jax.tree.map(lambda a: a.astype(jnp.bfloat16) if a.dtype == jnp.float32 else a, shard)


def normalize(values):
    center = values - jnp.mean(values, -1, keepdims=True)
    inverse = lax.rsqrt(jnp.mean(center * center, -1, keepdims=True) + eps_norm)
    return (center * inverse, inverse)


def norm_backward(d_result, normed, inverse, gain):
    scaled = d_result * gain
    d_gain = jnp.sum(d_result * normed, 0)
    d_input = inverse * (
        scaled
        - jnp.mean(scaled, -1, keepdims=True)
        - normed * jnp.mean(scaled * normed, -1, keepdims=True)
    )
    return (d_input, d_gain)


def split_heads(matrix):
    return matrix.reshape(matrix.shape[0], HEADS, HEAD).transpose(1, 0, 2)


def join_heads(stacked):
    return stacked.transpose(1, 0, 2).reshape(stacked.shape[1], HEADS * HEAD)


def as_layout(matrix):
    return matrix.reshape(matrix.shape[0] // BLOCK, BLOCK, matrix.shape[1])


def to_pieces(shard):
    band_count, band_rows, col_count = shard.shape
    return (
        shard.reshape(band_count, band_rows, col_count // BLOCK, BLOCK)
        .transpose(0, 2, 1, 3)
        .reshape(-1, band_rows, BLOCK)
    )


def from_pieces(pieces, band_count, col_count):
    band_rows = pieces.shape[1]
    return (
        pieces.reshape(band_count, col_count // BLOCK, band_rows, BLOCK)
        .transpose(0, 2, 1, 3)
        .reshape(band_count, band_rows, col_count)
    )


def masked_scores(visible, score_scale, queries, keyset):
    scores = (
        jnp.einsum("te,se->ts", queries, keyset, preferred_element_type=jnp.float32) * score_scale
    )
    return jnp.where(visible[None, :], scores, neg_large)


def attend_head(visible, score_scale, parts):
    queries, keyset, valueset = parts
    scores = masked_scores(visible, score_scale, queries, keyset)
    topmost = jnp.max(scores, -1, keepdims=True)
    expo_vals = jnp.exp(scores - topmost)
    totals = jnp.sum(expo_vals, -1, keepdims=True)
    attn_probs = expo_vals / totals
    mixed = jnp.dot(attn_probs.astype(jnp.bfloat16), valueset, preferred_element_type=jnp.float32)
    return (mixed, (topmost + jnp.log(totals))[:, 0])


def head_backward(visible, score_scale, parts):
    queries, keyset, valueset, d_mixed, log_total = parts
    scores = masked_scores(visible, score_scale, queries, keyset)
    attn_probs = jnp.exp(scores - log_total[:, None])
    d_probs = jnp.einsum("te,se->ts", d_mixed, valueset, preferred_element_type=jnp.float32)
    d_values = jnp.einsum(
        "ts,te->se", attn_probs.astype(jnp.bfloat16), d_mixed, preferred_element_type=jnp.float32
    )
    inner = jnp.sum(attn_probs * d_probs, -1, keepdims=True)
    d_scores = (attn_probs * (d_probs - inner)).astype(jnp.bfloat16)
    d_queries = jnp.dot(d_scores, keyset, preferred_element_type=jnp.float32) * score_scale
    d_keys = (
        jnp.einsum("ts,te->se", d_scores, queries, preferred_element_type=jnp.float32) * score_scale
    )
    return (d_queries, d_keys, d_values)


def batched(spec, left, right):
    return jnp.einsum(spec, left, right, precision=highest)


def renew_basis(stat, basis):
    turned = batched("sij,sjk->sik", stat, basis)
    gram_matrix = batched("sji,sjk->sik", turned, turned)
    factor_low = jnp.linalg.cholesky(gram_matrix)
    solved = jax.scipy.linalg.solve_triangular(factor_low, turned.transpose(0, 2, 1), lower=True)
    return solved.transpose(0, 2, 1)


def soap_update(gradient, first_old, second_old, left_old, right_old, left_base, right_base):
    left_new = decay_rate * left_old + (1.0 - decay_rate) * batched(
        "sij,skj->sik", gradient, gradient
    )
    right_new = decay_rate * right_old + (1.0 - decay_rate) * batched(
        "sji,sjk->sik", gradient, gradient
    )
    turned = batched("sji,sjk->sik", left_base, batched("sij,sjk->sik", gradient, right_base))
    first_new = decay_rate * first_old + (1.0 - decay_rate) * turned
    second_new = decay_rate * second_old + (1.0 - decay_rate) * turned * turned
    correct = 1.0 - decay_rate**STEP
    direction = first_new / correct / (jnp.sqrt(second_new / correct) + eps_adam)
    restored = batched("sij,sjk->sik", left_base, batched("sij,skj->sik", direction, right_base))
    return (
        restored,
        first_new,
        second_new,
        left_new,
        right_new,
        renew_basis(left_new, left_base),
        renew_basis(right_new, right_base),
    )


def unpack(gathered):
    matrices = [
        layout.reshape(layout.shape[0] * layout.shape[1], layout.shape[2])
        for layout in gathered[:4]
    ]
    return (matrices, gathered[4].astype(jnp.float32))


def global_norm(squares):
    return jnp.sqrt(lax.psum(squares, ("wide", "narrow")))


def body(
    tokens,
    cotangent,
    lengths,
    owners,
    w_qkv,
    w_out,
    w_up,
    w_down,
    norm_gains,
    gain_first,
    gain_second,
    moment_first,
    moment_second,
    left_stat,
    right_stat,
    left_basis,
    right_basis,
):
    tok_rows, width = tokens.shape
    narrow_count = lax.axis_size("narrow")
    device_count = lax.axis_size("wide") * narrow_count
    seq_len = tok_rows * narrow_count
    cap_slots = moment_first.shape[0]
    score_scale = HEAD ** (-0.5)
    masters = (w_qkv, w_out, w_up, w_down)
    lowered = tuple((layout.astype(jnp.bfloat16) for layout in masters)) + (
        norm_gains.astype(jnp.bfloat16),
    )
    weight_list, gain_pair = unpack(
        jax.tree.map(
            lambda part, own: part.astype(own.dtype),
            lax.all_gather(shortened(lowered), ("wide", "narrow"), axis=1, tiled=True),
            lowered,
        )
    )
    w_attn, w_proj, w_hidden, w_back = weight_list
    inputs = tokens.astype(jnp.float32)
    normed_one, inverse_one = normalize(inputs)
    act_one = (normed_one * gain_pair[0]).astype(jnp.bfloat16)
    packed = jnp.dot(act_one, w_attn, preferred_element_type=jnp.float32).astype(jnp.bfloat16)
    queries = packed[:, :width]
    keyset, valueset = (
        lax.all_gather(packed[:, width : 2 * width], "narrow", axis=0, tiled=True),
        lax.all_gather(packed[:, 2 * width :], "narrow", axis=0, tiled=True),
    )
    visible = lax.iota(jnp.int32, seq_len) < lengths[0]
    head_parts = (split_heads(queries), split_heads(keyset), split_heads(valueset))
    mixed, log_totals = lax.map(partial(attend_head, visible, score_scale), head_parts)
    merged = join_heads(mixed).astype(jnp.bfloat16)
    middle = inputs + jnp.dot(merged, w_proj, preferred_element_type=jnp.float32)
    normed_two, inverse_two = normalize(middle)
    act_two = (normed_two * gain_pair[1]).astype(jnp.bfloat16)
    hidden = jnp.dot(act_two, w_hidden, preferred_element_type=jnp.float32)
    active = jax.nn.gelu(hidden, approximate=True).astype(jnp.bfloat16)
    block_out = (middle + jnp.dot(active, w_back, preferred_element_type=jnp.float32)).astype(
        jnp.bfloat16
    )
    weight_list, gain_pair = unpack(
        jax.tree.map(
            lambda part, own: part.astype(own.dtype),
            lax.all_gather(shortened(lowered), ("wide", "narrow"), axis=1, tiled=True),
            lowered,
        )
    )
    w_attn, w_proj, w_hidden, w_back = weight_list
    d_back = jnp.einsum("tf,td->fd", active, cotangent, preferred_element_type=jnp.float32)
    d_active = jnp.einsum("td,fd->tf", cotangent, w_back, preferred_element_type=jnp.float32)
    _, gelu_pull = jax.vjp(partial(jax.nn.gelu, approximate=True), hidden)
    d_hidden = gelu_pull(d_active)[0].astype(jnp.bfloat16)
    d_w_hidden = jnp.einsum("td,tf->df", act_two, d_hidden, preferred_element_type=jnp.float32)
    d_act_two = jnp.einsum("tf,df->td", d_hidden, w_hidden, preferred_element_type=jnp.float32)
    d_norm_two, d_gain_two = norm_backward(d_act_two, normed_two, inverse_two, gain_pair[1])
    d_middle = cotangent.astype(jnp.float32) + d_norm_two
    mlp_sums = (
        lax.psum_scatter(
            as_layout(d_w_hidden), ("wide", "narrow"), scatter_dimension=1, tiled=True
        ),
        lax.psum_scatter(as_layout(d_back), ("wide", "narrow"), scatter_dimension=1, tiled=True),
    )
    d_branch = d_middle.astype(jnp.bfloat16)
    d_proj = jnp.einsum("td,te->de", merged, d_branch, preferred_element_type=jnp.float32)
    d_merged = jnp.einsum("te,de->td", d_branch, w_proj, preferred_element_type=jnp.float32).astype(
        jnp.bfloat16
    )
    back_parts = head_parts + (split_heads(d_merged), log_totals)
    d_queries, d_keys, d_values = lax.map(partial(head_backward, visible, score_scale), back_parts)
    key_sums = (
        lax.psum_scatter(
            join_heads(d_keys).astype(jnp.bfloat16), "narrow", scatter_dimension=0, tiled=True
        ).astype(jnp.float32),
        lax.psum_scatter(
            join_heads(d_values).astype(jnp.bfloat16), "narrow", scatter_dimension=0, tiled=True
        ).astype(jnp.float32),
    )
    key_grad, value_grad = (key_sums[0], key_sums[1])
    d_packed = jnp.concatenate([join_heads(d_queries), key_grad, value_grad], 1).astype(
        jnp.bfloat16
    )
    d_attn = jnp.einsum("td,te->de", act_one, d_packed, preferred_element_type=jnp.float32)
    d_act_one = jnp.einsum("te,de->td", d_packed, w_attn, preferred_element_type=jnp.float32)
    d_norm_one, d_gain_one = norm_backward(d_act_one, normed_one, inverse_one, gain_pair[0])
    grad_tokens = (d_middle + d_norm_one).astype(jnp.bfloat16)
    attn_sums = (
        lax.psum_scatter(as_layout(d_attn), ("wide", "narrow"), scatter_dimension=1, tiled=True),
        lax.psum_scatter(as_layout(d_proj), ("wide", "narrow"), scatter_dimension=1, tiled=True),
        lax.psum_scatter(
            jnp.stack([d_gain_one, d_gain_two]), ("wide", "narrow"), scatter_dimension=1, tiled=True
        ),
    )
    grad_shards = (attn_sums[0], attn_sums[1], mlp_sums[0], mlp_sums[1])
    gain_grad = attn_sums[2]
    local_squares = jnp.sum(gain_grad * gain_grad) + sum(
        (jnp.sum(shard * shard) for shard in grad_shards)
    )
    pieces = jnp.concatenate([to_pieces(shard) for shard in grad_shards], 0)
    block_count = pieces.shape[0]
    order = lax.iota(jnp.int32, block_count)
    earlier = (owners[None, :] == owners[:, None]) & (order[None, :] < order[:, None])
    slots = owners * cap_slots + jnp.sum(earlier.astype(jnp.int32), 1)
    routing = (slots[None, :] == lax.iota(jnp.int32, device_count * cap_slots)[:, None]).astype(
        jnp.float32
    )
    routing = routing.reshape(device_count, cap_slots, block_count)
    grad_norm = global_norm(local_squares)
    factor = jnp.minimum(1.0, clip_bound / grad_norm)
    outgoing = pieces * factor
    arrived = lax.all_to_all(
        jnp.einsum("okb,bxy->koxy", routing, outgoing, precision=highest).astype(jnp.bfloat16),
        ("wide", "narrow"),
        split_axis=1,
        concat_axis=1,
        tiled=True,
    ).astype(jnp.float32)
    slot_grads = arrived.reshape(cap_slots, BLOCK, BLOCK)
    restored, first_new, second_new, left_new, right_new, left_turn, right_turn = soap_update(
        slot_grads, moment_first, moment_second, left_stat, right_stat, left_basis, right_basis
    )
    returned = lax.all_to_all(
        shortened(restored.reshape(cap_slots, device_count, -1, BLOCK)),
        ("wide", "narrow"),
        split_axis=1,
        concat_axis=1,
        tiled=True,
    )
    back_pieces = jnp.einsum("okb,koxy->bxy", routing, returned, precision=highest)
    fan_list = (2 * width, max(1, width * 16 // seq_len), width, FF)
    updated = []
    offset = 0
    for master, fan_in in zip(masters, fan_list):
        band_count, band_rows, col_count = master.shape
        piece_count = band_count * (col_count // BLOCK)
        direction = from_pieces(back_pieces[offset : offset + piece_count], band_count, col_count)
        updated.append(master - fan_in ** (-0.5) * (direction + weight_decay * master))
        offset += piece_count
    clipped = gain_grad * factor
    gain_one_new = decay_rate * gain_first + (1.0 - decay_rate) * clipped
    gain_two_new = decay_rate * gain_second + (1.0 - decay_rate) * clipped * clipped
    correct = 1.0 - decay_rate**STEP
    gain_values = norm_gains - gain_rate * (gain_one_new / correct) / (
        jnp.sqrt(gain_two_new / correct) + eps_adam
    )
    return (
        block_out,
        grad_tokens,
        grad_norm,
        updated[0],
        updated[1],
        updated[2],
        updated[3],
        gain_values,
        gain_one_new,
        gain_two_new,
        first_new,
        second_new,
        left_new,
        right_new,
        left_turn,
        right_turn,
    )


def solution(mesh):
    in_specs = (
        P(("wide", "narrow"), None),
        P(("wide", "narrow"), None),
        P("wide"),
        P(),
        P(None, ("wide", "narrow"), None),
        P(None, ("wide", "narrow"), None),
        P(None, ("wide", "narrow"), None),
        P(None, ("wide", "narrow"), None),
        P(None, ("wide", "narrow")),
        P(None, ("wide", "narrow")),
        P(None, ("wide", "narrow")),
        P(("wide", "narrow"), None, None),
        P(("wide", "narrow"), None, None),
        P(("wide", "narrow"), None, None),
        P(("wide", "narrow"), None, None),
        P(("wide", "narrow"), None, None),
        P(("wide", "narrow"), None, None),
    )
    out_specs = (
        P(("wide", "narrow"), None),
        P(("wide", "narrow"), None),
        P(),
        P(None, ("wide", "narrow"), None),
        P(None, ("wide", "narrow"), None),
        P(None, ("wide", "narrow"), None),
        P(None, ("wide", "narrow"), None),
        P(None, ("wide", "narrow")),
        P(None, ("wide", "narrow")),
        P(None, ("wide", "narrow")),
        P(("wide", "narrow"), None, None),
        P(("wide", "narrow"), None, None),
        P(("wide", "narrow"), None, None),
        P(("wide", "narrow"), None, None),
        P(("wide", "narrow"), None, None),
        P(("wide", "narrow"), None, None),
    )
    return jax.shard_map(body, mesh=mesh, in_specs=in_specs, out_specs=out_specs, check_vma=False)
```

profile of v0, /device:TPU:0, one launch (start us, length us, event | category | flops | bytes accessed | tf_op | source)
XLA Modules:
  0.0 2856.3 jit_solution(5572822229467778894)
XLA Ops:
  11.7 43.2 %all-gather = bf16[32,32,2]{1,2,0:T(2,128)(2,1)S(1)} all-gather(bf16[1,32,2]{1,2,0:T(2,128)(2,1)S(1)} %convert_bitcast_fusion), channel_id=1, replica_groups=mesh['wide'=8,'narrow'=4] {'wide','narrow'}, dimensions={0}, use_global_device_ids=true | all-gather | bytes 4224 | tf_op jit(solution)/shard_map/all_gather | solution.py:191
  57.9 26.0 all-gather.8.cloned.1.call-done
  105.0 58.6 %all-gather.18.cloned.1.call-done = bf16[16,256,1024]{2,1,0:T(8,128)(2,1)} async-done(((bf16[16,8,1024]{2,1,0:T(8,128)(2,1)}), bf16[16,256,1024]{2,1,0:T(8,128)(2,1)}) %all-gather.18.cloned.1.call-update) | async-done | bytes 8388624 | tf_op jit(solution)/shard_map/all_gather | solution.py:191
  176.4 35.0 %all-gather.10.cloned.1.call-done = bf16[3072,1024]{1,0:T(8,128)(2,1)} async-done(((bf16[768,1024]{1,0:T(8,128)(2,1)}), bf16[3072,1024]{1,0:T(8,128)(2,1)}) %all-gather.10.cloned.1.call-update) | async-done | bytes 6291472 | tf_op jit(solution)/shard_map/all_gather | solution.py:202
  232.3 27.5 all-gather.12.cloned.1.call-done
  281.8 160.9 %while.32 = (s32[]{:T(128)}, bf16[16,768,64]{1,2,0:T(8,128)(2,1)}, f32[16,768]{1,0:T(8,128)S(1)}, bf16[16,768,64]{2,1,0:T(8,128)(2,1)}, bf16[16,3072,64]{2,1,0:T...) while((s32[]{:T(128)}, bf16[16,768,64]{1,2,0:T(8,128)(2,1)}, ...), condition=%wide.region_5.6_spmd.clone, body=%wide.region_2.5_spmd.clone.sunk | while | flops 632293632 | bytes 30328940 | solution.py:207
  449.0 22.8 fusion.58
  492.9 570.7 %while.33 = (s32[]{:T(128)}, bf16[16,768,64]{1,2,0:T(8,128)(2,1)}, bf16[16,3072,64]{1,2,0:T(8,128)(2,1)}, bf16[16,3072,64]{1,2,0:T(8,128)(2,1)}, bf16[16,768,64]...) while((s32[]{:T(128)}, bf16[16,768,64]{1,2,0:T(8,128)(2,1)}, ...), condition=%wide.region_12.13_spmd.clone, body=%wide.region_10.12_spmd.clone.sunk | while | flops 1531431168 | bytes 132147384 | solution.py:245
  1070.8 51.3 %reduce-scatter.12.cloned.1.call-done = bf16[768,1024]{0,1:T(8,128)(2,1)} async-done(((bf16[3072,1024]{0,1:T(8,128)(2,1)}), bf16[768,1024]{0,1:T(8,128)(2,1)}) %reduce-scatter.12.cloned.1.call-update) | async-done | bytes 1572880 | tf_op jit(solution)/shard_map/reduce_scatter | solution.py:250
  1122.1 61.1 %reduce-scatter.10.cloned.1.call-done = bf16[768,1024]{0,1:T(8,128)(2,1)} async-done(((bf16[3072,1024]{0,1:T(8,128)(2,1)}), bf16[768,1024]{0,1:T(8,128)(2,1)}) %reduce-scatter.10.cloned.1.call-update) | async-done | bytes 1572880 | tf_op jit(solution)/shard_map/reduce_scatter | solution.py:247
  1252.8 73.6 %reduce-scatter.16.cloned.1.call-done = f32[4,8,1024]{2,1,0:T(8,128)} async-done(((f32[4,256,1024]{2,1,0:T(8,128)}), f32[4,8,1024]{2,1,0:T(8,128)}) %reduce-scatter.16.cloned.1.call-update) | async-done | bytes 131088 | tf_op jit(solution)/shard_map/reduce_scatter | solution.py:264
  1329.5 129.5 %reduce-scatter.22.cloned.1.call-done = f32[32,2]{1,0:T(8,128)} async-done(((f32[1024,2]{1,0:T(8,128)}), f32[32,2]{1,0:T(8,128)}) %reduce-scatter.22.cloned.1.call-update) | async-done | bytes 272
  1460.4 157.3 %reduce-scatter.14.cloned.1.call-done = f32[4,8,3072]{2,1,0:T(8,128)} async-done(((f32[4,256,3072]{2,1,0:T(8,128)}), f32[4,8,3072]{2,1,0:T(8,128)}) %reduce-scatter.14.cloned.1.call-update) | async-done | bytes 393232 | tf_op jit(solution)/shard_map/reduce_scatter | solution.py:263
  1620.7 181.4 %reduce-scatter.18.cloned.1.call-done = f32[4,8,4096]{2,1,0:T(8,128)} async-done(((f32[4,256,4096]{2,1,0:T(8,128)}), f32[4,8,4096]{2,1,0:T(8,128)}) %reduce-scatter.18.cloned.1.call-update) | async-done | bytes 524304 | tf_op jit(solution)/shard_map/reduce_scatter | solution.py:234
  1804.6 184.4 %reduce-scatter.20.cloned.1.call-done = f32[16,8,1024]{2,1,0:T(8,128)} async-done(((f32[16,256,1024]{2,1,0:T(8,128)}), f32[16,8,1024]{2,1,0:T(8,128)}) %reduce-scatter.20.cloned.1.call-update) | async-done | bytes 524304 | tf_op jit(solution)/shard_map/reduce_scatter | solution.py:237
  1993.2 41.9 %psum.7 = f32[]{:T(128)} all-reduce(f32[]{:T(128)S(6)} %add.166), channel_id=1, replica_groups=mesh['wide'=8,'narrow'=4] {'wide','narrow'}, use_global_device_ids=true, to_apply=%region_29.30 | all-reduce | flops 1 | bytes 8 | tf_op jit(solution)/shard_map/psum | solution.py:156
  2120.8 71.1 %custom-call.21 = f32[6,128,128]{2,1,0:T(8,128)S(1)} custom-call(f32[6,128,128]{2,1,0:T(8,128)} %cholesky.201), custom_call_target="Cholesky" | custom-call | tf_op jit(solution)/shard_map/jit(cholesky)/cholesky | solution.py:118
  2204.7 72.0 %custom-call.17 = f32[6,128,128]{2,1,0:T(8,128)} custom-call(f32[6,128,128]{2,1,0:T(8,128)} %cholesky.198), custom_call_target="Cholesky" | custom-call | tf_op jit(solution)/shard_map/jit(cholesky)/cholesky | solution.py:118
  2279.9 60.4 %custom-call.22 = f32[6,1,128,128]{2,3,1,0:T(8,128)} custom-call(f32[6,1,128,128]{3,2,1,0:T(8,128)} %get-tuple-element.442), custom_call_target="InvertDiagBlocksLowerTriangular" | custom-call | tf_op jit(solution)/shard_map/jit(cholesky)/cholesky | solution.py:118
  2345.4 71.8 %custom-call.23 = f32[6,128,128]{2,1,0:T(8,128)} custom-call(f32[6,128,128]{2,1,0:T(8,128)} %convolution_subtract_fusion.2), custom_call_target="Cholesky" | custom-call | tf_op jit(solution)/shard_map/jit(cholesky)/cholesky | solution.py:118
  2419.5 60.6 %custom-call.18 = f32[6,1,128,128]{2,3,1,0:T(8,128)} custom-call(f32[6,1,128,128]{3,2,1,0:T(8,128)} %get-tuple-element.443), custom_call_target="InvertDiagBlocksLowerTriangular" | custom-call | tf_op jit(solution)/shard_map/jit(cholesky)/cholesky | solution.py:118
  2485.2 71.8 %custom-call.19 = f32[6,128,128]{2,1,0:T(8,128)} custom-call(f32[6,128,128]{2,1,0:T(8,128)} %convolution_subtract_fusion.3), custom_call_target="Cholesky" | custom-call | tf_op jit(solution)/shard_map/jit(cholesky)/cholesky | solution.py:118
  2572.7 119.6 %custom-call.20 = f32[6,2,128,128]{2,3,1,0:T(8,128)} custom-call(f32[6,2,128,128]{3,2,1,0:T(8,128)} %bitcast.333), custom_call_target="InvertDiagBlocksLowerTriangular" | custom-call | tf_op jit(solution)/shard_map/jit(_solve_triangular)/vmap()/triangular_solve | solution.py:119
  2711.1 119.4 %custom-call.24 = f32[6,2,128,128]{2,3,1,0:T(8,128)} custom-call(f32[6,2,128,128]{3,2,1,0:T(8,128)} %bitcast.332), custom_call_target="InvertDiagBlocksLowerTriangular" | custom-call | tf_op jit(solution)/shard_map/jit(_solve_triangular)/vmap()/triangular_solve | solution.py:119
  (581 shorter events, 1109.9 us)
Async XLA Ops:
  7.2 2064.0 %copy-start = (f32[6,256,256]{2,1,0:T(8,128)S(1)}, f32[6,256,256]{2,1,0:T(8,128)}, u32[]{:S(2)}) copy-start(f32[6,256,256]{2,1,0:T(8,128)} %param.39) | copy-start | bytes 4718596
  7.2 49.5 %copy-start.6 = (bf16[768,1024]{1,0:T(8,128)(2,1)S(1)}, bf16[768,1024]{1,0:T(8,128)(2,1)}, u32[]{:S(2)}) copy-start(bf16[768,1024]{1,0:T(8,128)(2,1)} %param.24) | copy-start | bytes 4718596
  7.2 76.7 %all-gather.8.cloned.1.call-start = ((), (), s32[]{:S(2)}) async-start(), calls=%async_computation.9 | async-start | bytes 6488064 | tf_op jit(solution)/shard_map/all_gather | solution.py:191
  9.1 154.5 %all-gather.18.cloned.1.call-start = ((), (), s32[]{:S(2)}) async-start(), calls=%async_computation.14 | async-start | bytes 8650752 | tf_op jit(solution)/shard_map/all_gather | solution.py:191
  11.0 200.4 %all-gather.10.cloned.1.call-start = ((), (), s32[]{:S(2)}) async-start(), calls=%async_computation.10 | async-start | bytes 7864320 | tf_op jit(solution)/shard_map/all_gather | solution.py:202
  56.7 35.5 %copy-start.28 = (f32[768]{0:T(1024)}, f32[768]{0:T(1024)S(1)}, u32[]{:S(2)}) copy-start(f32[768]{0:T(1024)S(1)} %broadcast_multiply_fusion.5) | copy-start | bytes 9220
  57.3 34.9 %copy-start.31 = (f32[768]{0:T(1024)}, f32[768]{0:T(1024)S(1)}, u32[]{:S(2)}) copy-start(f32[768]{0:T(1024)S(1)} %add_rsqrt_fusion.1) | copy-start | bytes 9220
  94.5 165.2 %all-gather.12.cloned.1.call-start = ((), (), s32[]{:S(2)}) async-start(), calls=%async_computation.11 | async-start | bytes 7864320 | tf_op jit(solution)/shard_map/all_gather | solution.py:203
  95.1 347.6 %all-gather.14.cloned.1.call-start = ((), (), s32[]{:S(2)}) async-start(), calls=%async_computation.12 | async-start | bytes 2162688 | tf_op jit(solution)/shard_map/all_gather | solution.py:191
  96.1 352.9 %all-gather.16.cloned.1.call-start = ((), (), s32[]{:S(2)}) async-start(), calls=%async_computation.13 | async-start | bytes 8650752 | tf_op jit(solution)/shard_map/all_gather | solution.py:191
  97.9 1024.2 %reduce-scatter.12.cloned.1.call-start = ((), (), s32[]{:S(2)}) async-start(), calls=%async_computation.16 | async-start | bytes 7864320 | tf_op jit(solution)/shard_map/reduce_scatter | solution.py:250
  1063.6 119.6 %reduce-scatter.10.cloned.1.call-start = ((), (), s32[]{:S(2)}) async-start(), calls=%async_computation.15 | async-start | bytes 7864320 | tf_op jit(solution)/shard_map/reduce_scatter | solution.py:247
  1064.4 262.0 %reduce-scatter.16.cloned.1.call-start = ((), (), s32[]{:S(2)}) async-start(), calls=%async_computation.18 | async-start | bytes 4325376 | tf_op jit(solution)/shard_map/reduce_scatter | solution.py:264
  1070.7 112.5 %copy-start.7 = (bf16[768,1024]{1,0:T(8,128)(2,1)S(1)}, bf16[768,1024]{1,0:T(8,128)(2,1)}, u32[]{:S(2)}) copy-start(bf16[768,1024]{1,0:T(8,128)(2,1)} %param.24) | copy-start | bytes 4718596
  1070.7 112.5 %copy-start.29 = (f32[768]{0:T(1024)S(1)}, f32[768]{0:T(1024)}, u32[]{:S(2)}) copy-start(f32[768]{0:T(1024)} %copy-done.28) | copy-start | bytes 9220
  1070.7 112.5 %copy-start.32 = (f32[768]{0:T(1024)S(1)}, f32[768]{0:T(1024)}, u32[]{:S(2)}) copy-start(f32[768]{0:T(1024)} %copy-done.31) | copy-start | bytes 9220
  1070.8 112.5 %copy-start.35 = (f32[1,1024]{1,0:T(1,128)S(1)}, f32[1,1024]{1,0:T(1,128)}, u32[]{:S(2)}) copy-start(f32[1,1024]{1,0:T(1,128)} %copy-done.34) | copy-start | bytes 12292
  1070.8 388.2 %reduce-scatter.22.cloned.1.call-start = ((), (), s32[]{:S(2)}) async-start(), calls=%async_computation.21 | async-start | bytes 540672
  1195.7 422.1 %reduce-scatter.14.cloned.1.call-start = ((), (), s32[]{:S(2)}) async-start(), calls=%async_computation.17 | async-start | bytes 12976128 | tf_op jit(solution)/shard_map/reduce_scatter | solution.py:263
  1208.1 594.0 %reduce-scatter.18.cloned.1.call-start = ((), (), s32[]{:S(2)}) async-start(), calls=%async_computation.19 | async-start | bytes 17301504 | tf_op jit(solution)/shard_map/reduce_scatter | solution.py:234
  1222.1 766.9 %reduce-scatter.20.cloned.1.call-start = ((), (), s32[]{:S(2)}) async-start(), calls=%async_computation.20 | async-start | bytes 17301504 | tf_op jit(solution)/shard_map/reduce_scatter | solution.py:237
  1459.8 532.3 %copy-start.38 = (f32[2,32]{1,0:T(2,128)}, f32[2,32]{1,0:T(2,128)S(1)}, u32[]{:S(2)}) copy-start(f32[2,32]{1,0:T(2,128)S(1)} %copy.401) | copy-start | bytes 772
  2042.6 25.3 all-to-all-start
  2106.1 731.4 %all-to-all-start.1 = ((bf16[6,32,8,256]{3,2,0,1:T(8,128)(2,1)}), bf16[6,32,8,256]{3,2,0,1:T(8,128)(2,1)}, u32[]{:S(2)}, u32[]{:S(2)}) async-start(bf16[6,32,8,256]{3,2,0,1:T(8,128)(2,1)} %copy.338), calls=%async_computation.7 | async-start | bytes 1572864 | tf_op jit(solution)/shard_map/all_to_all | solution.py:297
  (70 other events, 487.7 us)
Sparse Core Ops, SparseCore 0:
  11.5 72.2 all-gather.7
  87.4 76.1 all-gather.17
  165.7 45.5 all-gather.9
  213.3 46.3 all-gather.11
  263.1 56.1 all-gather.13
  322.7 76.4 all-gather.15
  1063.8 58.3 reduce-scatter.11
  1124.8 58.3 reduce-scatter.9
  1185.5 140.8 reduce-scatter.15
  1329.1 129.8 reduce-scatter.21
  1466.1 151.6 reduce-scatter.13
  1619.9 182.2 reduce-scatter.17
  1804.4 184.5 reduce-scatter.19
where the time goes:
time: 2870 us; the launch traced here: 2860 us
  waiting for transfers between devices  990 us (34%)
  other arithmetic  920 us (32%)
  matrix products  697 us (24%)
  local copies, waits for them, and re-layouts  133 us (5%)
  blocking collectives  85.1 us (3%)
    another operation x16, other arithmetic, renew_basis(): factor_low = jnp.linalg.cholesky(gram_matrix)  413 us
    another operation x5, other arithmetic, renew_basis(): jax.scipy.linalg.solve_triangular(factor_low, turned.transpose(0, 2, 1),...  244 us
    reduce_scatter x1, waiting for transfers between devices, body(): lax.psum_scatter(as_layout(d_back), ('wide', 'narrow'), scatter_dimension...  184 us
    reduce_scatter x1, waiting for transfers between devices, body(): lax.psum_scatter(as_layout(d_w_hidden), ('wide', 'narrow'), scatter_dimen...  181 us
    dot_general x32, matrix products, masked_scores(): jnp.einsum('te,se->ts', queries, keyset, preferred_element_type=jnp.float32)  181 us
    convert_element_type x16, other arithmetic, head_backward(): d_scores = (attn_probs * (d_probs - inner)).astype(jnp.bfloat16)  176 us
    reduce_scatter x1, waiting for transfers between devices, body(): lax.psum_scatter(as_layout(d_attn), ('wide', 'narrow'), scatter_dimension...  157 us
    unnamed x14, waiting for transfers between devices  131 us
  transfers between devices with their start and end apart: 15, of which 12 were waited for; matrix products, arithmetic and copies ran while one was open for 37% of the time, Pallas kernels for 0%

commit v1 on v0

--- a/solution.py
+++ b/solution.py
@@ -3,6 +3,8 @@
 import jax
 import jax.numpy as jnp
 from jax import lax
+from jax.experimental import pallas as pl
+from jax.experimental.pallas import tpu as pltpu
 from jax.sharding import PartitionSpec as P
 
 FF = 4096
@@ -20,6 +22,12 @@
 gain_rate = 1.0
 neg_large = -1e30
 highest = lax.Precision.HIGHEST
+float32 = jnp.float32
+bfloat16 = jnp.bfloat16
+PAIR = 2 * HEAD
+NT = (((1,), (1,)), ((), ()))
+TN = (((0,), (0,)), ((), ()))
+VMEM_LIMIT = 48 * 2**20
 
 
 def shortened(shard):
@@ -43,14 +51,6 @@
     return (d_input, d_gain)
 
 
-def split_heads(matrix):
-    return matrix.reshape(matrix.shape[0], HEADS, HEAD).transpose(1, 0, 2)
-
-
-def join_heads(stacked):
-    return stacked.transpose(1, 0, 2).reshape(stacked.shape[1], HEADS * HEAD)
-
-
 def as_layout(matrix):
     return matrix.reshape(matrix.shape[0] // BLOCK, BLOCK, matrix.shape[1])
 
@@ -73,75 +73,278 @@
     )
 
 
-def masked_scores(visible, score_scale, queries, keyset):
-    scores = (
-        jnp.einsum("te,se->ts", queries, keyset, preferred_element_type=jnp.float32) * score_scale
-    )
-    return jnp.where(visible[None, :], scores, neg_large)
-
-
-def attend_head(visible, score_scale, parts):
-    queries, keyset, valueset = parts
-    scores = masked_scores(visible, score_scale, queries, keyset)
-    topmost = jnp.max(scores, -1, keepdims=True)
-    expo_vals = jnp.exp(scores - topmost)
-    totals = jnp.sum(expo_vals, -1, keepdims=True)
-    attn_probs = expo_vals / totals
-    mixed = jnp.dot(attn_probs.astype(jnp.bfloat16), valueset, preferred_element_type=jnp.float32)
-    return (mixed, (topmost + jnp.log(totals))[:, 0])
-
-
-def head_backward(visible, score_scale, parts):
-    queries, keyset, valueset, d_mixed, log_total = parts
-    scores = masked_scores(visible, score_scale, queries, keyset)
-    attn_probs = jnp.exp(scores - log_total[:, None])
-    d_probs = jnp.einsum("te,se->ts", d_mixed, valueset, preferred_element_type=jnp.float32)
-    d_values = jnp.einsum(
-        "ts,te->se", attn_probs.astype(jnp.bfloat16), d_mixed, preferred_element_type=jnp.float32
-    )
-    inner = jnp.sum(attn_probs * d_probs, -1, keepdims=True)
-    d_scores = (attn_probs * (d_probs - inner)).astype(jnp.bfloat16)
-    d_queries = jnp.dot(d_scores, keyset, preferred_element_type=jnp.float32) * score_scale
-    d_keys = (
-        jnp.einsum("ts,te->se", d_scores, queries, preferred_element_type=jnp.float32) * score_scale
-    )
-    return (d_queries, d_keys, d_values)
-
-
-def batched(spec, left, right):
-    return jnp.einsum(spec, left, right, precision=highest)
-
-
-def renew_basis(stat, basis):
-    turned = batched("sij,sjk->sik", stat, basis)
-    gram_matrix = batched("sji,sjk->sik", turned, turned)
-    factor_low = jnp.linalg.cholesky(gram_matrix)
-    solved = jax.scipy.linalg.solve_triangular(factor_low, turned.transpose(0, 2, 1), lower=True)
-    return solved.transpose(0, 2, 1)
-
-
-def soap_update(gradient, first_old, second_old, left_old, right_old, left_base, right_base):
-    left_new = decay_rate * left_old + (1.0 - decay_rate) * batched(
-        "sij,skj->sik", gradient, gradient
-    )
-    right_new = decay_rate * right_old + (1.0 - decay_rate) * batched(
-        "sji,sjk->sik", gradient, gradient
-    )
-    turned = batched("sji,sjk->sik", left_base, batched("sij,sjk->sik", gradient, right_base))
-    first_new = decay_rate * first_old + (1.0 - decay_rate) * turned
-    second_new = decay_rate * second_old + (1.0 - decay_rate) * turned * turned
+def one_head(matrix, head):
+    lane = lax.broadcasted_iota(jnp.int32, matrix.shape, 1)
+    return jnp.where(lane // HEAD == head, matrix, jnp.zeros_like(matrix))
+
+
+def hide(scores, start, safe, length):
+    if start + scores.shape[0] <= safe:
+        return scores
+    position = start + lax.broadcasted_iota(jnp.int32, scores.shape, 0)
+    return jnp.where(position < length, scores, neg_large)
+
+
+def attend_kernel(safe, chunk, length_ref, q_ref, k_ref, v_ref, o_ref, log_ref, vt_ref, s_ref):
+    seq_len = k_ref.shape[0]
+    length = length_ref[0]
+
+    @pl.when(pl.program_id(1) == 0)
+    def _():
+        vt_ref[...] = v_ref[...].T
+
+    outs = []
+    for head in range(2):
+        queries = one_head(q_ref[...], head) * bfloat16(HEAD**-0.5)
+        topmost = None
+        for at in range(0, seq_len, chunk):
+            scores = lax.dot_general(
+                k_ref[at : at + chunk, :], queries, NT, preferred_element_type=float32
+            )
+            scores = hide(scores, at, safe, length)
+            s_ref[head, at : at + chunk, :] = scores
+            top = jnp.max(scores, 0, keepdims=True)
+            topmost = top if topmost is None else jnp.maximum(topmost, top)
+        totals = jnp.zeros_like(topmost)
+        mixed = jnp.zeros((HEAD, q_ref.shape[0]), float32)
+        for at in range(0, seq_len, chunk):
+            expo = jnp.exp(s_ref[head, at : at + chunk, :] - topmost)
+            totals += jnp.sum(expo, 0, keepdims=True)
+            mixed += jnp.dot(
+                vt_ref[head * HEAD : (head + 1) * HEAD, at : at + chunk],
+                expo.astype(bfloat16),
+                preferred_element_type=float32,
+            )
+        outs.append(mixed * (1.0 / totals))
+        log_ref[0, head : head + 1, :] = topmost + jnp.log(totals)
+    o_ref[...] = jnp.concatenate(outs, 0).T.astype(bfloat16)
+
+
+def attend(lengths, scene, safe, rows=1024, chunk=512):
+    seq_len, width = scene.shape[0], scene.shape[1] // 3
+    pairs = width // PAIR
+    return pl.pallas_call(
+        partial(attend_kernel, safe, chunk),
+        grid=(pairs, seq_len // rows),
+        in_specs=[
+            pl.BlockSpec(memory_space=pltpu.SMEM),
+            pl.BlockSpec((rows, PAIR), lambda p, i: (i, p)),
+            pl.BlockSpec((seq_len, PAIR), lambda p, i: (0, pairs + p)),
+            pl.BlockSpec((seq_len, PAIR), lambda p, i: (0, 2 * pairs + p)),
+        ],
+        out_specs=[
+            pl.BlockSpec((rows, PAIR), lambda p, i: (i, p)),
+            pl.BlockSpec((1, 2, rows), lambda p, i: (p, 0, i)),
+        ],
+        out_shape=[
+            jax.ShapeDtypeStruct((seq_len, width), bfloat16),
+            jax.ShapeDtypeStruct((pairs, 2, seq_len), float32),
+        ],
+        scratch_shapes=[
+            pltpu.VMEM((PAIR, seq_len), bfloat16),
+            pltpu.VMEM((2, seq_len, rows), float32),
+        ],
+        compiler_params=pltpu.CompilerParams(vmem_limit_bytes=VMEM_LIMIT),
+        cost_estimate=pl.CostEstimate(
+            flops=4 * pairs * 2 * 4 * seq_len * seq_len * HEAD,
+            bytes_accessed=8 * seq_len * width,
+            transcendentals=0,
+        ),
+    )(lengths, scene, scene, scene)
+
+
+def attend_backward_kernel(
+    safe, chunk, length_ref, q_ref, k_ref, v_ref, o_ref, do_ref, log_ref, dq_ref, dk_ref, dv_ref, kt_ref, dk_sum, dv_sum
+):
+    seq_len = k_ref.shape[0]
+    length = length_ref[0]
+
+    @pl.when(pl.program_id(1) == 0)
+    def _():
+        kt_ref[...] = k_ref[...].T
+        dk_sum[...] = jnp.zeros_like(dk_sum)
+        dv_sum[...] = jnp.zeros_like(dv_sum)
+
+    products = (o_ref[...].astype(float32) * do_ref[...].astype(float32)).T
+    turned = []
+    for head in range(2):
+        lanes = slice(head * HEAD, (head + 1) * HEAD)
+        queries = one_head(q_ref[...], head) * bfloat16(HEAD**-0.5)
+        d_mixed = one_head(do_ref[...], head)
+        inner = jnp.sum(products[lanes, :], 0, keepdims=True)
+        log_total = log_ref[0, head : head + 1, :]
+        d_queries = jnp.zeros((HEAD, q_ref.shape[0]), float32)
+        for at in range(0, seq_len, chunk):
+            part = slice(at, at + chunk)
+            scores = lax.dot_general(k_ref[part, :], queries, NT, preferred_element_type=float32)
+            probs = jnp.exp(hide(scores, at, safe, length) - log_total)
+            d_probs = lax.dot_general(v_ref[part, :], d_mixed, NT, preferred_element_type=float32)
+            dv_sum[part, :] += jnp.dot(
+                probs.astype(bfloat16), d_mixed, preferred_element_type=float32
+            )
+            d_scores = (probs * (d_probs - inner)).astype(bfloat16)
+            dk_sum[part, :] += jnp.dot(d_scores, queries, preferred_element_type=float32)
+            d_queries += jnp.dot(kt_ref[lanes, part], d_scores, preferred_element_type=float32)
+        turned.append(d_queries * HEAD**-0.5)
+    dq_ref[...] = jnp.concatenate(turned, 0).T.astype(bfloat16)
+
+    @pl.when(pl.program_id(1) == pl.num_programs(1) - 1)
+    def _():
+        dk_ref[...] = dk_sum[...].astype(bfloat16)
+        dv_ref[...] = dv_sum[...].astype(bfloat16)
+
+
+def attend_backward(lengths, scene, mixed, d_mixed, log_totals, safe, rows=512, chunk=1024):
+    seq_len, width = mixed.shape
+    pairs = width // PAIR
+    tile = pl.BlockSpec((rows, PAIR), lambda p, i: (i, p))
+    full = pl.BlockSpec((seq_len, PAIR), lambda p, i: (0, p))
+    return pl.pallas_call(
+        partial(attend_backward_kernel, safe, chunk),
+        grid=(pairs, seq_len // rows),
+        in_specs=[
+            pl.BlockSpec(memory_space=pltpu.SMEM),
+            tile,
+            pl.BlockSpec((seq_len, PAIR), lambda p, i: (0, pairs + p)),
+            pl.BlockSpec((seq_len, PAIR), lambda p, i: (0, 2 * pairs + p)),
+            tile,
+            tile,
+            pl.BlockSpec((1, 2, rows), lambda p, i: (p, 0, i)),
+        ],
+        out_specs=[tile, full, full],
+        out_shape=[jax.ShapeDtypeStruct((seq_len, width), bfloat16)] * 3,
+        scratch_shapes=[
+            pltpu.VMEM((PAIR, seq_len), bfloat16),
+            pltpu.VMEM((seq_len, PAIR), float32),
+            pltpu.VMEM((seq_len, PAIR), float32),
+        ],
+        compiler_params=pltpu.CompilerParams(vmem_limit_bytes=VMEM_LIMIT),
+        cost_estimate=pl.CostEstimate(
+            flops=4 * pairs * 2 * 10 * seq_len * seq_len * HEAD,
+            bytes_accessed=16 * seq_len * width,
+            transcendentals=0,
+        ),
+    )(lengths, scene, scene, scene, mixed, d_mixed, log_totals)
+
+
+def exact(left, right, dims=(((1,), (0,)), ((), ()))):
+    return lax.dot_general(left, right, dims, precision=highest, preferred_element_type=float32)
+
+
+def soap_kernel(
+    g_ref, first_ref, second_ref, ls_ref, rs_ref, lb_ref, rb_ref,
+    back_ref, first_out, second_out, ls_out, rs_out, gram_ref, turn_ref,
+):
+    gradient = g_ref[0].astype(float32)
+    left_base, right_base = lb_ref[0], rb_ref[0]
+    left_new = decay_rate * ls_ref[0] + (1.0 - decay_rate) * exact(gradient, gradient, NT)
+    right_new = decay_rate * rs_ref[0] + (1.0 - decay_rate) * exact(gradient, gradient, TN)
+    ls_out[0] = left_new
+    rs_out[0] = right_new
+    turned = exact(left_base, exact(gradient, right_base), TN)
+    first_new = decay_rate * first_ref[0] + (1.0 - decay_rate) * turned
+    second_new = decay_rate * second_ref[0] + (1.0 - decay_rate) * turned * turned
+    first_out[0] = first_new
+    second_out[0] = second_new
     correct = 1.0 - decay_rate**STEP
     direction = first_new / correct / (jnp.sqrt(second_new / correct) + eps_adam)
-    restored = batched("sij,sjk->sik", left_base, batched("sij,skj->sik", direction, right_base))
-    return (
-        restored,
-        first_new,
-        second_new,
-        left_new,
-        right_new,
-        renew_basis(left_new, left_base),
-        renew_basis(right_new, right_base),
-    )
+    back_ref[0] = exact(left_base, exact(direction, right_base, NT)).astype(back_ref.dtype)
+    for side, stat, base in ((0, left_new, left_base), (1, right_new, right_base)):
+        turn = exact(stat, base).T
+        turn_ref[0, side] = turn
+        gram_ref[0, side] = exact(turn, turn, NT)
+
+
+def soap_update(gradient, first_old, second_old, left_old, right_old, left_base, right_base):
+    slots, order, _ = gradient.shape
+    one = pl.BlockSpec((1, order, order), lambda s: (s, 0, 0))
+    two = pl.BlockSpec((1, 2, order, order), lambda s: (s, 0, 0, 0))
+    single = jax.ShapeDtypeStruct((slots, order, order), float32)
+    double = jax.ShapeDtypeStruct((slots, 2, order, order), float32)
+    return pl.pallas_call(
+        soap_kernel,
+        grid=(slots,),
+        in_specs=[one] * 7,
+        out_specs=[one] * 5 + [two] * 2,
+        out_shape=[jax.ShapeDtypeStruct((slots, order, order), bfloat16)] + [single] * 4 + [double] * 2,
+        compiler_params=pltpu.CompilerParams(vmem_limit_bytes=VMEM_LIMIT),
+        cost_estimate=pl.CostEstimate(
+            flops=slots * 120 * order**3, bytes_accessed=slots * 60 * order**2, transcendentals=0
+        ),
+    )(gradient, first_old, second_old, left_old, right_old, left_base, right_base)
+
+
+def renew_kernel(rows, gram_ref, turn_ref, q_ref, x_ref, u_ref):
+    count, order = gram_ref.shape[0], gram_ref.shape[1]
+    eye = (
+        lax.broadcasted_iota(jnp.int32, (rows, rows), 0)
+        == lax.broadcasted_iota(jnp.int32, (rows, rows), 1)
+    ).astype(float32)
+    sublane = lax.broadcasted_iota(jnp.int32, (1, 8, 1), 1)
+    for low in range(0, order, rows):
+        part = slice(low, low + rows)
+
+        def panel(at, carry, low=low, part=part):
+            row = jnp.concatenate([gram_ref[at, part, :], turn_ref[at, part, :]], 1)
+            if low:
+                row = row - exact(u_ref[at, :low, part], u_ref[at, :low, :], TN)
+            u_ref[at, part, :] = row
+            x_ref[at] = jnp.concatenate([row[:, part], eye], 1)
+            return carry
+
+        lax.fori_loop(0, count, panel, 0, unroll=2)
+        for j in range(rows):
+            tile = j // 8 * 8
+            row = x_ref[:, j : j + 1, :]
+            row = row * (1.0 / row[:, :, j : j + 1])
+            top = x_ref[:, tile : tile + 8, :]
+            below = jnp.where(sublane > j - tile, top[:, :, j : j + 1], 0.0)
+            x_ref[:, tile : tile + 8, :] = top - below * row
+            if tile + 8 < rows:
+                rest = x_ref[:, tile + 8 :, :]
+                x_ref[:, tile + 8 :, :] = rest - rest[:, :, j : j + 1] * row
+
+        def solve(at, carry, part=part):
+            both = x_ref[at]
+            diagonal = jnp.sum(both[:, :rows] * eye, 1, keepdims=True)
+            u_ref[at, part, :] = exact(both[:, rows:] * lax.rsqrt(diagonal), u_ref[at, part, :])
+            return carry
+
+        lax.fori_loop(0, count, solve, 0, unroll=2)
+
+    def turn_back(at, carry):
+        q_ref[at] = u_ref[at, :, order:].T
+        return carry
+
+    lax.fori_loop(0, count, turn_back, 0)
+
+
+def renew_bases(gram, turn, rows=64):
+    count, order, _ = gram.shape
+    return pl.pallas_call(
+        partial(renew_kernel, rows),
+        out_shape=jax.ShapeDtypeStruct(gram.shape, float32),
+        in_specs=[pl.BlockSpec(memory_space=pltpu.VMEM)] * 2,
+        out_specs=pl.BlockSpec(memory_space=pltpu.VMEM),
+        scratch_shapes=[
+            pltpu.VMEM((count, rows, 2 * rows), float32),
+            pltpu.VMEM((count, order, 2 * order), float32),
+        ],
+        compiler_params=pltpu.CompilerParams(vmem_limit_bytes=VMEM_LIMIT),
+        cost_estimate=pl.CostEstimate(
+            flops=count * 200 * order**3, bytes_accessed=count * 12 * order**2, transcendentals=0
+        ),
+    )(gram, turn)
+
+
+def exchange(groups):
+    return lax.all_to_all(groups, "narrow", split_axis=0, concat_axis=0, tiled=True)
+
+
+def scattered(layout, dimension):
+    return lax.psum_scatter(
+        layout.astype(bfloat16), ("wide", "narrow"), scatter_dimension=dimension, tiled=True
+    ).astype(float32)
 
 
 def unpack(gathered):
@@ -180,7 +383,6 @@
     device_count = lax.axis_size("wide") * narrow_count
     seq_len = tok_rows * narrow_count
     cap_slots = moment_first.shape[0]
-    score_scale = HEAD ** (-0.5)
     masters = (w_qkv, w_out, w_up, w_down)
     lowered = tuple((layout.astype(jnp.bfloat16) for layout in masters)) + (
         norm_gains.astype(jnp.bfloat16),
@@ -196,16 +398,15 @@
     inputs = tokens.astype(jnp.float32)
     normed_one, inverse_one = normalize(inputs)
     act_one = (normed_one * gain_pair[0]).astype(jnp.bfloat16)
-    packed = jnp.dot(act_one, w_attn, preferred_element_type=jnp.float32).astype(jnp.bfloat16)
-    queries = packed[:, :width]
-    keyset, valueset = (
-        lax.all_gather(packed[:, width : 2 * width], "narrow", axis=0, tiled=True),
-        lax.all_gather(packed[:, 2 * width :], "narrow", axis=0, tiled=True),
-    )
-    visible = lax.iota(jnp.int32, seq_len) < lengths[0]
-    head_parts = (split_heads(queries), split_heads(keyset), split_heads(valueset))
-    mixed, log_totals = lax.map(partial(attend_head, visible, score_scale), head_parts)
-    merged = join_heads(mixed).astype(jnp.bfloat16)
+    head_width = width // narrow_count
+    safe = seq_len - tok_rows
+    w_groups = w_attn.reshape(width, 3, narrow_count, head_width)
+    packed = jnp.einsum("td,dkge->gtke", act_one, w_groups, preferred_element_type=jnp.float32)
+    packed = packed.astype(jnp.bfloat16).reshape(narrow_count, tok_rows, 3 * head_width)
+    scene = exchange(packed).reshape(seq_len, 3 * head_width)
+    mixed, log_totals = attend(lengths, scene, safe)
+    merged = exchange(mixed.reshape(narrow_count, tok_rows, head_width))
+    merged = merged.transpose(1, 0, 2).reshape(tok_rows, width)
     middle = inputs + jnp.dot(merged, w_proj, preferred_element_type=jnp.float32)
     normed_two, inverse_two = normalize(middle)
     act_two = (normed_two * gain_pair[1]).astype(jnp.bfloat16)
@@ -214,14 +415,6 @@
     block_out = (middle + jnp.dot(active, w_back, preferred_element_type=jnp.float32)).astype(
         jnp.bfloat16
     )
-    weight_list, gain_pair = unpack(
-        jax.tree.map(
-            lambda part, own: part.astype(own.dtype),
-            lax.all_gather(shortened(lowered), ("wide", "narrow"), axis=1, tiled=True),
-            lowered,
-        )
-    )
-    w_attn, w_proj, w_hidden, w_back = weight_list
     d_back = jnp.einsum("tf,td->fd", active, cotangent, preferred_element_type=jnp.float32)
     d_active = jnp.einsum("td,fd->tf", cotangent, w_back, preferred_element_type=jnp.float32)
     _, gelu_pull = jax.vjp(partial(jax.nn.gelu, approximate=True), hidden)
@@ -230,38 +423,32 @@
     d_act_two = jnp.einsum("tf,df->td", d_hidden, w_hidden, preferred_element_type=jnp.float32)
     d_norm_two, d_gain_two = norm_backward(d_act_two, normed_two, inverse_two, gain_pair[1])
     d_middle = cotangent.astype(jnp.float32) + d_norm_two
-    mlp_sums = (
-        lax.psum_scatter(
-            as_layout(d_w_hidden), ("wide", "narrow"), scatter_dimension=1, tiled=True
-        ),
-        lax.psum_scatter(as_layout(d_back), ("wide", "narrow"), scatter_dimension=1, tiled=True),
-    )
+    mlp_sums = (scattered(as_layout(d_w_hidden), 1), scattered(as_layout(d_back), 1))
     d_branch = d_middle.astype(jnp.bfloat16)
     d_proj = jnp.einsum("td,te->de", merged, d_branch, preferred_element_type=jnp.float32)
     d_merged = jnp.einsum("te,de->td", d_branch, w_proj, preferred_element_type=jnp.float32).astype(
         jnp.bfloat16
     )
-    back_parts = head_parts + (split_heads(d_merged), log_totals)
-    d_queries, d_keys, d_values = lax.map(partial(head_backward, visible, score_scale), back_parts)
-    key_sums = (
-        lax.psum_scatter(
-            join_heads(d_keys).astype(jnp.bfloat16), "narrow", scatter_dimension=0, tiled=True
-        ).astype(jnp.float32),
-        lax.psum_scatter(
-            join_heads(d_values).astype(jnp.bfloat16), "narrow", scatter_dimension=0, tiled=True
-        ).astype(jnp.float32),
-    )
-    key_grad, value_grad = (key_sums[0], key_sums[1])
-    d_packed = jnp.concatenate([join_heads(d_queries), key_grad, value_grad], 1).astype(
-        jnp.bfloat16
-    )
-    d_attn = jnp.einsum("td,te->de", act_one, d_packed, preferred_element_type=jnp.float32)
-    d_act_one = jnp.einsum("te,de->td", d_packed, w_attn, preferred_element_type=jnp.float32)
+    d_mixed = d_merged.reshape(tok_rows, narrow_count, head_width).transpose(1, 0, 2)
+    d_mixed = exchange(d_mixed).reshape(seq_len, head_width)
+    d_scene = jnp.concatenate(attend_backward(lengths, scene, mixed, d_mixed, log_totals, safe), 1)
+    d_packed = exchange(d_scene.reshape(narrow_count, tok_rows, 3 * head_width))
+    d_attn = jnp.einsum("td,gtc->gdc", act_one, d_packed, preferred_element_type=jnp.float32)
+    d_act_one = jnp.einsum(
+        "gtke,dkge->td",
+        d_packed.reshape(narrow_count, tok_rows, 3, head_width),
+        w_groups,
+        preferred_element_type=jnp.float32,
+    )
     d_norm_one, d_gain_one = norm_backward(d_act_one, normed_one, inverse_one, gain_pair[0])
     grad_tokens = (d_middle + d_norm_one).astype(jnp.bfloat16)
+    attn_sum = scattered(d_attn.reshape(narrow_count, -1, BLOCK, 3 * head_width), 2)
+    band_rows = attn_sum.shape[2]
+    attn_sum = attn_sum.reshape(narrow_count, -1, band_rows, 3, head_width)
+    attn_sum = attn_sum.transpose(1, 2, 3, 0, 4).reshape(-1, band_rows, 3 * width)
     attn_sums = (
-        lax.psum_scatter(as_layout(d_attn), ("wide", "narrow"), scatter_dimension=1, tiled=True),
-        lax.psum_scatter(as_layout(d_proj), ("wide", "narrow"), scatter_dimension=1, tiled=True),
+        attn_sum,
+        scattered(as_layout(d_proj), 1),
         lax.psum_scatter(
             jnp.stack([d_gain_one, d_gain_two]), ("wide", "narrow"), scatter_dimension=1, tiled=True
         ),
@@ -291,9 +478,13 @@
         tiled=True,
     ).astype(jnp.float32)
     slot_grads = arrived.reshape(cap_slots, BLOCK, BLOCK)
-    restored, first_new, second_new, left_new, right_new, left_turn, right_turn = soap_update(
+    restored, first_new, second_new, left_new, right_new, gram, turn = soap_update(
         slot_grads, moment_first, moment_second, left_stat, right_stat, left_basis, right_basis
     )
+    square = (-1, BLOCK, BLOCK)
+    bases = renew_bases(gram.reshape(square), turn.reshape(square))
+    bases = bases.reshape(cap_slots, 2, BLOCK, BLOCK)
+    left_turn, right_turn = bases[:, 0], bases[:, 1]
     returned = lax.all_to_all(
         shortened(restored.reshape(cap_slots, device_count, -1, BLOCK)),
         ("wide", "narrow"),

time: 2870 us -> 1370 us (0.48)
  other arithmetic: 920 us -> 28.1 us
  matrix products: 697 us -> 130 us
  waiting for transfers between devices: 990 us -> 685 us
  Pallas kernels: 0 us -> 240 us
    reduce_scatter x6 -> x0, waiting for transfers between devices: 709 us -> none  [the longest x1 184 us: body(): lax.psum_scatter(as_layout(d_back), ('wide', 'narrow'), scatter_dimension...]
    another operation x25 -> x1, other arithmetic: 657 us -> 0.04 us  [the longest x16 413 us: renew_basis(): factor_low = jnp.linalg.cholesky(gram_matrix)]
    dot_general x125 -> x3, matrix products: 568 us -> 32.3 us  [the longest x1 11.6 us: body(): jnp.einsum('gtke,dkge->td', d_packed.reshape(narrow_count, tok_rows, 3, h...]
    unnamed x14, waiting for transfers between devices: 131 us -> 494 us
    pallas_call x0 -> x4, Pallas kernels: none -> 240 us  [the longest x1 99.7 us: attend_backward(): pl.pallas_call(partial(attend_backward_kernel, safe, chunk), grid=(pairs,...]
    convert_element_type x16 -> x3, other arithmetic: 176 us -> 1.93 us  [scattered(): return lax.psum_scatter(layout.astype(bfloat16), ('wide', 'narrow'), scat...]
    all_to_all x0 -> x3, waiting for transfers between devices: none -> 130 us  [exchange(): lax.all_to_all(groups, 'narrow', split_axis=0, concat_axis=0, tiled=True)]
    all_gather x2 -> x0, waiting for transfers between devices: 62.4 us -> none  [the longest x1 35 us: body(): lax.all_gather(packed[:, width:2 * width], 'narrow', axis=0, tiled=True)]
  transfers between devices with their start and end apart: 15 -> 14, of which waited for: 12 -> 10; matrix products, arithmetic and copies ran while one was open for 37% -> 16% of each run, Pallas kernels for 0% -> 9%
where the time goes in v1:
time: 1370 us; the launch traced here: 1360 us
  waiting for transfers between devices  685 us (50%)
  Pallas kernels  240 us (18%)
  local copies, waits for them, and re-layouts  131 us (10%)
  matrix products  130 us (9%)
  blocking collectives  103 us (8%)
  other arithmetic  28.1 us (2%)
  starting transfers between devices  24.1 us (2%)
  between operations  20.8 us (2%)
    unnamed x14, waiting for transfers between devices  494 us
    all_to_all x3, waiting for transfers between devices, exchange(): lax.all_to_all(groups, 'narrow', split_axis=0, concat_axis=0, tiled=True)  130 us
    pallas_call x1, Pallas kernels, attend_backward(): pl.pallas_call(partial(attend_backward_kernel, safe, chunk), grid=(pairs,...  99.7 us
    unnamed x95, local copies, waits for them, and re-layouts  79.2 us
    pallas_call x1, Pallas kernels, attend(): pl.pallas_call(partial(attend_kernel, safe, chunk), grid=(pairs, seq_len...  62 us
    all_gather x4, waiting for transfers between devices, body(): lax.all_gather(shortened(lowered), ('wide', 'narrow'), axis=1, tiled=True)  57.9 us
    pallas_call x1, Pallas kernels, renew_bases(): pl.pallas_call(partial(renew_kernel, rows), out_shape=jax.ShapeDtypeStruc...  54.8 us
    all_gather x1, blocking collectives, body(): lax.all_gather(shortened(lowered), ('wide', 'narrow'), axis=1, tiled=True)  43.1 us
  transfers between devices with their start and end apart: 14, of which 10 were waited for; matrix products, arithmetic and copies ran while one was open for 16% of the time, Pallas kernels for 9%

profile of v1, /device:TPU:0, one launch (start us, length us, event | category | flops | bytes accessed | tf_op | source)
XLA Modules:
  0.0 1363.0 jit_solution(15044725324889699315)
XLA Ops:
  14.4 43.1 %all-gather = bf16[32,32,2]{1,2,0:T(2,128)(2,1)S(1)} all-gather(bf16[1,32,2]{1,2,0:T(2,128)(2,1)S(1)} %convert_bitcast_fusion.2), channel_id=1, replica_groups=mesh['wide'=8,'narrow'=4] {'wide','narrow'}, dimensions={0}, use_global_device_ids=true | all-gather | bytes 4224 | tf_op jit(solution)/shard_map/all_gather | solution.py:393
  58.5 25.5 %all-gather.6.cloned.1.call-done = bf16[4,256,3072]{2,1,0:T(8,128)(2,1)} async-done(((bf16[4,8,3072]{2,1,0:T(8,128)(2,1)}), bf16[4,256,3072]{2,1,0:T(8,128)(2,1)}) %all-gather.6.cloned.1.call-update) | async-done | bytes 6291472 | tf_op jit(solution)/shard_map/all_gather | solution.py:393
  84.0 12.2 reshape.239
  116.0 67.5 %all-to-all-done = bf16[4,768,768]{1,2,0:T(8,128)(2,1)} async-done(((bf16[4,768,768]{1,2,0:T(8,128)(2,1)}), bf16[4,768,768]{1,2,0:T(8,128)(2,1)}, u32[]{:S(2)}, u32[]{:S(2)}) %all-to-all-start) | async-done | bytes 4718624 | tf_op jit(solution)/shard_map/all_to_all | solution.py:341
  190.1 62.0 %shard_map.288 = (bf16[3072,256]{1,0:T(8,128)(2,1)}, f32[2,2,3072]{2,1,0:T(2,128)S(1)}) custom-call(s32[1]{0:T(128)S(6)} %copy.272.length_ref, bf16[3072,768]{1,0:T(8,128)(2,1)} %bitcast.189, bf16[3072,768]{1,0:T(8,128)(2,1)} %bitcast.190, bf16[3072,768]{1,0:T(8,128)(2,1)} %bitcast.191), custom_call_target="tpu_custom_call" | custom-call | flops 38654705664 | bytes 6291456 | tf_op jit(solution)/shard_map/pallas_call | solution.py:126
  255.8 12.3 fusion.72
  268.1 11.6 all-to-all-done.1
  285.8 32.4 %all-gather.10.cloned.1.call-done = bf16[4,256,4096]{2,1,0:T(8,128)(2,1)} async-done(((bf16[4,8,4096]{2,1,0:T(8,128)(2,1)}), bf16[4,256,4096]{2,1,0:T(8,128)(2,1)}) %all-gather.10.cloned.1.call-update) | async-done | bytes 8388624 | tf_op jit(solution)/shard_map/all_gather | solution.py:393
  318.2 22.8 %fusion.6 = (bf16[768,4096]{1,0:T(8,128)(2,1)}, f32[768,4096]{1,0:T(8,128)}) fusion(f32[768,4096]{1,0:T(8,128)} %fusion.72, bf16[1024,4096]{1,0:T(8,128)(2,1)} %bitcast.232, f32[768,1024]{1,0:T(8,128)} %copy-done.5, f32[1024]{0:T(1024)S(1)} %bitcast.219, f32[768]{0:T(1024)S(1)} %add_rsqrt_fusion, f32[768]{0:T(1024)S(1)} %broadcast_multiply_fusion.4), kind=kOutput, calls=%fused_computation.8 | convolution fusion | flops 6508511232 | bytes 43001856 | tf_op jit(solution)/shard_map/dot_general | solution.py:413
  341.1 12.1 multiply_reduce_fusion
  356.8 23.5 %all_to_all.30 = bf16[4,768,256]{2,1,0:T(8,128)(2,1)} all-to-all(bf16[4,768,256]{2,1,0:T(8,128)(2,1)S(1)} %bitcast.187), channel_id=1, replica_groups=mesh['wide'=8,'narrow'=4] {'narrow'}, dimensions={0} | all-to-all | bytes 3145728 | tf_op jit(solution)/shard_map/all_to_all | solution.py:341
  380.3 99.7 %shard_map.289 = (bf16[3072,256]{1,0:T(8,128)(2,1)S(1)}, bf16[3072,256]{1,0:T(8,128)(2,1)S(1)}, bf16[3072,256]{1,0:T(8,128)(2,1)S(1)}) custom-call(s32[1]{0:T(128)S(6)} %copy.272.length_ref, bf16[3072,768]{1,0:T(8,128)(2,1)} %bitcast.192, bf16[3072,768]{1,0:T(8,128)(2,1)} %bitcast.193, bf16[3072,768]{1,0:T(8,128)(2,1)} %bitcast.194, ...), custom_call_target="tpu_custom_call" | custom-call | flops 96636764160 | bytes 12582912 | tf_op jit(solution)/shard_map/pallas_call | solution.py:202
  504.1 51.0 %all-to-all-done.3 = bf16[4,768,768]{1,2,0:T(8,128)(2,1)} async-done(((bf16[4,768,768]{1,2,0:T(8,128)(2,1)}), bf16[4,768,768]{1,2,0:T(8,128)(2,1)}, u32[]{:S(2)}, u32[]{:S(2)}) %all-to-all-start.3) | async-done | bytes 4718624 | tf_op jit(solution)/shard_map/all_to_all | solution.py:341
  620.1 19.3 %copy.232 = bf16[4,256,4096]{2,0,1:T(4,128)(2,1)} copy(bf16[4,256,4096]{2,1,0:T(8,128)(2,1)S(1)} %bitcast.182) | data formatting | bytes 16777216
  639.4 15.5 %copy.240 = bf16[32,8,4,4096]{3,1,2,0:T(8,128)(2,1)} copy(bf16[32,8,4,4096]{3,2,1,0:T(4,128)(2,1)} %bitcast.177) | data formatting | bytes 16777216
  655.0 14.5 %convolution_convert_fusion = bf16[4096,1024]{1,0:T(8,128)(2,1)} fusion(bf16[768,1024]{1,0:T(8,128)(2,1)} %param.18, f32[768,4096]{1,0:T(8,128)} %get-tuple-element.66), kind=kOutput, calls=%fused_computation.10 | convolution fusion | flops 6474956800 | bytes 22544384 | tf_op jit(solution)/shard_map/tf,td->fd/dot_general | solution.py:418
  681.3 93.1 %reduce-scatter.16.cloned.1.call-done = f32[32,2]{1,0:T(8,128)} async-done(((f32[1024,2]{1,0:T(8,128)}), f32[32,2]{1,0:T(8,128)}) %reduce-scatter.16.cloned.1.call-update) | async-done | bytes 272
  775.9 114.6 %reduce-scatter.18.cloned.1.call-done = bf16[8,12288]{1,0:T(8,128)(2,1)} async-done(((bf16[256,12288]{1,0:T(8,128)(2,1)}), bf16[8,12288]{1,0:T(8,128)(2,1)}) %reduce-scatter.18.cloned.1.call-update) | async-done | bytes 196624
  899.3 141.4 %reduce-scatter.22.cloned.1.call-done = bf16[8,16384]{1,0:T(8,128)(2,1)} async-done(((bf16[256,16384]{1,0:T(8,128)(2,1)}), bf16[8,16384]{1,0:T(8,128)(2,1)}) %reduce-scatter.22.cloned.1.call-update) | async-done | bytes 262160
  1043.6 144.2 %reduce-scatter.24.cloned.1.call-done = bf16[8,16384]{1,0:T(8,128)(2,1)} async-done(((bf16[256,16384]{1,0:T(8,128)(2,1)}), bf16[8,16384]{1,0:T(8,128)(2,1)}) %reduce-scatter.24.cloned.1.call-update) | async-done | bytes 262160
  1192.6 36.8 %psum.7 = f32[]{:T(128)} all-reduce(f32[]{:T(128)S(6)} %add.103), channel_id=1, replica_groups=mesh['wide'=8,'narrow'=4] {'wide','narrow'}, use_global_device_ids=true, to_apply=%region_20.0 | all-reduce | flops 1 | bytes 8 | tf_op jit(solution)/shard_map/psum | solution.py:359
  1242.5 14.2 %add_convert_fusion = bf16[768,1024]{1,0:T(8,128)(2,1)} fusion(f32[768,1024]{1,0:T(8,128)S(1)} %copy-done.7, bf16[4096,1024]{1,0:T(8,128)(2,1)} %bitcast.231, f32[768,4096]{1,0:T(8,128)} %get-tuple-element.66), kind=kOutput, calls=%fused_computation.41 | convolution fusion | flops 6472335360 | bytes 25690112 | tf_op jit(solution)/shard_map/dot_general | solution.py:415
  1264.3 23.9 %shard_map.290 = (bf16[6,256,256]{2,1,0:T(8,128)(2,1)S(1)}, f32[6,256,256]{2,1,0:T(8,128)}, f32[6,256,256]{2,1,0:T(8,128)}, f32[6,256,256]{2,1,0:T(8,128)}, f32[...) custom-call(f32[6,256,256]{2,1,0:T(8,128)S(1)} %copy_bitcast_fusion.1.g_ref, ...), custom_call_target="tpu_custom_call" | custom-call | flops 12079595520 | bytes 23592960 | tf_op jit(solution)/shard_map/pallas_call | solution.py:264
  1293.0 54.8 %shard_map.291 = f32[12,256,256]{2,1,0:T(8,128)S(1)} custom-call(f32[12,256,256]{2,1,0:T(8,128)} %bitcast.235, f32[12,256,256]{2,1,0:T(8,128)} %bitcast.236), custom_call_target="tpu_custom_call" | custom-call | flops 40265318400 | bytes 9437184 | tf_op jit(solution)/shard_map/pallas_call | solution.py:324
  (198 shorter events, 194.3 us)
Async XLA Ops:
  7.2 50.4 %copy-start.2 = (bf16[768,1024]{1,0:T(8,128)(2,1)S(1)}, bf16[768,1024]{1,0:T(8,128)(2,1)}, u32[]{:S(2)}) copy-start(bf16[768,1024]{1,0:T(8,128)(2,1)} %param.17) | copy-start | bytes 4718596
  7.2 76.8 %all-gather.6.cloned.1.call-start = ((), (), s32[]{:S(2)}) async-start(), calls=%async_computation.11 | async-start | bytes 6488064 | tf_op jit(solution)/shard_map/all_gather | solution.py:393
  9.1 246.7 %all-gather.12.cloned.1.call-start = ((), (), s32[]{:S(2)}) async-start(), calls=%async_computation.14 | async-start | bytes 8650752 | tf_op jit(solution)/shard_map/all_gather | solution.py:393
  10.9 257.2 %all-gather.8.cloned.1.call-start = ((), (), s32[]{:S(2)}) async-start(), calls=%async_computation.12 | async-start | bytes 2162688 | tf_op jit(solution)/shard_map/all_gather | solution.py:393
  12.6 305.7 %all-gather.10.cloned.1.call-start = ((), (), s32[]{:S(2)}) async-start(), calls=%async_computation.13 | async-start | bytes 8650752 | tf_op jit(solution)/shard_map/all_gather | solution.py:393
  58.5 294.7 %copy-start.25 = (f32[1,1024]{1,0:T(1,128)}, f32[1,1024]{1,0:T(1,128)S(1)}, u32[]{:S(2)}) copy-start(f32[1,1024]{1,0:T(1,128)S(1)} %get-tuple-element.61) | copy-start | bytes 12292
  109.6 73.8 %all-to-all-start = ((bf16[4,768,768]{1,2,0:T(8,128)(2,1)}), bf16[4,768,768]{1,2,0:T(8,128)(2,1)}, u32[]{:S(2)}, u32[]{:S(2)}) async-start(bf16[4,768,768]{1,2,0:T(8,128)(2,1)} %bitcast.180), calls=%async_computation | async-start | bytes 9437184 | tf_op jit(solution)/shard_map/all_to_all | solution.py:341
  252.1 27.6 %all-to-all-start.1 = ((bf16[4,768,256]{2,1,0:T(8,128)(2,1)}), bf16[4,768,256]{2,1,0:T(8,128)(2,1)S(1)}, u32[]{:S(2)}, u32[]{:S(2)}) async-start(bf16[4,768,256]{2,1,0:T(8,128)(2,1)} %bitcast.9), calls=%async_computation.1 | async-start | bytes 3145728 | tf_op jit(solution)/shard_map/all_to_all | solution.py:341
  283.8 69.4 %copy-start.19 = (f32[768]{0:T(1024)}, f32[768]{0:T(1024)S(1)}, u32[]{:S(2)}) copy-start(f32[768]{0:T(1024)S(1)} %broadcast_multiply_fusion.4) | copy-start | bytes 9220
  285.8 67.3 %copy-start.23 = (f32[768]{0:T(1024)}, f32[768]{0:T(1024)S(1)}, u32[]{:S(2)}) copy-start(f32[768]{0:T(1024)S(1)} %add_rsqrt_fusion) | copy-start | bytes 9220
  354.5 142.5 %copy-start.8 = (f32[768,1024]{1,0:T(8,128)}, f32[768,1024]{1,0:T(8,128)S(1)}, u32[]{:S(2)}) copy-start(f32[768,1024]{1,0:T(8,128)S(1)} %multiply_add_fusion) | copy-start | bytes 9437188
  488.9 66.2 %all-to-all-start.3 = ((bf16[4,768,768]{1,2,0:T(8,128)(2,1)}), bf16[4,768,768]{1,2,0:T(8,128)(2,1)}, u32[]{:S(2)}, u32[]{:S(2)}) async-start(bf16[4,768,768]{1,2,0:T(8,128)(2,1)} %copy.196), calls=%async_computation.3 | async-start | bytes 9437184 | tf_op jit(solution)/shard_map/all_to_all | solution.py:341
  493.9 185.2 %reduce-scatter.20.cloned.1.call-start = ((), (), s32[]{:S(2)}) async-start(), calls=%async_computation.17 | async-start | bytes 2162688
  501.8 53.3 %copy-start.3 = (bf16[768,1024]{1,0:T(8,128)(2,1)S(1)}, bf16[768,1024]{1,0:T(8,128)(2,1)}, u32[]{:S(2)}) copy-start(bf16[768,1024]{1,0:T(8,128)(2,1)} %param.17) | copy-start | bytes 4718596
  501.8 53.3 %copy-start.22 = (f32[768]{0:T(1024)S(1)}, f32[768]{0:T(1024)}, u32[]{:S(2)}) copy-start(f32[768]{0:T(1024)} %copy-done.21) | copy-start | bytes 9220
  501.8 53.3 %copy-start.28 = (f32[768]{0:T(1024)S(1)}, f32[768]{0:T(1024)}, u32[]{:S(2)}) copy-start(f32[768]{0:T(1024)} %copy-done.27) | copy-start | bytes 9220
  501.9 53.3 %copy-start.30 = (f32[1,1024]{1,0:T(1,128)S(1)}, f32[1,1024]{1,0:T(1,128)}, u32[]{:S(2)}) copy-start(f32[1,1024]{1,0:T(1,128)} %copy-done.29) | copy-start | bytes 12292
  504.1 270.4 %reduce-scatter.16.cloned.1.call-start = ((), (), s32[]{:S(2)}) async-start(), calls=%async_computation.15 | async-start | bytes 540672
  567.8 322.7 %reduce-scatter.18.cloned.1.call-start = ((), (), s32[]{:S(2)}) async-start(), calls=%async_computation.16 | async-start | bytes 6488064
  608.0 432.8 %reduce-scatter.22.cloned.1.call-start = ((), (), s32[]{:S(2)}) async-start(), calls=%async_computation.18 | async-start | bytes 8650752
  655.0 532.9 %reduce-scatter.24.cloned.1.call-start = ((), (), s32[]{:S(2)}) async-start(), calls=%async_computation.19 | async-start | bytes 8650752
  1192.6 40.7 %copy-start.18 = (f32[48,8,256]{2,0,1:T(8,128)S(1)}, f32[48,8,256]{2,0,1:T(8,128)}, u32[]{:S(2)}) copy-start(f32[48,8,256]{2,0,1:T(8,128)} %copy.203) | copy-start | bytes 1179652
  1236.9 26.1 %all-to-all-start.4 = ((bf16[6,32,8,256]{3,2,0,1:T(8,128)(2,1)}), bf16[6,32,8,256]{3,2,0,1:T(8,128)(2,1)}, u32[]{:S(2)}, u32[]{:S(2)}) async-start(bf16[6,32,8,256]{3,2,0,1:T(8,128)(2,1)} %copy.206), calls=%async_computation.4 | async-start | bytes 1572864 | tf_op jit(solution)/shard_map/all_to_all | solution.py:473
  1289.1 60.5 %all-to-all-start.5 = ((bf16[6,32,8,256]{3,2,0,1:T(8,128)(2,1)}), bf16[6,32,8,256]{3,2,0,1:T(8,128)(2,1)S(1)}, u32[]{:S(2)}, u32[]{:S(2)}) async-start(bf16[6,32,8,256]{3,2,0,1:T(8,128)(2,1)} %copy.208), calls=%async_computation.5 | async-start | bytes 1572864 | tf_op jit(solution)/shard_map/all_to_all | solution.py:488
  (31 other events, 278.5 us)
Sparse Core Ops, SparseCore 0:
  11.5 72.3 all-gather.5
  87.5 90.6 all-gather.11
  181.6 54.8 all-gather.7
  239.9 78.2 all-gather.9
  504.2 137.5 reduce-scatter.19
  644.6 129.8 reduce-scatter.15
  780.1 110.2 reduce-scatter.17
  892.8 147.9 reduce-scatter.21
  1043.2 144.6 reduce-scatter.23

commit v2 on v1

--- a/solution.py
+++ b/solution.py
@@ -27,7 +27,9 @@
 PAIR = 2 * HEAD
 NT = (((1,), (1,)), ((), ()))
 TN = (((0,), (0,)), ((), ()))
+MESH = pl.DeviceIdType.MESH
 VMEM_LIMIT = 48 * 2**20
+AHEAD = 4
 
 
 def shortened(shard):
@@ -49,19 +51,6 @@
         - normed * jnp.mean(scaled * normed, -1, keepdims=True)
     )
     return (d_input, d_gain)
-
-
-def as_layout(matrix):
-    return matrix.reshape(matrix.shape[0] // BLOCK, BLOCK, matrix.shape[1])
-
-
-def to_pieces(shard):
-    band_count, band_rows, col_count = shard.shape
-    return (
-        shard.reshape(band_count, band_rows, col_count // BLOCK, BLOCK)
-        .transpose(0, 2, 1, 3)
-        .reshape(-1, band_rows, BLOCK)
-    )
 
 
 def from_pieces(pieces, band_count, col_count):
@@ -232,10 +221,10 @@
 
 
 def soap_kernel(
-    g_ref, first_ref, second_ref, ls_ref, rs_ref, lb_ref, rb_ref,
+    factor_ref, g_ref, first_ref, second_ref, ls_ref, rs_ref, lb_ref, rb_ref,
     back_ref, first_out, second_out, ls_out, rs_out, gram_ref, turn_ref,
 ):
-    gradient = g_ref[0].astype(float32)
+    gradient = factor_ref[0, 0] * g_ref[0].astype(float32)
     left_base, right_base = lb_ref[0], rb_ref[0]
     left_new = decay_rate * ls_ref[0] + (1.0 - decay_rate) * exact(gradient, gradient, NT)
     right_new = decay_rate * rs_ref[0] + (1.0 - decay_rate) * exact(gradient, gradient, TN)
@@ -255,7 +244,7 @@
         gram_ref[0, side] = exact(turn, turn, NT)
 
 
-def soap_update(gradient, first_old, second_old, left_old, right_old, left_base, right_base):
+def soap_update(factor, gradient, first_old, second_old, left_old, right_old, left_base, right_base):
     slots, order, _ = gradient.shape
     one = pl.BlockSpec((1, order, order), lambda s: (s, 0, 0))
     two = pl.BlockSpec((1, 2, order, order), lambda s: (s, 0, 0, 0))
@@ -264,14 +253,14 @@
     return pl.pallas_call(
         soap_kernel,
         grid=(slots,),
-        in_specs=[one] * 7,
+        in_specs=[pl.BlockSpec(memory_space=pltpu.SMEM)] + [one] * 7,
         out_specs=[one] * 5 + [two] * 2,
         out_shape=[jax.ShapeDtypeStruct((slots, order, order), bfloat16)] + [single] * 4 + [double] * 2,
         compiler_params=pltpu.CompilerParams(vmem_limit_bytes=VMEM_LIMIT),
         cost_estimate=pl.CostEstimate(
             flops=slots * 120 * order**3, bytes_accessed=slots * 60 * order**2, transcendentals=0
         ),
-    )(gradient, first_old, second_old, left_old, right_old, left_base, right_base)
+    )(factor.reshape(1, 1), gradient, first_old, second_old, left_old, right_old, left_base, right_base)
 
 
 def renew_kernel(rows, gram_ref, turn_ref, q_ref, x_ref, u_ref):
@@ -341,10 +330,228 @@
     return lax.all_to_all(groups, "narrow", split_axis=0, concat_axis=0, tiled=True)
 
 
-def scattered(layout, dimension):
-    return lax.psum_scatter(
-        layout.astype(bfloat16), ("wide", "narrow"), scatter_dimension=dimension, tiled=True
-    ).astype(float32)
+def partner(bit, narrow_bits):
+    axis, step = ("narrow", 1 << bit) if bit < narrow_bits else ("wide", 1 << (bit - narrow_bits))
+    place = lax.axis_index(axis)
+    mine = lax.rem(place // step, 2)
+    return {axis: place + step - 2 * step * mine}, mine
+
+
+def greet(peers):
+    barrier = pltpu.get_barrier_semaphore()
+    for device, _ in peers:
+        pl.semaphore_signal(barrier, inc=1, device_id=device, device_id_type=MESH)
+    pl.semaphore_wait(barrier, len(peers))
+
+
+def mesh_bits():
+    narrow_bits = lax.axis_size("narrow").bit_length() - 1
+    return narrow_bits + lax.axis_size("wide").bit_length() - 1, narrow_bits
+
+
+def reduce_kernel(bits, narrow_bits, plans, chunks, count, *refs):
+    sources, outs, scratch = refs[:count], refs[count : 2 * count], refs[2 * count :]
+    held = scratch[:count]
+    arrived = [scratch[count * (1 + s) : count * (2 + s)] for s in range(bits)]
+    load_sem, send_sem, recv_sem = scratch[count * (1 + bits) :]
+    peers = [partner(b, narrow_bits) for b in range(bits)]
+    greet(peers)
+    first = plans[0][0]
+    order_of_dims = list(reversed(range(bits)))
+    whole = slice(None)
+
+    def within(order, stage, current):
+        return tuple(
+            peers[b][1] if b in order[:stage] else current if b == order[stage] else whole
+            for b in order_of_dims
+            if b != first
+        )
+
+    def of_source(value):
+        return tuple(value if b == first else whole for b in order_of_dims)
+
+    def rows_of(chunk):
+        at, row, rows, colour = chunks[chunk]
+        return at, plans[colour], (pl.ds(row, rows), whole)
+
+    def send(chunk, stage):
+        at, order, part = rows_of(chunk)
+        device, mine = peers[order[stage]]
+        if stage == 0:
+            source = sources[at].at[of_source(1 - mine) + part]
+        else:
+            source = held[at].at[within(order, stage, 1 - mine) + part]
+        return pltpu.make_async_remote_copy(
+            src_ref=source,
+            dst_ref=arrived[stage][at].at[(whole,) * (bits - 1 - stage) + part],
+            send_sem=send_sem.at[chunk, stage],
+            recv_sem=recv_sem.at[chunk, stage],
+            device_id=device,
+            device_id_type=MESH,
+        )
+
+    def load(chunk):
+        at, order, part = rows_of(chunk)
+        return pltpu.make_async_copy(
+            sources[at].at[of_source(peers[first][1]) + part],
+            held[at].at[(whole,) * (bits - 1) + part],
+            load_sem.at[chunk],
+        )
+
+    def begin(chunk):
+        send(chunk, 0).start()
+        load(chunk).start()
+
+    def finish(chunk, stage):
+        at, order, part = rows_of(chunk)
+        if stage == 0:
+            load(chunk).wait()
+        send(chunk, stage).wait_recv()
+        left = bits - 1 - stage
+        keep = within(order, stage, peers[order[stage]][1])
+        if left == 0:
+            own = held[at][keep + part].astype(float32)
+            outs[at][part] = own + arrived[stage][at][part].astype(float32)
+            return
+        free = [i for i, k in enumerate(keep) if isinstance(k, slice)]
+
+        def add(m, carry):
+            which = tuple(m // (1 << (left - 1 - i)) % 2 for i in range(left))
+            spot = list(keep)
+            for i, f in enumerate(free):
+                spot[f] = which[i]
+            spot = tuple(spot) + part
+            held[at][spot] = held[at][spot] + arrived[stage][at][which + part]
+            return carry
+
+        lax.fori_loop(0, 1 << left, add, 0)
+        send(chunk, stage + 1).start()
+
+    total = len(chunks)
+    for chunk in range(min(AHEAD, total)):
+        begin(chunk)
+    for step in range(total + 2 * bits):
+        for stage in reversed(range(bits)):
+            chunk = step - 2 * stage
+            if 0 <= chunk < total:
+                finish(chunk, stage)
+                if stage == 0 and chunk + AHEAD < total:
+                    begin(chunk + AHEAD)
+    for chunk in range(total):
+        for stage in range(bits):
+            send(chunk, stage).wait_send()
+
+
+def reduce_to_shards(parts, pieces, collective_id):
+    bits, narrow_bits = mesh_bits()
+    shapes = [part.shape[1:] for part in parts]
+    kinds = [part.dtype for part in parts]
+    chunks = []
+    for at, (shape, cut) in enumerate(zip(shapes, pieces)):
+        rows = shape[0] // cut
+        chunks += [(at, row, rows, len(chunks) % 2) for row in range(0, shape[0], rows)]
+        chunks = [(a, r, n, i % 2) for i, (a, r, n, _) in enumerate(chunks)]
+    later = tuple(range(3, bits))
+    plans = ((0, 2, 1) + later, (0, 1, 2) + later)
+    sizes = [bits - 1] + [bits - 1 - stage for stage in range(bits)]
+    scratch = [
+        pltpu.VMEM((2,) * size + shape, kind)
+        for size in sizes
+        for shape, kind in zip(shapes, kinds)
+    ]
+    total = len(chunks)
+    scratch += [
+        pltpu.SemaphoreType.DMA((total,)),
+        pltpu.SemaphoreType.DMA((total, bits)),
+        pltpu.SemaphoreType.DMA((total, bits)),
+    ]
+    return pl.pallas_call(
+        partial(reduce_kernel, bits, narrow_bits, plans, tuple(chunks), len(parts)),
+        out_shape=[jax.ShapeDtypeStruct(shape, float32) for shape in shapes],
+        in_specs=[pl.BlockSpec(memory_space=pl.ANY)] * len(parts),
+        out_specs=[pl.BlockSpec(memory_space=pltpu.VMEM)] * len(parts),
+        scratch_shapes=scratch,
+        compiler_params=pltpu.CompilerParams(
+            collective_id=collective_id, has_side_effects=True, vmem_limit_bytes=58 * 2**20
+        ),
+        cost_estimate=pl.CostEstimate(flops=10**8, bytes_accessed=4 * 10**8, transcendentals=0),
+    )(*(part.reshape((2,) * bits + shape) for part, shape in zip(parts, shapes)))
+
+
+def total_kernel(bits, narrow_bits, own_ref, sum_ref, arrived, send_sem, recv_sem):
+    peers = [partner(b, narrow_bits) for b in range(bits)]
+    greet(peers)
+    sum_ref[...] = own_ref[...]
+    for stage in range(bits):
+        copy = pltpu.make_async_remote_copy(
+            src_ref=sum_ref,
+            dst_ref=arrived.at[stage],
+            send_sem=send_sem.at[stage],
+            recv_sem=recv_sem.at[stage],
+            device_id=peers[stage][0],
+            device_id_type=MESH,
+        )
+        copy.start()
+        copy.wait()
+        sum_ref[...] = sum_ref[...] + arrived[stage]
+
+
+def total_of(value, collective_id):
+    bits, narrow_bits = mesh_bits()
+    tile = (8, 128)
+    return pl.pallas_call(
+        partial(total_kernel, bits, narrow_bits),
+        out_shape=jax.ShapeDtypeStruct(tile, float32),
+        in_specs=[pl.BlockSpec(memory_space=pltpu.VMEM)],
+        out_specs=pl.BlockSpec(memory_space=pltpu.VMEM),
+        scratch_shapes=[
+            pltpu.VMEM((bits,) + tile, float32),
+            pltpu.SemaphoreType.DMA((bits,)),
+            pltpu.SemaphoreType.DMA((bits,)),
+        ],
+        compiler_params=pltpu.CompilerParams(collective_id=collective_id, has_side_effects=True),
+    )(jnp.broadcast_to(value, tile))[0, 0]
+
+
+def weight_grad_kernel(columns, band_rows, left_ref, right_ref, out_ref):
+    left = left_ref[...].T
+    for at in range(0, len(columns), 2):
+        blocks = []
+        for group, start in columns[at : at + 2]:
+            block = jnp.dot(
+                left, right_ref[group, :, start : start + BLOCK], preferred_element_type=float32
+            )
+            blocks.append(block.astype(bfloat16).reshape(-1, band_rows, BLOCK))
+        out_ref[:, at * band_rows : (at + 2) * band_rows, :] = jnp.concatenate(blocks, 1)
+
+
+def weight_grad(left, right, columns, device_count):
+    tok_rows, height = left.shape
+    band_rows = BLOCK // device_count
+    bands, wide = height // BLOCK, len(columns)
+    if band_rows % 8:
+        product = jnp.einsum("td,gte->dge", left, right, preferred_element_type=float32)
+        product = jnp.concatenate(
+            [product[:, group, start : start + BLOCK] for group, start in columns], 1
+        )
+        product = product.astype(bfloat16).reshape(bands, device_count, band_rows, wide, BLOCK)
+        return product.transpose(1, 0, 3, 2, 4).reshape(device_count, -1, BLOCK)
+    return pl.pallas_call(
+        partial(weight_grad_kernel, columns, band_rows),
+        grid=(bands,),
+        in_specs=[
+            pl.BlockSpec((tok_rows, BLOCK), lambda i: (0, i)),
+            pl.BlockSpec(right.shape, lambda i: (0, 0, 0)),
+        ],
+        out_specs=pl.BlockSpec((device_count, wide * band_rows, BLOCK), lambda i: (0, i, 0)),
+        out_shape=jax.ShapeDtypeStruct((device_count, bands * wide * band_rows, BLOCK), bfloat16),
+        compiler_params=pltpu.CompilerParams(vmem_limit_bytes=VMEM_LIMIT),
+        cost_estimate=pl.CostEstimate(
+            flops=2 * tok_rows * bands * wide * BLOCK**2,
+            bytes_accessed=2 * (tok_rows * (height + wide * BLOCK) + bands * wide * BLOCK**2),
+            transcendentals=0,
+        ),
+    )(left, right)
 
 
 def unpack(gathered):
@@ -353,10 +560,6 @@
         for layout in gathered[:4]
     ]
     return (matrices, gathered[4].astype(jnp.float32))
-
-
-def global_norm(squares):
-    return jnp.sqrt(lax.psum(squares, ("wide", "narrow")))
 
 
 def body(
@@ -415,17 +618,17 @@
     block_out = (middle + jnp.dot(active, w_back, preferred_element_type=jnp.float32)).astype(
         jnp.bfloat16
     )
-    d_back = jnp.einsum("tf,td->fd", active, cotangent, preferred_element_type=jnp.float32)
+    plain = lambda size: tuple((0, start) for start in range(0, size, BLOCK))
+    d_back = weight_grad(active, cotangent[None], plain(width), device_count)
     d_active = jnp.einsum("td,fd->tf", cotangent, w_back, preferred_element_type=jnp.float32)
     _, gelu_pull = jax.vjp(partial(jax.nn.gelu, approximate=True), hidden)
     d_hidden = gelu_pull(d_active)[0].astype(jnp.bfloat16)
-    d_w_hidden = jnp.einsum("td,tf->df", act_two, d_hidden, preferred_element_type=jnp.float32)
+    d_w_hidden = weight_grad(act_two, d_hidden[None], plain(FF), device_count)
     d_act_two = jnp.einsum("tf,df->td", d_hidden, w_hidden, preferred_element_type=jnp.float32)
     d_norm_two, d_gain_two = norm_backward(d_act_two, normed_two, inverse_two, gain_pair[1])
     d_middle = cotangent.astype(jnp.float32) + d_norm_two
-    mlp_sums = (scattered(as_layout(d_w_hidden), 1), scattered(as_layout(d_back), 1))
     d_branch = d_middle.astype(jnp.bfloat16)
-    d_proj = jnp.einsum("td,te->de", merged, d_branch, preferred_element_type=jnp.float32)
+    d_proj = weight_grad(merged, d_branch[None], plain(width), device_count)
     d_merged = jnp.einsum("te,de->td", d_branch, w_proj, preferred_element_type=jnp.float32).astype(
         jnp.bfloat16
     )
@@ -433,7 +636,13 @@
     d_mixed = exchange(d_mixed).reshape(seq_len, head_width)
     d_scene = jnp.concatenate(attend_backward(lengths, scene, mixed, d_mixed, log_totals, safe), 1)
     d_packed = exchange(d_scene.reshape(narrow_count, tok_rows, 3 * head_width))
-    d_attn = jnp.einsum("td,gtc->gdc", act_one, d_packed, preferred_element_type=jnp.float32)
+    grouped = tuple(
+        (group, third * head_width + start)
+        for third in range(3)
+        for group in range(narrow_count)
+        for start in range(0, head_width, BLOCK)
+    )
+    d_attn = weight_grad(act_one, d_packed, grouped, device_count)
     d_act_one = jnp.einsum(
         "gtke,dkge->td",
         d_packed.reshape(narrow_count, tok_rows, 3, head_width),
@@ -442,23 +651,18 @@
     )
     d_norm_one, d_gain_one = norm_backward(d_act_one, normed_one, inverse_one, gain_pair[0])
     grad_tokens = (d_middle + d_norm_one).astype(jnp.bfloat16)
-    attn_sum = scattered(d_attn.reshape(narrow_count, -1, BLOCK, 3 * head_width), 2)
-    band_rows = attn_sum.shape[2]
-    attn_sum = attn_sum.reshape(narrow_count, -1, band_rows, 3, head_width)
-    attn_sum = attn_sum.transpose(1, 2, 3, 0, 4).reshape(-1, band_rows, 3 * width)
-    attn_sums = (
-        attn_sum,
-        scattered(as_layout(d_proj), 1),
-        lax.psum_scatter(
-            jnp.stack([d_gain_one, d_gain_two]), ("wide", "narrow"), scatter_dimension=1, tiled=True
-        ),
-    )
-    grad_shards = (attn_sums[0], attn_sums[1], mlp_sums[0], mlp_sums[1])
-    gain_grad = attn_sums[2]
+    share = width // device_count
+    gain_parts = jnp.stack([d_gain_one, d_gain_two]).reshape(2, device_count, share)
+    gain_parts = jnp.pad(gain_parts.transpose(1, 0, 2), ((0, 0), (0, 6), (0, 128 - share)))
+    *grad_shards, gain_grad = reduce_to_shards(
+        (d_attn, d_proj, d_w_hidden, d_back, gain_parts), (6, 2, 8, 8, 1), 1
+    )
+    gain_grad = gain_grad[:2, :share]
+    band_rows = BLOCK // device_count
     local_squares = jnp.sum(gain_grad * gain_grad) + sum(
         (jnp.sum(shard * shard) for shard in grad_shards)
     )
-    pieces = jnp.concatenate([to_pieces(shard) for shard in grad_shards], 0)
+    pieces = jnp.concatenate(grad_shards, 0).reshape(-1, band_rows, BLOCK)
     block_count = pieces.shape[0]
     order = lax.iota(jnp.int32, block_count)
     earlier = (owners[None, :] == owners[:, None]) & (order[None, :] < order[:, None])
@@ -467,19 +671,18 @@
         jnp.float32
     )
     routing = routing.reshape(device_count, cap_slots, block_count)
-    grad_norm = global_norm(local_squares)
+    grad_norm = jnp.sqrt(total_of(local_squares, 2))
     factor = jnp.minimum(1.0, clip_bound / grad_norm)
-    outgoing = pieces * factor
     arrived = lax.all_to_all(
-        jnp.einsum("okb,bxy->koxy", routing, outgoing, precision=highest).astype(jnp.bfloat16),
+        jnp.einsum("okb,bxy->koxy", routing, pieces, precision=highest).astype(jnp.bfloat16),
         ("wide", "narrow"),
         split_axis=1,
         concat_axis=1,
         tiled=True,
-    ).astype(jnp.float32)
+    )
     slot_grads = arrived.reshape(cap_slots, BLOCK, BLOCK)
     restored, first_new, second_new, left_new, right_new, gram, turn = soap_update(
-        slot_grads, moment_first, moment_second, left_stat, right_stat, left_basis, right_basis
+        factor, slot_grads, moment_first, moment_second, left_stat, right_stat, left_basis, right_basis
     )
     square = (-1, BLOCK, BLOCK)
     bases = renew_bases(gram.reshape(square), turn.reshape(square))

time: 1370 us -> 841 us (0.61)
  waiting for transfers between devices: 685 us -> 144 us
  Pallas kernels: 240 us -> 422 us
  local copies, waits for them, and re-layouts: 131 us -> 42.2 us
  matrix products: 130 us -> 86.5 us
  blocking collectives: 103 us -> 66.6 us
    unnamed x14 -> x4, waiting for transfers between devices: 494 us -> 0.07 us
    pallas_call x1 -> x7, Pallas kernels: 23.9 us -> 206 us  [the longest x1 124 us: reduce_to_shards(): pl.pallas_call(partial(reduce_kernel, bits, narrow_bits, plans, tuple(chu...]
    unnamed x95 -> x70, local copies, waits for them, and re-layouts: 79.2 us -> 3.1 us
    all_to_all x3, waiting for transfers between devices: 130 us -> 88.8 us  [exchange(): lax.all_to_all(groups, 'narrow', split_axis=0, concat_axis=0, tiled=True)]
    dot_general x5 -> x1, matrix products: 39.9 us -> 1.36 us  [body(): jnp.einsum('okb,bxy->koxy', routing, pieces, precision=highest)]
    psum x1 -> x0, blocking collectives: 36.8 us -> none  [global_norm(): return jnp.sqrt(lax.psum(squares, ('wide', 'narrow')))]
  transfers between devices with their start and end apart: 14 -> 9, of which waited for: 10 -> 5; matrix products, arithmetic and copies ran while one was open for 16% -> 10% of each run, Pallas kernels for 9% -> 20%
where the time goes in v2:
time: 841 us; the launch traced here: 834 us
  Pallas kernels  422 us (50%)
  waiting for transfers between devices  144 us (17%)
  matrix products  86.5 us (10%)
  blocking collectives  66.6 us (8%)
  local copies, waits for them, and re-layouts  42.2 us (5%)
  other arithmetic  29.6 us (4%)
  starting transfers between devices  22.5 us (3%)
  between operations  20.7 us (2%)
    pallas_call x1, Pallas kernels, reduce_to_shards(): pl.pallas_call(partial(reduce_kernel, bits, narrow_bits, plans, tuple(chu...  124 us
    pallas_call x1, Pallas kernels, attend_backward(): pl.pallas_call(partial(attend_backward_kernel, safe, chunk), grid=(pairs,...  99.7 us
    all_to_all x3, waiting for transfers between devices, exchange(): lax.all_to_all(groups, 'narrow', split_axis=0, concat_axis=0, tiled=True)  88.8 us
    pallas_call x1, Pallas kernels, attend(): pl.pallas_call(partial(attend_kernel, safe, chunk), grid=(pairs, seq_len...  62 us
    all_gather x4, waiting for transfers between devices, body(): lax.all_gather(shortened(lowered), ('wide', 'narrow'), axis=1, tiled=True)  55.4 us
    pallas_call x1, Pallas kernels, renew_bases(): pl.pallas_call(partial(renew_kernel, rows), out_shape=jax.ShapeDtypeStruc...  54.8 us
    all_gather x1, blocking collectives, body(): lax.all_gather(shortened(lowered), ('wide', 'narrow'), axis=1, tiled=True)  43.1 us
    pallas_call x4, Pallas kernels, weight_grad(): pl.pallas_call(partial(weight_grad_kernel, columns, band_rows), grid=(ban...  41.5 us
  transfers between devices with their start and end apart: 9, of which 5 were waited for; matrix products, arithmetic and copies ran while one was open for 10% of the time, Pallas kernels for 20%

profile of v2, /device:TPU:0, one launch (start us, length us, event | category | flops | bytes accessed | tf_op | source)
XLA Modules:
  0.0 834.4 jit_solution(8912746581971398638)
XLA Ops:
  14.4 43.1 %all-gather = bf16[32,32,2]{1,2,0:T(2,128)(2,1)S(1)} all-gather(bf16[1,32,2]{1,2,0:T(2,128)(2,1)S(1)} %convert_bitcast_fusion.2), channel_id=1, replica_groups=mesh['wide'=8,'narrow'=4] {'wide','narrow'}, dimensions={0}, use_global_device_ids=true | all-gather | bytes 4224 | tf_op jit(solution)/shard_map/all_gather | solution.py:596
  59.6 24.4 %all-gather.6.cloned.1.call-done = bf16[4,256,3072]{2,1,0:T(8,128)(2,1)} async-done(((bf16[4,8,3072]{2,1,0:T(8,128)(2,1)}), bf16[4,256,3072]{2,1,0:T(8,128)(2,1)}) %all-gather.6.cloned.1.call-update) | async-done | bytes 6291472 | tf_op jit(solution)/shard_map/all_gather | solution.py:596
  84.0 12.2 %reshape.232 = bf16[1024,3,4,256]{3,2,1,0:T(4,128)(2,1)} reshape(bf16[4,256,3072]{2,1,0:T(8,128)(2,1)} %all-gather.6.cloned.1.call-done) | data formatting | bytes 12582912 | tf_op jit(solution)/shard_map/reshape;reshape | solution.py:606
  96.1 10.8 %convert_bitcast_fusion = bf16[4,768,3,256]{1,3,0,2:T(8,128)(2,1)S(1)} fusion(bf16[1024,3,4,256]{3,2,1,0:T(4,128)(2,1)} %reshape.232, bf16[768,1024]{1,0:T(8,128)(2,1)S(1)} %fusion.17.left_ref), kind=kOutput, calls=%fused_computation.18 | convolution fusion | flops 4834197504 | bytes 12582912 | tf_op jit(solution)/shard_map/td,dkge->gtke/dot_general | solution.py:607
  115.8 67.7 %all-to-all-done = bf16[4,768,768]{1,2,0:T(8,128)(2,1)} async-done(((bf16[4,768,768]{1,2,0:T(8,128)(2,1)}), bf16[4,768,768]{1,2,0:T(8,128)(2,1)}, u32[]{:S(2)}, u32[]{:S(2)}) %all-to-all-start) | async-done | bytes 4718624 | tf_op jit(solution)/shard_map/all_to_all | solution.py:330
  183.5 6.7 copy.128
  190.2 62.0 %shard_map.288 = (bf16[3072,256]{1,0:T(8,128)(2,1)}, f32[2,2,3072]{2,1,0:T(2,128)S(1)}) custom-call(s32[1]{0:T(128)S(6)} %copy.181.length_ref, bf16[3072,768]{1,0:T(8,128)(2,1)} %bitcast.134, bf16[3072,768]{1,0:T(8,128)(2,1)} %bitcast.135, bf16[3072,768]{1,0:T(8,128)(2,1)} %bitcast.136), custom_call_target="tpu_custom_call" | custom-call | flops 38654705664 | bytes 6291456 | tf_op jit(solution)/shard_map/pallas_call | solution.py:115
  256.8 12.6 %fusion.54 = f32[768,4096]{1,0:T(8,128)} fusion(bf16[768,1024]{1,0:T(8,128)(2,1)S(1)} %copy-done.1, bf16[4096,1024]{1,0:T(8,128)(2,1)} %bitcast.158), kind=kOutput, calls=%fused_computation.99 | convolution fusion | flops 6442450944 | bytes 22544384 | tf_op jit(solution)/shard_map/td,fd->tf/dot_general | solution.py:623
  269.4 11.4 %all-to-all-done.1 = bf16[4,768,256]{2,1,0:T(8,128)(2,1)} async-done(((bf16[4,768,256]{2,1,0:T(8,128)(2,1)}), bf16[4,768,256]{2,1,0:T(8,128)(2,1)}, u32[]{:S(2)}, u32[]{:S(2)}) %all-to-all-start.1) | async-done | bytes 1572896 | tf_op jit(solution)/shard_map/all_to_all | solution.py:330
  287.3 31.0 %all-gather.10.cloned.1.call-done = bf16[4,256,4096]{2,1,0:T(8,128)(2,1)} async-done(((bf16[4,8,4096]{2,1,0:T(8,128)(2,1)}), bf16[4,256,4096]{2,1,0:T(8,128)(2,1)}) %all-gather.10.cloned.1.call-update) | async-done | bytes 8388624 | tf_op jit(solution)/shard_map/all_gather | solution.py:596
  318.3 22.4 %fusion.6 = (bf16[768,4096]{1,0:T(8,128)(2,1)}, bf16[768,4096]{1,0:T(8,128)(2,1)}) fusion(f32[768,4096]{1,0:T(8,128)} %fusion.54, bf16[768,1024]{1,0:T(8,128)(2,1)S(1)} %multiply_convert_fusion.1.left_ref, bf16[1024,4096]{1,0:T(8,128)(2,1)} %bitcast.162), kind=kOutput, calls=%fused_computation.8 | convolution fusion | flops 6511656960 | bytes 35127296 | tf_op jit(solution)/shard_map/dot_general | solution.py:616
  340.7 12.0 %multiply_reduce_fusion = (f32[1024]{0:T(1024)S(1)}, f32[768]{0:T(1024)S(1)}, f32[768]{0:T(1024)S(1)}, f32[768,1024]{1,0:T(8,128)S(1)}) fusion(f32[768,1024]{1,0:T(8,128)S(1)} %copy-done.8, f32[768]{0:T(1024)S(1)} %add_rsqrt_fusion, f32[768]{0:T(1024)S(1)} %broadcast_multiply_fusion.4, f32[1024]{0:T(1024)S(1)} %bitcast.155, ...), kind=kOutput, calls=%fused_computation.34 | convolution fusion | flops 6448739328 | bytes 20992000 | tf_op jit(solution)/shard_map/tf,df->td/dot_general | solution.py:627
  357.0 23.5 %all_to_all.30 = bf16[4,768,256]{2,1,0:T(8,128)(2,1)} all-to-all(bf16[4,768,256]{2,1,0:T(8,128)(2,1)S(1)} %bitcast.132), channel_id=1, replica_groups=mesh['wide'=8,'narrow'=4] {'narrow'}, dimensions={0} | all-to-all | bytes 3145728 | tf_op jit(solution)/shard_map/all_to_all | solution.py:330
  380.5 99.7 %shard_map.289 = (bf16[3072,256]{1,0:T(8,128)(2,1)S(1)}, bf16[3072,256]{1,0:T(8,128)(2,1)S(1)}, bf16[3072,256]{1,0:T(8,128)(2,1)S(1)}) custom-call(s32[1]{0:T(128)S(6)} %copy.181.length_ref, bf16[3072,768]{1,0:T(8,128)(2,1)} %bitcast.137, bf16[3072,768]{1,0:T(8,128)(2,1)} %bitcast.138, bf16[3072,768]{1,0:T(8,128)(2,1)} %bitcast.139, ...), custom_call_target="tpu_custom_call" | custom-call | flops 96636764160 | bytes 12582912 | tf_op jit(solution)/shard_map/pallas_call | solution.py:191
  493.2 12.5 %shard_map.292 = bf16[32,512,256]{2,1,0:T(8,128)(2,1)} custom-call(bf16[768,1024]{1,0:T(8,128)(2,1)S(1)} %multiply_convert_fusion.1.left_ref, bf16[1,768,4096]{2,1,0:T(8,128)(2,1)} %bitcast.165), custom_call_target="tpu_custom_call" | custom-call | flops 6442450944 | bytes 16252928 | tf_op jit(solution)/shard_map/pallas_call | solution.py:539
  505.7 16.8 %shard_map.293 = bf16[32,512,256]{2,1,0:T(8,128)(2,1)} custom-call(bf16[768,4096]{1,0:T(8,128)(2,1)} %get-tuple-element.62.left_ref, bf16[1,768,1024]{2,1,0:T(8,128)(2,1)S(1)} %bitcast.125), custom_call_target="tpu_custom_call" | custom-call | flops 6442450944 | bytes 16252928 | tf_op jit(solution)/shard_map/pallas_call | solution.py:539
  522.6 9.6 %add_convert_fusion = bf16[768,1024]{1,0:T(8,128)(2,1)} fusion(f32[768,1024]{1,0:T(8,128)S(1)} %copy-done.9, bf16[768,4096]{1,0:T(8,128)(2,1)} %get-tuple-element.62.left_ref, bf16[4096,1024]{1,0:T(8,128)(2,1)S(1)} %bitcast.161), kind=kOutput, calls=%fused_computation.37 | convolution fusion | flops 6444023808 | bytes 19398656 | tf_op jit(solution)/shard_map/dot_general | solution.py:618
  532.2 9.8 %all-to-all-done.3.right_ref = bf16[4,768,768]{2,1,0:T(8,128)(2,1)} async-done(((bf16[4,768,768]{2,1,0:T(8,128)(2,1)}), bf16[4,768,768]{2,1,0:T(8,128)(2,1)}, u32[]{:S(2)}, u32[]{:S(2)}) %all-to-all-start.3) | async-done | bytes 4718624 | tf_op jit(solution)/shard_map/all_to_all | solution.py:330
  548.6 11.0 %fusion.23 = (f32[1024]{0:T(1024)S(1)}, f32[768]{0:T(1024)S(1)}, f32[768]{0:T(1024)S(1)}, f32[768,1024,1,1]{1,0,3,2:T(8,128)}) fusion(bf16[768,1024]{1,0:T(8,128)(2,1)S(1)} %copy-done.11, f32[768]{0:T(1024)S(1)} %copy-done.23, f32[768]{0:T(1024)S(1)} %copy-done.21, f32[1024]{0:T(1024)S(1)} %bitcast.152, bf16[4,768,3,256]{1,3,2,0:T(8,128)(2,1)} %bitcast.140, ...), kind=kOutput, calls=%fused_computation.31 | convolution fusion | flops 4838913024 | bytes 15749120 | tf_op jit(solution)/shard_map/gtke,dkge->td/dot_general | solution.py:646
  560.4 9.4 %shard_map.290 = bf16[32,384,256]{2,1,0:T(8,128)(2,1)} custom-call(bf16[768,1024]{1,0:T(8,128)(2,1)S(1)} %fusion.17.left_ref, bf16[4,768,768]{2,1,0:T(8,128)(2,1)} %all-to-all-done.3.right_ref), custom_call_target="tpu_custom_call" | custom-call | flops 4831838208 | bytes 12582912 | tf_op jit(solution)/shard_map/pallas_call | solution.py:539
  569.8 124.0 %shard_map.294 = (f32[384,256]{1,0:T(8,128)}, f32[128,256]{1,0:T(8,128)}, f32[512,256]{1,0:T(8,128)}, f32[512,256]{1,0:T(8,128)}, f32[8,128]{1,0:T(8,128)}) custom-call(bf16[2,2,2,2,2,384,256]{6,5,4,3,2,1,0:T(8,128)(2,1)} %bitcast.133, bf16[2,2,2,2,2,128,256]{6,5,4,3,2,1,0:T(8,128)(2,1)} %bitcast.123, bf16[2,2,2,2,2,512,256]{6,5,4,3,2,1,0:T(8,128)(2,1)} %bitcast.130, ...), custom_call_target="tpu_custom_call" | custom-call | flops 100000000 | bytes 400000000 | tf_op jit(solution)/shard_map/pallas_call | solution.py:468
  710.7 16.2 %shard_map.295 = f32[8,128]{1,0:T(8,128)} custom-call(f32[8,128]{1,0:T(8,128)} %broadcast_in_dim.11.own_ref), custom_call_target="tpu_custom_call" | custom-call | tf_op jit(solution)/shard_map/pallas_call | solution.py:502
  735.6 23.8 %shard_map.296 = (bf16[6,256,256]{2,1,0:T(8,128)(2,1)S(1)}, f32[6,256,256]{2,1,0:T(8,128)}, f32[6,256,256]{2,1,0:T(8,128)}, f32[6,256,256]{2,1,0:T(8,128)}, f32[...) custom-call(f32[1,1]{1,0:T(1,128)} %bitcast.34.factor_ref, ...), custom_call_target="tpu_custom_call" | custom-call | flops 12079595520 | bytes 23592960 | tf_op jit(solution)/shard_map/pallas_call | solution.py:253
  763.4 54.8 %shard_map.297 = f32[12,256,256]{2,1,0:T(8,128)S(1)} custom-call(f32[12,256,256]{2,1,0:T(8,128)} %bitcast.166, f32[12,256,256]{2,1,0:T(8,128)} %bitcast.167), custom_call_target="tpu_custom_call" | custom-call | flops 40265318400 | bytes 9437184 | tf_op jit(solution)/shard_map/pallas_call | solution.py:313
  (155 shorter events, 86.5 us)
Async XLA Ops:
  7.2 50.4 %copy-start.10 = (bf16[768,1024]{1,0:T(8,128)(2,1)S(1)}, bf16[768,1024]{1,0:T(8,128)(2,1)}, u32[]{:S(2)}) copy-start(bf16[768,1024]{1,0:T(8,128)(2,1)} %param.17) | copy-start | bytes 4718596
  7.2 76.8 %all-gather.6.cloned.1.call-start = ((), (), s32[]{:S(2)}) async-start(), calls=%async_computation.6 | async-start | bytes 6488064 | tf_op jit(solution)/shard_map/all_gather | solution.py:596
  9.1 247.7 %all-gather.12.cloned.1.call-start = ((), (), s32[]{:S(2)}) async-start(), calls=%async_computation.9 | async-start | bytes 8650752 | tf_op jit(solution)/shard_map/all_gather | solution.py:596
  10.9 258.5 %all-gather.8.cloned.1.call-start = ((), (), s32[]{:S(2)}) async-start(), calls=%async_computation.7 | async-start | bytes 2162688 | tf_op jit(solution)/shard_map/all_gather | solution.py:596
  12.6 305.7 %all-gather.10.cloned.1.call-start = ((), (), s32[]{:S(2)}) async-start(), calls=%async_computation.8 | async-start | bytes 8650752 | tf_op jit(solution)/shard_map/all_gather | solution.py:596
  109.6 73.9 %all-to-all-start = ((bf16[4,768,768]{1,2,0:T(8,128)(2,1)}), bf16[4,768,768]{1,2,0:T(8,128)(2,1)}, u32[]{:S(2)}, u32[]{:S(2)}) async-start(bf16[4,768,768]{1,2,0:T(8,128)(2,1)} %bitcast.129), calls=%async_computation | async-start | bytes 9437184 | tf_op jit(solution)/shard_map/all_to_all | solution.py:330
  252.1 28.6 %all-to-all-start.1 = ((bf16[4,768,256]{2,1,0:T(8,128)(2,1)}), bf16[4,768,256]{2,1,0:T(8,128)(2,1)}, u32[]{:S(2)}, u32[]{:S(2)}) async-start(bf16[4,768,256]{2,1,0:T(8,128)(2,1)} %bitcast.9), calls=%async_computation.1 | async-start | bytes 3145728 | tf_op jit(solution)/shard_map/all_to_all | solution.py:330
  318.3 22.4 %copy-start.8 = (f32[768,1024]{1,0:T(8,128)S(1)}, f32[768,1024]{1,0:T(8,128)}, u32[]{:S(2)}) copy-start(f32[768,1024]{1,0:T(8,128)} %copy-done.7) | copy-start | bytes 9437188
  340.7 12.0 %copy-start.2 = (bf16[768,1024]{1,0:T(8,128)(2,1)S(1)}, bf16[768,1024]{1,0:T(8,128)(2,1)}, u32[]{:S(2)}) copy-start(bf16[768,1024]{1,0:T(8,128)(2,1)} %param.18) | copy-start | bytes 4718596
  482.6 59.4 %all-to-all-start.3 = ((bf16[4,768,768]{2,1,0:T(8,128)(2,1)}), bf16[4,768,768]{2,1,0:T(8,128)(2,1)}, u32[]{:S(2)}, u32[]{:S(2)}) async-start(bf16[4,768,768]{2,1,0:T(8,128)(2,1)} %bitcast.128), calls=%async_computation.3 | async-start | bytes 9437184 | tf_op jit(solution)/shard_map/all_to_all | solution.py:330
  493.1 12.6 %copy-start = (bf16[32,128,256]{2,1,0:T(8,128)(2,1)}, bf16[32,128,256]{2,1,0:T(8,128)(2,1)S(1)}, u32[]{:S(2)}) copy-start(bf16[32,128,256]{2,1,0:T(8,128)(2,1)S(1)} %shard_map.291) | copy-start | bytes 6291460
  493.2 12.5 %copy-start.3 = (bf16[768,1024]{1,0:T(8,128)(2,1)S(1)}, bf16[768,1024]{1,0:T(8,128)(2,1)}, u32[]{:S(2)}) copy-start(bf16[768,1024]{1,0:T(8,128)(2,1)} %param.18) | copy-start | bytes 4718596
  493.2 29.4 %slice-start.2 = ((s8[8388608]{0:T(1024)(128)(4,1)}), s8[4194304]{0:T(1024)(128)(4,1)S(1)}, s32[]{:S(2)}) async-start(s8[8388608]{0:T(1024)(128)(4,1)} %bitcast.159), calls=%async_computation.12 | async-start | bytes 8388608
  505.7 16.9 %slice-start.3 = ((s8[8388608]{0:T(1024)(128)(4,1)}), s8[4194304]{0:T(1024)(128)(4,1)S(1)}, s32[]{:S(2)}) async-start(s8[8388608]{0:T(1024)(128)(4,1)} %bitcast.159), calls=%async_computation.13 | async-start | bytes 8388608
  505.7 16.8 %copy-start.9 = (f32[768,1024]{1,0:T(8,128)S(1)}, f32[768,1024]{1,0:T(8,128)}, u32[]{:S(2)}) copy-start(f32[768,1024]{1,0:T(8,128)} %copy-done.7) | copy-start | bytes 9437188
  532.2 16.4 %copy-start.11 = (bf16[768,1024]{1,0:T(8,128)(2,1)S(1)}, bf16[768,1024]{1,0:T(8,128)(2,1)}, u32[]{:S(2)}) copy-start(bf16[768,1024]{1,0:T(8,128)(2,1)} %param.17) | copy-start | bytes 4718596
  532.2 16.4 %copy-start.21 = (f32[768]{0:T(1024)S(1)}, f32[768]{0:T(1024)}, u32[]{:S(2)}) copy-start(f32[768]{0:T(1024)} %copy-done.20) | copy-start | bytes 9220
  532.2 16.4 %copy-start.23 = (f32[768]{0:T(1024)S(1)}, f32[768]{0:T(1024)}, u32[]{:S(2)}) copy-start(f32[768]{0:T(1024)} %copy-done.22) | copy-start | bytes 9220
  532.2 16.4 %copy-start.25 = (f32[1,1024]{1,0:T(1,128)S(1)}, f32[1,1024]{1,0:T(1,128)}, u32[]{:S(2)}) copy-start(f32[1,1024]{1,0:T(1,128)} %copy-done.24) | copy-start | bytes 12292
  698.6 30.3 %copy-start.28 = (f32[2,32]{1,0:T(2,128)S(1)}, f32[2,32]{1,0:T(2,128)}, u32[]{:S(2)}) copy-start(f32[2,32]{1,0:T(2,128)} %param.25) | copy-start | bytes 772
  698.6 30.3 %copy-start.29 = (f32[2,32]{1,0:T(2,128)S(1)}, f32[2,32]{1,0:T(2,128)}, u32[]{:S(2)}) copy-start(f32[2,32]{1,0:T(2,128)} %param.26) | copy-start | bytes 772
  698.6 30.3 %copy-start.30 = (f32[2,32]{1,0:T(2,128)S(1)}, f32[2,32]{1,0:T(2,128)}, u32[]{:S(2)}) copy-start(f32[2,32]{1,0:T(2,128)} %param.27) | copy-start | bytes 772
  701.3 33.1 %all-to-all-start.4 = ((bf16[6,32,8,256]{3,2,0,1:T(8,128)(2,1)}), bf16[6,32,8,256]{3,2,0,1:T(8,128)(2,1)}, u32[]{:S(2)}, u32[]{:S(2)}) async-start(bf16[6,32,8,256]{3,2,0,1:T(8,128)(2,1)} %copy.135), calls=%async_computation.4 | async-start | bytes 1572864 | tf_op jit(solution)/shard_map/all_to_all | solution.py:676
  760.3 59.8 %all-to-all-start.5 = ((bf16[6,32,8,256]{3,2,0,1:T(8,128)(2,1)}), bf16[6,32,8,256]{3,2,0,1:T(8,128)(2,1)S(1)}, u32[]{:S(2)}, u32[]{:S(2)}) async-start(bf16[6,32,8,256]{3,2,0,1:T(8,128)(2,1)} %copy.137), calls=%async_computation.5 | async-start | bytes 1572864 | tf_op jit(solution)/shard_map/all_to_all | solution.py:691
  (22 other events, 83.5 us)
Sparse Core Ops, SparseCore 0:
  11.5 72.3 all-gather.5
  87.5 90.7 all-gather.11
  181.7 54.8 all-gather.7
  240.0 78.2 all-gather.9

commit v3 on v2

--- a/solution.py
+++ b/solution.py
@@ -30,6 +30,7 @@
 MESH = pl.DeviceIdType.MESH
 VMEM_LIMIT = 48 * 2**20
 AHEAD = 4
+SKEW = 3
 
 
 def shortened(shard):
@@ -143,7 +144,7 @@
 
 
 def attend_backward_kernel(
-    safe, chunk, length_ref, q_ref, k_ref, v_ref, o_ref, do_ref, log_ref, dq_ref, dk_ref, dv_ref, kt_ref, dk_sum, dv_sum
+    safe, chunk, length_ref, q_ref, k_ref, v_ref, o_ref, do_ref, log_ref, out_ref, kt_ref, dk_sum, dv_sum
 ):
     seq_len = k_ref.shape[0]
     length = length_ref[0]
@@ -175,19 +176,20 @@
             dk_sum[part, :] += jnp.dot(d_scores, queries, preferred_element_type=float32)
             d_queries += jnp.dot(kt_ref[lanes, part], d_scores, preferred_element_type=float32)
         turned.append(d_queries * HEAD**-0.5)
-    dq_ref[...] = jnp.concatenate(turned, 0).T.astype(bfloat16)
+    rows = q_ref.shape[0]
+    here = pl.ds(pl.multiple_of(pl.program_id(1) * rows, rows), rows)
+    out_ref[here, :PAIR] = jnp.concatenate(turned, 0).T.astype(bfloat16)
 
     @pl.when(pl.program_id(1) == pl.num_programs(1) - 1)
     def _():
-        dk_ref[...] = dk_sum[...].astype(bfloat16)
-        dv_ref[...] = dv_sum[...].astype(bfloat16)
+        out_ref[:, PAIR : 2 * PAIR] = dk_sum[...].astype(bfloat16)
+        out_ref[:, 2 * PAIR :] = dv_sum[...].astype(bfloat16)
 
 
 def attend_backward(lengths, scene, mixed, d_mixed, log_totals, safe, rows=512, chunk=1024):
     seq_len, width = mixed.shape
     pairs = width // PAIR
     tile = pl.BlockSpec((rows, PAIR), lambda p, i: (i, p))
-    full = pl.BlockSpec((seq_len, PAIR), lambda p, i: (0, p))
     return pl.pallas_call(
         partial(attend_backward_kernel, safe, chunk),
         grid=(pairs, seq_len // rows),
@@ -200,8 +202,8 @@
             tile,
             pl.BlockSpec((1, 2, rows), lambda p, i: (p, 0, i)),
         ],
-        out_specs=[tile, full, full],
-        out_shape=[jax.ShapeDtypeStruct((seq_len, width), bfloat16)] * 3,
+        out_specs=pl.BlockSpec((seq_len, 3 * PAIR), lambda p, i: (0, p)),
+        out_shape=jax.ShapeDtypeStruct((seq_len, 3 * width), bfloat16),
         scratch_shapes=[
             pltpu.VMEM((PAIR, seq_len), bfloat16),
             pltpu.VMEM((seq_len, PAIR), float32),
@@ -214,6 +216,80 @@
             transcendentals=0,
         ),
     )(lengths, scene, scene, scene, mixed, d_mixed, log_totals)
+
+
+def project_kernel(acts_ref, wq_ref, wk_ref, wv_ref, *out_refs):
+    thirds = (wq_ref, wk_ref, wv_ref)
+    halves = len(out_refs)
+    weights = jnp.concatenate(
+        [third[:, h * PAIR : (h + 1) * PAIR] for h in range(halves) for third in thirds], 1
+    )
+    result = jnp.dot(acts_ref[...], weights, preferred_element_type=float32).astype(bfloat16)
+    for h, out_ref in enumerate(out_refs):
+        out_ref[0] = result[:, h * 3 * PAIR : (h + 1) * 3 * PAIR]
+
+
+def project(acts, weights, groups):
+    tok_rows, width = acts.shape
+    head_width = width // groups
+    halves = head_width // PAIR
+
+    def third(k):
+        return pl.BlockSpec((width, head_width), lambda g: (0, k * groups + g))
+
+    return pl.pallas_call(
+        project_kernel,
+        grid=(groups,),
+        in_specs=[pl.BlockSpec((tok_rows, width), lambda g: (0, 0)), third(0), third(1), third(2)],
+        out_specs=[pl.BlockSpec((1, tok_rows, 3 * PAIR), lambda g: (g, 0, 0))] * halves,
+        out_shape=[jax.ShapeDtypeStruct((groups, tok_rows, 3 * PAIR), bfloat16)] * halves,
+        compiler_params=pltpu.CompilerParams(vmem_limit_bytes=VMEM_LIMIT),
+        cost_estimate=pl.CostEstimate(
+            flops=6 * tok_rows * width**2, bytes_accessed=6 * width**2 + 8 * tok_rows * width,
+            transcendentals=0,
+        ),
+    )(acts, weights, weights, weights)
+
+
+def project_back_kernel(halves, *refs):
+    grads, (wq_ref, wk_ref, wv_ref, out_ref) = refs[:halves], refs[halves:]
+    thirds = (wq_ref, wk_ref, wv_ref)
+    weights = jnp.concatenate(
+        [third[:, h * PAIR : (h + 1) * PAIR] for h in range(halves) for third in thirds], 1
+    )
+    rows = jnp.concatenate([grad[0] for grad in grads], 1)
+    result = lax.dot_general(rows, weights, NT, preferred_element_type=float32)
+
+    @pl.when(pl.program_id(0) == 0)
+    def _():
+        out_ref[...] = result
+
+    @pl.when(pl.program_id(0) > 0)
+    def _():
+        out_ref[...] += result
+
+
+def project_back(grads, weights):
+    groups, tok_rows, _ = grads[0].shape
+    width = weights.shape[0]
+    head_width = width // groups
+
+    def third(k):
+        return pl.BlockSpec((width, head_width), lambda g: (0, k * groups + g))
+
+    return pl.pallas_call(
+        partial(project_back_kernel, len(grads)),
+        grid=(groups,),
+        in_specs=[pl.BlockSpec((1, tok_rows, 3 * PAIR), lambda g: (g, 0, 0))] * len(grads)
+        + [third(0), third(1), third(2)],
+        out_specs=pl.BlockSpec((tok_rows, width), lambda g: (0, 0)),
+        out_shape=jax.ShapeDtypeStruct((tok_rows, width), float32),
+        compiler_params=pltpu.CompilerParams(vmem_limit_bytes=VMEM_LIMIT),
+        cost_estimate=pl.CostEstimate(
+            flops=6 * tok_rows * width**2, bytes_accessed=6 * width**2 + 10 * tok_rows * width,
+            transcendentals=0,
+        ),
+    )(*grads, weights, weights, weights)
 
 
 def exact(left, right, dims=(((1,), (0,)), ((), ()))):
@@ -478,6 +554,89 @@
     )(*(part.reshape((2,) * bits + shape) for part, shape in zip(parts, shapes)))
 
 
+def gather_kernel(bits, narrow_bits, plans, chunks, count, *refs):
+    sources, outs = refs[:count], refs[count : 2 * count]
+    own_sem, send_sem, recv_sem = refs[2 * count :]
+    peers = [partner(b, narrow_bits) for b in range(bits)]
+    greet(peers)
+    dims = list(reversed(range(bits)))
+
+    def place(chunk, stage):
+        at, band, bands, col, cols, colour = chunks[chunk]
+        done = plans[colour][:stage]
+        index = tuple(slice(None) if b in done else peers[b][1] for b in dims)
+        return outs[at].at[(pl.ds(band, bands),) + index + (slice(None), pl.ds(col, cols))]
+
+    def own(chunk):
+        at, band, bands, col, cols, colour = chunks[chunk]
+        return sources[at].at[pl.ds(band, bands), :, pl.ds(col, cols)]
+
+    def send(chunk, stage):
+        colour = chunks[chunk][-1]
+        target = place(chunk, stage)
+        return pltpu.make_async_remote_copy(
+            src_ref=target if stage else own(chunk),
+            dst_ref=target,
+            send_sem=send_sem.at[chunk, stage],
+            recv_sem=recv_sem.at[chunk, stage],
+            device_id=peers[plans[colour][stage]][0],
+            device_id_type=MESH,
+        )
+
+    def keep(chunk):
+        return pltpu.make_async_copy(own(chunk), place(chunk, 0), own_sem.at[chunk])
+
+    total = len(chunks)
+    for chunk in range(total):
+        send(chunk, 0).start()
+        keep(chunk).start()
+    for step in range(total + SKEW * bits):
+        for stage in reversed(range(bits)):
+            chunk = step - SKEW * stage
+            if 0 <= chunk < total:
+                if stage == 0:
+                    keep(chunk).wait()
+                send(chunk, stage).wait_recv()
+                if stage + 1 < bits:
+                    send(chunk, stage + 1).start()
+    for chunk in range(total):
+        for stage in range(bits):
+            send(chunk, stage).wait_send()
+
+
+def gather_bands(parts, pieces, collective_id):
+    bits, narrow_bits = mesh_bits()
+    chunks = []
+    for at, (part, (cut, cut_cols)) in enumerate(zip(parts, pieces)):
+        bands, cols = part.shape[0] // cut, part.shape[2] // cut_cols
+        for band in range(0, part.shape[0], bands):
+            for col in range(0, part.shape[2], cols):
+                chunks.append((at, band, bands, col, cols, len(chunks) % 2))
+    later = tuple(reversed(range(3, bits)))
+    plans = (later + (1, 2, 0), later + (2, 1, 0))
+    total = len(chunks)
+    results = pl.pallas_call(
+        partial(gather_kernel, bits, narrow_bits, plans, tuple(chunks), len(parts)),
+        out_shape=[
+            jax.ShapeDtypeStruct(part.shape[:1] + (2,) * bits + part.shape[1:], part.dtype)
+            for part in parts
+        ],
+        in_specs=[pl.BlockSpec(memory_space=pl.ANY)] * len(parts),
+        out_specs=[pl.BlockSpec(memory_space=pl.ANY)] * len(parts),
+        scratch_shapes=[
+            pltpu.SemaphoreType.DMA((total,)),
+            pltpu.SemaphoreType.DMA((total, bits)),
+            pltpu.SemaphoreType.DMA((total, bits)),
+        ],
+        compiler_params=pltpu.CompilerParams(collective_id=collective_id, has_side_effects=True),
+        cost_estimate=pl.CostEstimate(flops=0, bytes_accessed=10**8, transcendentals=0),
+    )(*parts)
+    return [
+        result.reshape(part.shape[:1] + (1 << bits,) + part.shape[1:])
+        for result, part in zip(results, parts)
+    ]
+
+
 def total_kernel(bits, narrow_bits, own_ref, sum_ref, arrived, send_sem, recv_sem):
     peers = [partner(b, narrow_bits) for b in range(bits)]
     greet(peers)
@@ -513,27 +672,27 @@
     )(jnp.broadcast_to(value, tile))[0, 0]
 
 
-def weight_grad_kernel(columns, band_rows, left_ref, right_ref, out_ref):
+def weight_grad_kernel(columns, band_rows, left_ref, *refs):
+    right_refs, out_ref = refs[:-1], refs[-1]
     left = left_ref[...].T
     for at in range(0, len(columns), 2):
         blocks = []
-        for group, start in columns[at : at + 2]:
-            block = jnp.dot(
-                left, right_ref[group, :, start : start + BLOCK], preferred_element_type=float32
-            )
+        for spots in columns[at : at + 2]:
+            right = [right_refs[i][g, :, start : start + size] for i, g, start, size in spots]
+            right = right[0] if len(right) == 1 else jnp.concatenate(right, 1)
+            block = jnp.dot(left, right, preferred_element_type=float32)
             blocks.append(block.astype(bfloat16).reshape(-1, band_rows, BLOCK))
         out_ref[:, at * band_rows : (at + 2) * band_rows, :] = jnp.concatenate(blocks, 1)
 
 
-def weight_grad(left, right, columns, device_count):
+def weight_grad(left, rights, columns, device_count):
     tok_rows, height = left.shape
     band_rows = BLOCK // device_count
     bands, wide = height // BLOCK, len(columns)
     if band_rows % 8:
-        product = jnp.einsum("td,gte->dge", left, right, preferred_element_type=float32)
-        product = jnp.concatenate(
-            [product[:, group, start : start + BLOCK] for group, start in columns], 1
-        )
+        right = [rights[i][g, :, start : start + n] for spots in columns for i, g, start, n in spots]
+        right = jnp.concatenate(right, 1)
+        product = jnp.einsum("td,te->de", left, right, preferred_element_type=float32)
         product = product.astype(bfloat16).reshape(bands, device_count, band_rows, wide, BLOCK)
         return product.transpose(1, 0, 3, 2, 4).reshape(device_count, -1, BLOCK)
     return pl.pallas_call(
@@ -541,8 +700,8 @@
         grid=(bands,),
         in_specs=[
             pl.BlockSpec((tok_rows, BLOCK), lambda i: (0, i)),
-            pl.BlockSpec(right.shape, lambda i: (0, 0, 0)),
-        ],
+        ]
+        + [pl.BlockSpec(right.shape, lambda i: (0, 0, 0)) for right in rights],
         out_specs=pl.BlockSpec((device_count, wide * band_rows, BLOCK), lambda i: (0, i, 0)),
         out_shape=jax.ShapeDtypeStruct((device_count, bands * wide * band_rows, BLOCK), bfloat16),
         compiler_params=pltpu.CompilerParams(vmem_limit_bytes=VMEM_LIMIT),
@@ -551,15 +710,7 @@
             bytes_accessed=2 * (tok_rows * (height + wide * BLOCK) + bands * wide * BLOCK**2),
             transcendentals=0,
         ),
-    )(left, right)
-
-
-def unpack(gathered):
-    matrices = [
-        layout.reshape(layout.shape[0] * layout.shape[1], layout.shape[2])
-        for layout in gathered[:4]
-    ]
-    return (matrices, gathered[4].astype(jnp.float32))
+    )(left, *rights)
 
 
 def body(
@@ -590,26 +741,31 @@
     lowered = tuple((layout.astype(jnp.bfloat16) for layout in masters)) + (
         norm_gains.astype(jnp.bfloat16),
     )
-    weight_list, gain_pair = unpack(
-        jax.tree.map(
-            lambda part, own: part.astype(own.dtype),
-            lax.all_gather(shortened(lowered), ("wide", "narrow"), axis=1, tiled=True),
-            lowered,
-        )
-    )
-    w_attn, w_proj, w_hidden, w_back = weight_list
+    share = norm_gains.shape[1]
+    gains_low = jnp.pad(lowered[4], ((0, 6), (0, 128 - share)))[None]
+    w_attn, gain_pair = gather_bands((lowered[0], gains_low), ((4, 2), (1, 1)), 3)
+    w_attn = w_attn.reshape(width, 3 * width)
+    gain_pair = gain_pair[0, :, :2, :share].transpose(1, 0, 2).reshape(2, width)
+    gain_pair = gain_pair.astype(jnp.float32)
+    w_proj, w_hidden, w_back = (
+        gathered.reshape(-1, gathered.shape[2])
+        for gathered in lax.all_gather(lowered[1:4], ("wide", "narrow"), axis=1, tiled=True)
+    )
     inputs = tokens.astype(jnp.float32)
     normed_one, inverse_one = normalize(inputs)
     act_one = (normed_one * gain_pair[0]).astype(jnp.bfloat16)
     head_width = width // narrow_count
     safe = seq_len - tok_rows
-    w_groups = w_attn.reshape(width, 3, narrow_count, head_width)
-    packed = jnp.einsum("td,dkge->gtke", act_one, w_groups, preferred_element_type=jnp.float32)
-    packed = packed.astype(jnp.bfloat16).reshape(narrow_count, tok_rows, 3 * head_width)
-    scene = exchange(packed).reshape(seq_len, 3 * head_width)
-    mixed, log_totals = attend(lengths, scene, safe)
-    merged = exchange(mixed.reshape(narrow_count, tok_rows, head_width))
-    merged = merged.transpose(1, 0, 2).reshape(tok_rows, width)
+    halves = head_width // PAIR
+    scenes = [
+        exchange(part).reshape(seq_len, 3 * PAIR)
+        for part in project(act_one, w_attn, narrow_count)
+    ]
+    attended = [attend(lengths, scene, safe) for scene in scenes]
+    merged = [exchange(o.reshape(narrow_count, tok_rows, PAIR)) for o, _ in attended]
+    merged = jnp.concatenate(
+        [merged[half][group] for group in range(narrow_count) for half in range(halves)], 1
+    )
     middle = inputs + jnp.dot(merged, w_proj, preferred_element_type=jnp.float32)
     normed_two, inverse_two = normalize(middle)
     act_two = (normed_two * gain_pair[1]).astype(jnp.bfloat16)
@@ -618,40 +774,36 @@
     block_out = (middle + jnp.dot(active, w_back, preferred_element_type=jnp.float32)).astype(
         jnp.bfloat16
     )
-    plain = lambda size: tuple((0, start) for start in range(0, size, BLOCK))
-    d_back = weight_grad(active, cotangent[None], plain(width), device_count)
+    plain = lambda size: tuple(((0, 0, start, BLOCK),) for start in range(0, size, BLOCK))
+    d_back = weight_grad(active, [cotangent[None]], plain(width), device_count)
     d_active = jnp.einsum("td,fd->tf", cotangent, w_back, preferred_element_type=jnp.float32)
     _, gelu_pull = jax.vjp(partial(jax.nn.gelu, approximate=True), hidden)
     d_hidden = gelu_pull(d_active)[0].astype(jnp.bfloat16)
-    d_w_hidden = weight_grad(act_two, d_hidden[None], plain(FF), device_count)
+    d_w_hidden = weight_grad(act_two, [d_hidden[None]], plain(FF), device_count)
     d_act_two = jnp.einsum("tf,df->td", d_hidden, w_hidden, preferred_element_type=jnp.float32)
     d_norm_two, d_gain_two = norm_backward(d_act_two, normed_two, inverse_two, gain_pair[1])
     d_middle = cotangent.astype(jnp.float32) + d_norm_two
     d_branch = d_middle.astype(jnp.bfloat16)
-    d_proj = weight_grad(merged, d_branch[None], plain(width), device_count)
+    d_proj = weight_grad(merged, [d_branch[None]], plain(width), device_count)
     d_merged = jnp.einsum("te,de->td", d_branch, w_proj, preferred_element_type=jnp.float32).astype(
         jnp.bfloat16
     )
-    d_mixed = d_merged.reshape(tok_rows, narrow_count, head_width).transpose(1, 0, 2)
-    d_mixed = exchange(d_mixed).reshape(seq_len, head_width)
-    d_scene = jnp.concatenate(attend_backward(lengths, scene, mixed, d_mixed, log_totals, safe), 1)
-    d_packed = exchange(d_scene.reshape(narrow_count, tok_rows, 3 * head_width))
+    d_mixed = d_merged.reshape(tok_rows, narrow_count, halves, PAIR).transpose(2, 1, 0, 3)
+    d_mixed = [exchange(d_mixed[half]).reshape(seq_len, PAIR) for half in range(halves)]
+    d_scenes = [
+        attend_backward(lengths, scene, mixed, d_mixed_one, log_total, safe)
+        for scene, (mixed, log_total), d_mixed_one in zip(scenes, attended, d_mixed)
+    ]
+    d_packed = [exchange(d.reshape(narrow_count, tok_rows, 3 * PAIR)) for d in d_scenes]
     grouped = tuple(
-        (group, third * head_width + start)
+        tuple((half, group, third * PAIR, PAIR) for half in range(halves))
         for third in range(3)
         for group in range(narrow_count)
-        for start in range(0, head_width, BLOCK)
     )
     d_attn = weight_grad(act_one, d_packed, grouped, device_count)
-    d_act_one = jnp.einsum(
-        "gtke,dkge->td",
-        d_packed.reshape(narrow_count, tok_rows, 3, head_width),
-        w_groups,
-        preferred_element_type=jnp.float32,
-    )
+    d_act_one = project_back(d_packed, w_attn)
     d_norm_one, d_gain_one = norm_backward(d_act_one, normed_one, inverse_one, gain_pair[0])
     grad_tokens = (d_middle + d_norm_one).astype(jnp.bfloat16)
-    share = width // device_count
     gain_parts = jnp.stack([d_gain_one, d_gain_two]).reshape(2, device_count, share)
     gain_parts = jnp.pad(gain_parts.transpose(1, 0, 2), ((0, 0), (0, 6), (0, 128 - share)))
     *grad_shards, gain_grad = reduce_to_shards(

time: 841 us -> 769 us (0.914)
  waiting for transfers between devices: 144 us -> 71 us
  Pallas kernels: 422 us -> 493 us
  blocking collectives: 66.6 us -> 0 us
  matrix products: 86.5 us -> 67.7 us
  starting transfers between devices: 22.5 us -> 40.2 us
    pallas_call x0 -> x3, Pallas kernels: none -> 71.5 us  [the longest x1 52.8 us: gather_bands(): pl.pallas_call(partial(gather_kernel, bits, narrow_bits, plans, tuple(chu...]
    all_gather x4 -> x3, waiting for transfers between devices: 55.4 us -> 6.68 us  [body(): lax.all_gather(lowered[1:4], ('wide', 'narrow'), axis=1, tiled=True)]
    all_gather x1 -> x0, blocking collectives: 43.1 us -> none  [body(): lax.all_gather(shortened(lowered), ('wide', 'narrow'), axis=1, tiled=True)]
    all_to_all x3 -> x8, waiting for transfers between devices: 88.8 us -> 64.2 us  [exchange(): lax.all_to_all(groups, 'narrow', split_axis=0, concat_axis=0, tiled=True)]
    all_to_all x1 -> x0, blocking collectives: 23.5 us -> none  [exchange(): lax.all_to_all(groups, 'narrow', split_axis=0, concat_axis=0, tiled=True)]
    dot_general x2 -> x0, matrix products: 21.8 us -> none  [the longest x1 11 us: body(): jnp.einsum('gtke,dkge->td', d_packed.reshape(narrow_count, tok_rows, 3, h...]
    all_to_all x3 -> x8, starting transfers between devices: 15.8 us -> 33.6 us  [exchange(): lax.all_to_all(groups, 'narrow', split_axis=0, concat_axis=0, tiled=True)]
    unnamed x70 -> x93, local copies, waits for them, and re-layouts: 3.1 us -> 19.8 us
  transfers between devices with their start and end apart: 9 -> 13, of which waited for: 5 -> 5; matrix products, arithmetic and copies ran while one was open for 10% -> 8% of each run, Pallas kernels for 20% -> 43%
where the time goes in v3:
time: 769 us; the launch traced here: 763 us
  Pallas kernels  493 us (64%)
  waiting for transfers between devices  71 us (9%)
  matrix products  67.7 us (9%)
  starting transfers between devices  40.2 us (5%)
  local copies, waits for them, and re-layouts  37.4 us (5%)
  other arithmetic  33.1 us (4%)
  between operations  20.8 us (3%)
    pallas_call x1, Pallas kernels, reduce_to_shards(): pl.pallas_call(partial(reduce_kernel, bits, narrow_bits, plans, tuple(chu...  124 us
    pallas_call x2, Pallas kernels, attend_backward(): pl.pallas_call(partial(attend_backward_kernel, safe, chunk), grid=(pairs,...  100 us
    all_to_all x8, waiting for transfers between devices, exchange(): lax.all_to_all(groups, 'narrow', split_axis=0, concat_axis=0, tiled=True)  64.2 us
    pallas_call x2, Pallas kernels, attend(): pl.pallas_call(partial(attend_kernel, safe, chunk), grid=(pairs, seq_len...  63.1 us
    pallas_call x1, Pallas kernels, renew_bases(): pl.pallas_call(partial(renew_kernel, rows), out_shape=jax.ShapeDtypeStruc...  54.8 us
    pallas_call x1, Pallas kernels, gather_bands(): pl.pallas_call(partial(gather_kernel, bits, narrow_bits, plans, tuple(chu...  52.8 us
    pallas_call x4, Pallas kernels, weight_grad(): pl.pallas_call(partial(weight_grad_kernel, columns, band_rows), grid=(ban...  39.7 us
    all_to_all x8, starting transfers between devices, exchange(): lax.all_to_all(groups, 'narrow', split_axis=0, concat_axis=0, tiled=True)  33.6 us
  transfers between devices with their start and end apart: 13, of which 5 were waited for; matrix products, arithmetic and copies ran while one was open for 8% of the time, Pallas kernels for 43%

profile of v3, /device:TPU:0, one launch (start us, length us, event | category | flops | bytes accessed | tf_op | source)
XLA Modules:
  0.0 763.4 jit_solution(7210911257141545305)
XLA Ops:
  15.6 52.8 %shard_map.288 = (bf16[4,2,2,2,2,2,8,3072]{7,6,5,4,3,2,1,0:T(8,128)(2,1)}, bf16[1,2,2,2,2,2,8,128]{7,6,5,4,3,2,1,0:T(8,128)(2,1)}) custom-call(bf16[4,8,3072]{2,1,0:T(8,128)(2,1)} %convert_element_type.70.refs_0_, bf16[1,8,128]{2,1,0:T(8,128)(2,1)} %pad_bitcast_fusion.refs_1_), custom_call_target="tpu_custom_call" | custom-call | bytes 100000000 | tf_op jit(solution)/shard_map/pallas_call | solution.py:618
  70.9 8.6 %shard_map.289 = (bf16[4,768,384]{2,1,0:T(8,128)(2,1)S(1)}, bf16[4,768,384]{2,1,0:T(8,128)(2,1)}) custom-call(bf16[768,1024]{1,0:T(8,128)(2,1)S(1)} %fusion.13.acts_ref.left_ref, bf16[1024,3072]{1,0:T(8,128)(2,1)} %bitcast.145, bf16[1024,3072]{1,0:T(8,128)(2,1)} %bitcast.146, bf16[1024,3072]{1,0:T(8,128)(2,1)} %bitcast.147), custom_call_target="tpu_custom_call" | custom-call | flops 4831838208 | bytes 12582912 | tf_op jit(solution)/shard_map/pallas_call | solution.py:240
  85.2 33.8 %all-to-all-done = bf16[4,768,384]{2,1,0:T(8,128)(2,1)S(1)} async-done(((bf16[4,768,384]{2,1,0:T(8,128)(2,1)}), bf16[4,768,384]{2,1,0:T(8,128)(2,1)S(1)}, u32[]{:S(2)}, u32[]{:S(2)}) %all-to-all-start) | async-done | bytes 2359328 | tf_op jit(solution)/shard_map/all_to_all | solution.py:406
  123.7 31.0 %shard_map.290 = (bf16[3072,128]{1,0:T(8,128)(2,1)}, f32[1,2,3072]{2,1,0:T(2,128)S(1)}) custom-call(s32[1]{0:T(128)S(6)} %copy.114.length_ref, bf16[3072,384]{1,0:T(8,128)(2,1)S(1)} %bitcast.132, bf16[3072,384]{1,0:T(8,128)(2,1)S(1)} %bitcast.133, bf16[3072,384]{1,0:T(8,128)(2,1)S(1)} %bitcast.134), custom_call_target="tpu_custom_call" | custom-call | flops 19327352832 | bytes 3145728 | tf_op jit(solution)/shard_map/pallas_call | solution.py:116
  154.7 11.6 %all-to-all-done.2 = bf16[4,768,384]{2,1,0:T(8,128)(2,1)} async-done(((bf16[4,768,384]{2,1,0:T(8,128)(2,1)}), bf16[4,768,384]{2,1,0:T(8,128)(2,1)}, u32[]{:S(2)}, u32[]{:S(2)}) %all-to-all-start.2) | async-done | bytes 2359328 | tf_op jit(solution)/shard_map/all_to_all | solution.py:406
  170.0 32.1 %shard_map.291 = (bf16[3072,128]{1,0:T(8,128)(2,1)}, f32[1,2,3072]{2,1,0:T(2,128)S(1)}) custom-call(s32[1]{0:T(128)S(6)} %copy.114.length_ref, bf16[3072,384]{1,0:T(8,128)(2,1)} %bitcast.8.q_ref.k_ref.v_ref, bf16[3072,384]{1,0:T(8,128)(2,1)} %bitcast.8.q_ref.k_ref.v_ref, bf16[3072,384]{1,0:T(8,128)(2,1)} %bitcast.8.q_ref.k_ref.v_ref), custom_call_target="tpu_custom_call" | custom-call | flops 19327352832 | bytes 3145728 | tf_op jit(solution)/shard_map/pallas_call | solution.py:116
  209.4 9.3 %all-to-all-done.3 = bf16[4,768,128]{2,1,0:T(8,128)(2,1)} async-done(((bf16[4,768,128]{2,1,0:T(8,128)(2,1)}), bf16[4,768,128]{2,1,0:T(8,128)(2,1)}, u32[]{:S(2)}, u32[]{:S(2)}) %all-to-all-start.3) | async-done | bytes 786464 | tf_op jit(solution)/shard_map/all_to_all | solution.py:406
  232.3 12.5 %fusion.52 = f32[768,4096]{1,0:T(8,128)} fusion(bf16[768,1024]{1,0:T(8,128)(2,1)S(1)} %copy-done.8, bf16[4096,1024]{1,0:T(8,128)(2,1)} %bitcast.164), kind=kOutput, calls=%fused_computation.110 | convolution fusion | flops 6442450944 | bytes 22544384 | tf_op jit(solution)/shard_map/td,fd->tf/dot_general | solution.py:779
  244.9 6.6 all-gather.6.cloned.1.call-done
  251.5 22.4 %fusion.6 = (bf16[768,4096]{1,0:T(8,128)(2,1)}, bf16[768,4096]{1,0:T(8,128)(2,1)}) fusion(f32[768,4096]{1,0:T(8,128)} %fusion.52, bf16[768,1024]{1,0:T(8,128)(2,1)S(1)} %multiply_convert_fusion.1.left_ref, bf16[1024,4096]{1,0:T(8,128)(2,1)} %bitcast.166), kind=kOutput, calls=%fused_computation.8 | convolution fusion | flops 6511656960 | bytes 35127296 | tf_op jit(solution)/shard_map/dot_general | solution.py:772
  273.9 11.9 %multiply_reduce_fusion = (f32[1024]{0:T(1024)S(1)}, f32[768]{0:T(1024)S(1)}, f32[768]{0:T(1024)S(1)}, f32[768,1024]{1,0:T(8,128)S(1)}) fusion(f32[768,1024]{1,0:T(8,128)S(1)} %copy-done.18, f32[768]{0:T(1024)S(1)} %add_rsqrt_fusion, f32[768]{0:T(1024)S(1)} %broadcast_multiply_fusion.4, f32[1024]{0:T(1024)S(1)} %mul.238, ...), kind=kOutput, calls=%fused_computation.27 | convolution fusion | flops 6448739328 | bytes 20992000 | tf_op jit(solution)/shard_map/tf,df->td/dot_general | solution.py:783
  303.5 11.6 %shard_map.297 = bf16[32,512,256]{2,1,0:T(8,128)(2,1)} custom-call(bf16[768,1024]{1,0:T(8,128)(2,1)S(1)} %multiply_convert_fusion.1.left_ref, bf16[1,768,4096]{2,1,0:T(8,128)(2,1)} %bitcast.170), custom_call_target="tpu_custom_call" | custom-call | flops 6442450944 | bytes 16252928 | tf_op jit(solution)/shard_map/pallas_call | solution.py:698
  315.2 15.8 %shard_map.298 = bf16[32,512,256]{2,1,0:T(8,128)(2,1)} custom-call(bf16[768,4096]{1,0:T(8,128)(2,1)} %get-tuple-element.70.left_ref, bf16[1,768,1024]{2,1,0:T(8,128)(2,1)S(1)} %bitcast.141), custom_call_target="tpu_custom_call" | custom-call | flops 6442450944 | bytes 16252928 | tf_op jit(solution)/shard_map/pallas_call | solution.py:698
  334.7 50.2 %shard_map.293 = bf16[3072,384]{1,0:T(8,128)(2,1)S(1)} custom-call(s32[1]{0:T(128)S(6)} %copy.114.length_ref, bf16[3072,384]{1,0:T(8,128)(2,1)} %bitcast.8.q_ref.k_ref.v_ref, bf16[3072,384]{1,0:T(8,128)(2,1)} %bitcast.8.q_ref.k_ref.v_ref, bf16[3072,384]{1,0:T(8,128)(2,1)} %bitcast.8.q_ref.k_ref.v_ref, bf16[3072,128]{1,0:T(8,128)(2,1)} %get-tuple-element.41.o_ref, ...), custom_call_target="tpu_custom_call" | custom-call | flops 48318382080 | bytes 6291456 | tf_op jit(solution)/shard_map/pallas_call | solution.py:193
  390.2 50.0 %shard_map.292 = bf16[3072,384]{1,0:T(8,128)(2,1)S(1)} custom-call(s32[1]{0:T(128)S(6)} %copy.114.length_ref, bf16[3072,384]{1,0:T(8,128)(2,1)} %bitcast.135, bf16[3072,384]{1,0:T(8,128)(2,1)} %bitcast.136, bf16[3072,384]{1,0:T(8,128)(2,1)} %bitcast.137, bf16[3072,128]{1,0:T(8,128)(2,1)} %get-tuple-element.39.o_ref, bf16[3072,128]{1,0:T(8,128)(2,1)S(1)} %bitcast.142, ...), custom_call_target="tpu_custom_call" | custom-call | flops 48318382080 | bytes 6291456 | tf_op jit(solution)/shard_map/pallas_call | solution.py:193
  441.7 5.0 all-to-all-start.5
  453.6 12.1 %add_convert_fusion = bf16[768,1024]{1,0:T(8,128)(2,1)} fusion(f32[768,1024]{1,0:T(8,128)S(1)} %copy-done.19, bf16[768,4096]{1,0:T(8,128)(2,1)} %get-tuple-element.70.left_ref, bf16[4096,1024]{1,0:T(8,128)(2,1)} %bitcast.165), kind=kOutput, calls=%fused_computation.30 | convolution fusion | flops 6444023808 | bytes 19398656 | tf_op jit(solution)/shard_map/dot_general | solution.py:774
  465.7 9.6 %all-to-all-done.5.refs_0_ = bf16[4,768,384]{2,1,0:T(8,128)(2,1)} async-done(((bf16[4,768,384]{2,1,0:T(8,128)(2,1)}), bf16[4,768,384]{2,1,0:T(8,128)(2,1)}, u32[]{:S(2)}, u32[]{:S(2)}) %all-to-all-start.5) | async-done | bytes 2359328 | tf_op jit(solution)/shard_map/all_to_all | solution.py:406
  475.3 10.1 %shard_map.294 = f32[768,1024]{1,0:T(8,128)} custom-call(bf16[4,768,384]{2,1,0:T(8,128)(2,1)} %all-to-all-done.5.refs_0_, bf16[4,768,384]{2,1,0:T(8,128)(2,1)S(1)} %all-to-all-done.7.refs_1_, bf16[1024,3072]{1,0:T(8,128)(2,1)} %bitcast.148, bf16[1024,3072]{1,0:T(8,128)(2,1)} %bitcast.149, bf16[1024,3072]{1,0:T(8,128)(2,1)} %bitcast.150), custom_call_target="tpu_custom_call" | custom-call | flops 4831838208 | bytes 14155776 | tf_op jit(solution)/shard_map/pallas_call | solution.py:280
  489.5 9.4 %shard_map.295 = bf16[32,384,256]{2,1,0:T(8,128)(2,1)} custom-call(bf16[768,1024]{1,0:T(8,128)(2,1)S(1)} %copy-done.2, bf16[4,768,384]{2,1,0:T(8,128)(2,1)} %all-to-all-done.5.refs_0_, bf16[4,768,384]{2,1,0:T(8,128)(2,1)} %copy-done), custom_call_target="tpu_custom_call" | custom-call | flops 4831838208 | bytes 12582912 | tf_op jit(solution)/shard_map/pallas_call | solution.py:698
  499.0 124.0 %shard_map.299 = (f32[384,256]{1,0:T(8,128)}, f32[128,256]{1,0:T(8,128)}, f32[512,256]{1,0:T(8,128)}, f32[512,256]{1,0:T(8,128)}, f32[8,128]{1,0:T(8,128)}) custom-call(bf16[2,2,2,2,2,384,256]{6,5,4,3,2,1,0:T(8,128)(2,1)} %bitcast.154, bf16[2,2,2,2,2,128,256]{6,5,4,3,2,1,0:T(8,128)(2,1)} %bitcast.140, bf16[2,2,2,2,2,512,256]{6,5,4,3,2,1,0:T(8,128)(2,1)} %bitcast.151, ...), custom_call_target="tpu_custom_call" | custom-call | flops 100000000 | bytes 400000000 | tf_op jit(solution)/shard_map/pallas_call | solution.py:544
  639.8 16.2 %shard_map.300 = f32[8,128]{1,0:T(8,128)} custom-call(f32[8,128]{1,0:T(8,128)} %broadcast_in_dim.14.own_ref), custom_call_target="tpu_custom_call" | custom-call | tf_op jit(solution)/shard_map/pallas_call | solution.py:661
  664.7 23.8 %shard_map.301 = (bf16[6,256,256]{2,1,0:T(8,128)(2,1)S(1)}, f32[6,256,256]{2,1,0:T(8,128)}, f32[6,256,256]{2,1,0:T(8,128)}, f32[6,256,256]{2,1,0:T(8,128)}, f32[...) custom-call(f32[1,1]{1,0:T(1,128)} %bitcast.39.factor_ref, ...), custom_call_target="tpu_custom_call" | custom-call | flops 12079595520 | bytes 23592960 | tf_op jit(solution)/shard_map/pallas_call | solution.py:329
  692.5 54.8 %shard_map.302 = f32[12,256,256]{2,1,0:T(8,128)S(1)} custom-call(f32[12,256,256]{2,1,0:T(8,128)} %bitcast.171, f32[12,256,256]{2,1,0:T(8,128)} %bitcast.172), custom_call_target="tpu_custom_call" | custom-call | flops 40265318400 | bytes 9437184 | tf_op jit(solution)/shard_map/pallas_call | solution.py:389
  (185 shorter events, 117.5 us)
Async XLA Ops:
  7.2 62.2 %copy-start.14 = (bf16[768,1024]{1,0:T(8,128)(2,1)S(1)}, bf16[768,1024]{1,0:T(8,128)(2,1)}, u32[]{:S(2)}) copy-start(bf16[768,1024]{1,0:T(8,128)(2,1)} %param.17) | copy-start | bytes 4718596
  7.2 218.6 %all-gather.4.cloned.1.call-start = ((), (), s32[]{:S(2)}) async-start(), calls=%async_computation.10 | async-start | bytes 2162688 | tf_op jit(solution)/shard_map/all_gather | solution.py:752
  8.9 223.0 %all-gather.8.cloned.1.call-start = ((), (), s32[]{:S(2)}) async-start(), calls=%async_computation.12 | async-start | bytes 8650752 | tf_op jit(solution)/shard_map/all_gather | solution.py:752
  10.8 240.7 %all-gather.6.cloned.1.call-start = ((), (), s32[]{:S(2)}) async-start(), calls=%async_computation.11 | async-start | bytes 8650752 | tf_op jit(solution)/shard_map/all_gather | solution.py:752
  80.9 38.1 %all-to-all-start = ((bf16[4,768,384]{2,1,0:T(8,128)(2,1)}), bf16[4,768,384]{2,1,0:T(8,128)(2,1)S(1)}, u32[]{:S(2)}, u32[]{:S(2)}) async-start(bf16[4,768,384]{2,1,0:T(8,128)(2,1)} %copy-done.6), calls=%async_computation | async-start | bytes 4718592 | tf_op jit(solution)/shard_map/all_to_all | solution.py:406
  119.0 35.7 %copy-start.3 = (bf16[4,768,384]{2,1,0:T(8,128)(2,1)}, bf16[4,768,384]{2,1,0:T(8,128)(2,1)S(1)}, u32[]{:S(2)}) copy-start(bf16[4,768,384]{2,1,0:T(8,128)(2,1)S(1)} %all-to-all-done) | copy-start | bytes 7077892
  119.0 47.3 %all-to-all-start.2 = ((bf16[4,768,384]{2,1,0:T(8,128)(2,1)}), bf16[4,768,384]{2,1,0:T(8,128)(2,1)}, u32[]{:S(2)}, u32[]{:S(2)}) async-start(bf16[4,768,384]{2,1,0:T(8,128)(2,1)} %get-tuple-element.40), calls=%async_computation.2 | async-start | bytes 4718592 | tf_op jit(solution)/shard_map/all_to_all | solution.py:406
  166.3 35.9 %all-to-all-start.1 = ((bf16[4,768,128]{2,1,0:T(8,128)(2,1)}), bf16[4,768,128]{2,1,0:T(8,128)(2,1)S(1)}, u32[]{:S(2)}, u32[]{:S(2)}) async-start(bf16[4,768,128]{2,1,0:T(8,128)(2,1)} %bitcast.6), calls=%async_computation.1 | async-start | bytes 1572864 | tf_op jit(solution)/shard_map/all_to_all | solution.py:406
  170.0 37.6 %copy-start.36 = (s32[192]{0:T(256)S(1)}, s32[192]{0:T(256)}, u32[]{:S(2)}) copy-start(s32[192]{0:T(256)} %param.20) | copy-start | bytes 2308
  202.1 23.6 %copy-start.15 = (bf16[768,1024]{1,0:T(8,128)(2,1)S(1)}, bf16[768,1024]{1,0:T(8,128)(2,1)}, u32[]{:S(2)}) copy-start(bf16[768,1024]{1,0:T(8,128)(2,1)} %param.17) | copy-start | bytes 4718596
  202.1 16.5 %all-to-all-start.3 = ((bf16[4,768,128]{2,1,0:T(8,128)(2,1)}), bf16[4,768,128]{2,1,0:T(8,128)(2,1)}, u32[]{:S(2)}, u32[]{:S(2)}) async-start(bf16[4,768,128]{2,1,0:T(8,128)(2,1)} %bitcast.9), calls=%async_computation.3 | async-start | bytes 1572864 | tf_op jit(solution)/shard_map/all_to_all | solution.py:406
  251.5 22.4 %copy-start.18 = (f32[768,1024]{1,0:T(8,128)S(1)}, f32[768,1024]{1,0:T(8,128)}, u32[]{:S(2)}) copy-start(f32[768,1024]{1,0:T(8,128)} %copy-done.17) | copy-start | bytes 9437188
  299.2 31.8 %all-to-all-start.6 = ((bf16[4,768,128]{2,1,0:T(8,128)(2,1)}), bf16[4,768,128]{2,1,0:T(8,128)(2,1)}, u32[]{:S(2)}, u32[]{:S(2)}) async-start(bf16[4,768,128]{2,1,0:T(8,128)(2,1)} %get-tuple-element.75), calls=%async_computation.6 | async-start | bytes 1572864 | tf_op jit(solution)/shard_map/all_to_all | solution.py:406
  331.0 55.3 %all-to-all-start.4 = ((bf16[4,768,128]{2,1,0:T(8,128)(2,1)}), bf16[4,768,128]{2,1,0:T(8,128)(2,1)S(1)}, u32[]{:S(2)}, u32[]{:S(2)}) async-start(bf16[4,768,128]{2,1,0:T(8,128)(2,1)} %get-tuple-element.76), calls=%async_computation.4 | async-start | bytes 1572864 | tf_op jit(solution)/shard_map/all_to_all | solution.py:406
  386.4 55.4 %all-to-all-start.7 = ((bf16[4,768,384]{2,1,0:T(8,128)(2,1)}), bf16[4,768,384]{2,1,0:T(8,128)(2,1)S(1)}, u32[]{:S(2)}, u32[]{:S(2)}) async-start(bf16[4,768,384]{2,1,0:T(8,128)(2,1)} %bitcast.139), calls=%async_computation.7 | async-start | bytes 4718592 | tf_op jit(solution)/shard_map/all_to_all | solution.py:406
  441.7 33.5 %copy-start = (bf16[4,768,384]{2,1,0:T(8,128)(2,1)}, bf16[4,768,384]{2,1,0:T(8,128)(2,1)S(1)}, u32[]{:S(2)}) copy-start(bf16[4,768,384]{2,1,0:T(8,128)(2,1)S(1)} %all-to-all-done.7.refs_1_) | copy-start | bytes 7077892
  441.7 33.5 %all-to-all-start.5 = ((bf16[4,768,384]{2,1,0:T(8,128)(2,1)}), bf16[4,768,384]{2,1,0:T(8,128)(2,1)}, u32[]{:S(2)}, u32[]{:S(2)}) async-start(bf16[4,768,384]{2,1,0:T(8,128)(2,1)} %bitcast.138), calls=%async_computation.5 | async-start | bytes 4718592 | tf_op jit(solution)/shard_map/all_to_all | solution.py:406
  465.7 19.7 %copy-start.32 = (f32[1024]{0:T(1024)S(1)}, f32[1024]{0:T(1024)}, u32[]{:S(2)}) copy-start(f32[1024]{0:T(1024)} %copy-done.31) | copy-start | bytes 12292
  465.7 19.7 %copy-start.34 = (f32[768]{0:T(1024)S(1)}, f32[768]{0:T(1024)}, u32[]{:S(2)}) copy-start(f32[768]{0:T(1024)} %copy-done.33) | copy-start | bytes 9220
  627.7 30.2 %copy-start.38 = (f32[2,32]{1,0:T(2,128)S(1)}, f32[2,32]{1,0:T(2,128)}, u32[]{:S(2)}) copy-start(f32[2,32]{1,0:T(2,128)} %param.25) | copy-start | bytes 772
  627.8 30.2 %copy-start.39 = (f32[2,32]{1,0:T(2,128)S(1)}, f32[2,32]{1,0:T(2,128)}, u32[]{:S(2)}) copy-start(f32[2,32]{1,0:T(2,128)} %param.26) | copy-start | bytes 772
  627.8 30.2 %copy-start.40 = (f32[2,32]{1,0:T(2,128)S(1)}, f32[2,32]{1,0:T(2,128)}, u32[]{:S(2)}) copy-start(f32[2,32]{1,0:T(2,128)} %param.27) | copy-start | bytes 772
  630.5 33.0 %all-to-all-start.8 = ((bf16[6,32,8,256]{3,2,0,1:T(8,128)(2,1)}), bf16[6,32,8,256]{3,2,0,1:T(8,128)(2,1)}, u32[]{:S(2)}, u32[]{:S(2)}) async-start(bf16[6,32,8,256]{3,2,0,1:T(8,128)(2,1)} %copy.79), calls=%async_computation.8 | async-start | bytes 1572864 | tf_op jit(solution)/shard_map/all_to_all | solution.py:828
  689.4 59.8 %all-to-all-start.9 = ((bf16[6,32,8,256]{3,2,0,1:T(8,128)(2,1)}), bf16[6,32,8,256]{3,2,0,1:T(8,128)(2,1)S(1)}, u32[]{:S(2)}, u32[]{:S(2)}) async-start(bf16[6,32,8,256]{3,2,0,1:T(8,128)(2,1)} %copy.81), calls=%async_computation.9 | async-start | bytes 1572864 | tf_op jit(solution)/shard_map/all_to_all | solution.py:843
  (34 other events, 142.8 us)
Sparse Core Ops, SparseCore 0:
  11.5 62.3 all-gather.3
  77.4 94.3 all-gather.7
  175.3 76.1 all-gather.5

commit v4 on v3

--- a/solution.py
+++ b/solution.py
@@ -31,6 +31,8 @@
 VMEM_LIMIT = 48 * 2**20
 AHEAD = 4
 SKEW = 3
+PACE = 0.9
+DELAY = 1.0
 
 
 def shortened(shard):
@@ -143,14 +145,35 @@
     )(lengths, scene, scene, scene)
 
 
-def attend_backward_kernel(
-    safe, chunk, length_ref, q_ref, k_ref, v_ref, o_ref, do_ref, log_ref, out_ref, kt_ref, dk_sum, dv_sum
-):
+def attend_backward_kernel(safe, chunk, plan, slots, length_ref, q_ref, k_ref, v_ref, o_ref, do_ref, log_ref, *refs):
+    count = plan[4]
+    sources, out_ref, outs = refs[:count], refs[count], refs[count + 1 : 2 * count + 1]
+    kt_ref, dk_sum, dv_sum = refs[2 * count + 1 : 2 * count + 4]
+    peers, begin, finish, drain = reduce_steps(*plan[:4], sources, outs, refs[2 * count + 4 :])
+    total = len(plan[3])
     seq_len = k_ref.shape[0]
     length = length_ref[0]
-
-    @pl.when(pl.program_id(1) == 0)
+    step = pl.program_id(0)
+
+    def move(chunk, stage):
+        finish(chunk, stage)
+        if stage == 0 and chunk + AHEAD < total:
+            begin(chunk + AHEAD)
+
+    def move_at(head):
+        for at in range(head, len(slots) - 1, 2):
+            if slots[at]:
+
+                @pl.when(step == at // 2)
+                def _(at=at):
+                    for chunk, stage in slots[at]:
+                        move(chunk, stage)
+
+    @pl.when(step == 0)
     def _():
+        greet(peers)
+        for chunk in range(min(AHEAD, total)):
+            begin(chunk)
         kt_ref[...] = k_ref[...].T
         dk_sum[...] = jnp.zeros_like(dk_sum)
         dv_sum[...] = jnp.zeros_like(dv_sum)
@@ -158,6 +181,7 @@
     products = (o_ref[...].astype(float32) * do_ref[...].astype(float32)).T
     turned = []
     for head in range(2):
+        move_at(head)
         lanes = slice(head * HEAD, (head + 1) * HEAD)
         queries = one_head(q_ref[...], head) * bfloat16(HEAD**-0.5)
         d_mixed = one_head(do_ref[...], head)
@@ -177,45 +201,63 @@
             d_queries += jnp.dot(kt_ref[lanes, part], d_scores, preferred_element_type=float32)
         turned.append(d_queries * HEAD**-0.5)
     rows = q_ref.shape[0]
-    here = pl.ds(pl.multiple_of(pl.program_id(1) * rows, rows), rows)
+    here = pl.ds(pl.multiple_of(step * rows, rows), rows)
     out_ref[here, :PAIR] = jnp.concatenate(turned, 0).T.astype(bfloat16)
 
-    @pl.when(pl.program_id(1) == pl.num_programs(1) - 1)
+    @pl.when(step == pl.num_programs(0) - 1)
     def _():
         out_ref[:, PAIR : 2 * PAIR] = dk_sum[...].astype(bfloat16)
         out_ref[:, 2 * PAIR :] = dv_sum[...].astype(bfloat16)
-
-
-def attend_backward(lengths, scene, mixed, d_mixed, log_totals, safe, rows=512, chunk=1024):
-    seq_len, width = mixed.shape
-    pairs = width // PAIR
-    tile = pl.BlockSpec((rows, PAIR), lambda p, i: (i, p))
+        for chunk, stage in slots[-1]:
+            move(chunk, stage)
+        drain()
+
+
+def attend_backward(
+    lengths, scene, mixed, d_mixed, log_totals, safe, parts, pieces, collective_id, rows=512, chunk=1024
+):
+    seq_len = scene.shape[0]
+    bits, narrow_bits, plans, chunks, halved, outs, scratch = reduce_plan(parts, pieces)
+    steps = seq_len // rows
+    slots = reduce_slots(len(chunks), bits, 2 * steps, PACE, DELAY)
+    tile = pl.BlockSpec((rows, PAIR), lambda i: (i, 0))
     return pl.pallas_call(
-        partial(attend_backward_kernel, safe, chunk),
-        grid=(pairs, seq_len // rows),
+        partial(
+            attend_backward_kernel,
+            safe,
+            chunk,
+            (bits, narrow_bits, plans, chunks, len(parts)),
+            slots,
+        ),
+        grid=(steps,),
         in_specs=[
             pl.BlockSpec(memory_space=pltpu.SMEM),
             tile,
-            pl.BlockSpec((seq_len, PAIR), lambda p, i: (0, pairs + p)),
-            pl.BlockSpec((seq_len, PAIR), lambda p, i: (0, 2 * pairs + p)),
+            pl.BlockSpec((seq_len, PAIR), lambda i: (0, 1)),
+            pl.BlockSpec((seq_len, PAIR), lambda i: (0, 2)),
             tile,
             tile,
-            pl.BlockSpec((1, 2, rows), lambda p, i: (p, 0, i)),
-        ],
-        out_specs=pl.BlockSpec((seq_len, 3 * PAIR), lambda p, i: (0, p)),
-        out_shape=jax.ShapeDtypeStruct((seq_len, 3 * width), bfloat16),
+            pl.BlockSpec((1, 2, rows), lambda i: (0, 0, i)),
+        ]
+        + [pl.BlockSpec(memory_space=pl.ANY)] * len(parts),
+        out_specs=[pl.BlockSpec((seq_len, 3 * PAIR), lambda i: (0, 0))]
+        + [pl.BlockSpec(out.shape, lambda i: (0, 0)) for out in outs],
+        out_shape=[jax.ShapeDtypeStruct((seq_len, 3 * PAIR), bfloat16)] + outs,
         scratch_shapes=[
             pltpu.VMEM((PAIR, seq_len), bfloat16),
             pltpu.VMEM((seq_len, PAIR), float32),
             pltpu.VMEM((seq_len, PAIR), float32),
-        ],
-        compiler_params=pltpu.CompilerParams(vmem_limit_bytes=VMEM_LIMIT),
+        ]
+        + scratch,
+        compiler_params=pltpu.CompilerParams(
+            collective_id=collective_id, has_side_effects=True, vmem_limit_bytes=58 * 2**20
+        ),
         cost_estimate=pl.CostEstimate(
-            flops=4 * pairs * 2 * 10 * seq_len * seq_len * HEAD,
-            bytes_accessed=16 * seq_len * width,
+            flops=4 * 2 * 10 * seq_len * seq_len * HEAD,
+            bytes_accessed=16 * seq_len * PAIR,
             transcendentals=0,
         ),
-    )(lengths, scene, scene, scene, mixed, d_mixed, log_totals)
+    )(lengths, scene, scene, scene, mixed, d_mixed, log_totals, *halved)
 
 
 def project_kernel(acts_ref, wq_ref, wk_ref, wv_ref, *out_refs):
@@ -425,13 +467,12 @@
     return narrow_bits + lax.axis_size("wide").bit_length() - 1, narrow_bits
 
 
-def reduce_kernel(bits, narrow_bits, plans, chunks, count, *refs):
-    sources, outs, scratch = refs[:count], refs[count : 2 * count], refs[2 * count :]
+def reduce_steps(bits, narrow_bits, plans, chunks, sources, outs, scratch):
+    count = len(sources)
     held = scratch[:count]
     arrived = [scratch[count * (1 + s) : count * (2 + s)] for s in range(bits)]
     load_sem, send_sem, recv_sem = scratch[count * (1 + bits) :]
     peers = [partner(b, narrow_bits) for b in range(bits)]
-    greet(peers)
     first = plans[0][0]
     order_of_dims = list(reversed(range(bits)))
     whole = slice(None)
@@ -503,6 +544,19 @@
         lax.fori_loop(0, 1 << left, add, 0)
         send(chunk, stage + 1).start()
 
+    def drain():
+        for chunk in range(len(chunks)):
+            for stage in range(bits):
+                send(chunk, stage).wait_send()
+
+    return peers, begin, finish, drain
+
+
+def reduce_kernel(bits, narrow_bits, plans, chunks, count, *refs):
+    peers, begin, finish, drain = reduce_steps(
+        bits, narrow_bits, plans, chunks, refs[:count], refs[count : 2 * count], refs[2 * count :]
+    )
+    greet(peers)
     total = len(chunks)
     for chunk in range(min(AHEAD, total)):
         begin(chunk)
@@ -513,20 +567,30 @@
                 finish(chunk, stage)
                 if stage == 0 and chunk + AHEAD < total:
                     begin(chunk + AHEAD)
-    for chunk in range(total):
-        for stage in range(bits):
-            send(chunk, stage).wait_send()
-
-
-def reduce_to_shards(parts, pieces, collective_id):
+    drain()
+
+
+def reduce_slots(chunks, bits, slots, pace, delay):
+    table = [[] for _ in range(slots + 1)]
+    done = sorted(
+        (chunk * pace + (stage + 1) * delay, -stage, chunk, stage)
+        for chunk in range(chunks)
+        for stage in range(bits)
+    )
+    for when, _, chunk, stage in done:
+        table[min(int(when), slots)].append((chunk, stage))
+    return table
+
+
+def reduce_plan(parts, pieces):
     bits, narrow_bits = mesh_bits()
     shapes = [part.shape[1:] for part in parts]
     kinds = [part.dtype for part in parts]
     chunks = []
     for at, (shape, cut) in enumerate(zip(shapes, pieces)):
         rows = shape[0] // cut
-        chunks += [(at, row, rows, len(chunks) % 2) for row in range(0, shape[0], rows)]
-        chunks = [(a, r, n, i % 2) for i, (a, r, n, _) in enumerate(chunks)]
+        for row in range(0, shape[0], rows):
+            chunks.append((at, row, rows, len(chunks) % 2))
     later = tuple(range(3, bits))
     plans = ((0, 2, 1) + later, (0, 1, 2) + later)
     sizes = [bits - 1] + [bits - 1 - stage for stage in range(bits)]
@@ -541,9 +605,16 @@
         pltpu.SemaphoreType.DMA((total, bits)),
         pltpu.SemaphoreType.DMA((total, bits)),
     ]
+    outs = [jax.ShapeDtypeStruct(shape, float32) for shape in shapes]
+    halved = [part.reshape((2,) * bits + shape) for part, shape in zip(parts, shapes)]
+    return bits, narrow_bits, plans, tuple(chunks), halved, outs, scratch
+
+
+def reduce_to_shards(parts, pieces, collective_id):
+    bits, narrow_bits, plans, chunks, halved, outs, scratch = reduce_plan(parts, pieces)
     return pl.pallas_call(
-        partial(reduce_kernel, bits, narrow_bits, plans, tuple(chunks), len(parts)),
-        out_shape=[jax.ShapeDtypeStruct(shape, float32) for shape in shapes],
+        partial(reduce_kernel, bits, narrow_bits, plans, chunks, len(parts)),
+        out_shape=outs,
         in_specs=[pl.BlockSpec(memory_space=pl.ANY)] * len(parts),
         out_specs=[pl.BlockSpec(memory_space=pltpu.VMEM)] * len(parts),
         scratch_shapes=scratch,
@@ -551,7 +622,7 @@
             collective_id=collective_id, has_side_effects=True, vmem_limit_bytes=58 * 2**20
         ),
         cost_estimate=pl.CostEstimate(flops=10**8, bytes_accessed=4 * 10**8, transcendentals=0),
-    )(*(part.reshape((2,) * bits + shape) for part, shape in zip(parts, shapes)))
+    )(*halved)
 
 
 def gather_kernel(bits, narrow_bits, plans, chunks, count, *refs):
@@ -790,10 +861,16 @@
     )
     d_mixed = d_merged.reshape(tok_rows, narrow_count, halves, PAIR).transpose(2, 1, 0, 3)
     d_mixed = [exchange(d_mixed[half]).reshape(seq_len, PAIR) for half in range(halves)]
-    d_scenes = [
-        attend_backward(lengths, scene, mixed, d_mixed_one, log_total, safe)
-        for scene, (mixed, log_total), d_mixed_one in zip(scenes, attended, d_mixed)
-    ]
+    ready = (((d_w_hidden, d_proj), (8, 2)), ((d_back,), (8,)))
+    d_scenes, summed = [], []
+    for half in range(halves):
+        mixed, log_total = attended[half]
+        parts, cuts = ready[half]
+        d_scene, *sums = attend_backward(
+            lengths, scenes[half], mixed, d_mixed[half], log_total, safe, parts, cuts, 4 + half
+        )
+        d_scenes.append(d_scene)
+        summed.append(sums)
     d_packed = [exchange(d.reshape(narrow_count, tok_rows, 3 * PAIR)) for d in d_scenes]
     grouped = tuple(
         tuple((half, group, third * PAIR, PAIR) for half in range(halves))
@@ -806,9 +883,9 @@
     grad_tokens = (d_middle + d_norm_one).astype(jnp.bfloat16)
     gain_parts = jnp.stack([d_gain_one, d_gain_two]).reshape(2, device_count, share)
     gain_parts = jnp.pad(gain_parts.transpose(1, 0, 2), ((0, 0), (0, 6), (0, 128 - share)))
-    *grad_shards, gain_grad = reduce_to_shards(
-        (d_attn, d_proj, d_w_hidden, d_back, gain_parts), (6, 2, 8, 8, 1), 1
-    )
+    attn_sum, gain_grad = reduce_to_shards((d_attn, gain_parts), (6, 1), 1)
+    (hidden_sum, proj_sum), (back_sum,) = summed
+    grad_shards = (attn_sum, proj_sum, hidden_sum, back_sum)
     gain_grad = gain_grad[:2, :share]
     band_rows = BLOCK // device_count
     local_squares = jnp.sum(gain_grad * gain_grad) + sum(

time: 769 us -> 772 us (level)
    unnamed x93 -> x97, local copies, waits for them, and re-layouts: 19.8 us -> 16.9 us
  transfers between devices with their start and end apart: 13 -> 13, of which waited for: 5 -> 5; matrix products, arithmetic and copies ran while one was open for 8% -> 8% of each run, Pallas kernels for 43% -> 53%
where the time goes in v4:
time: 772 us; the launch traced here: 766 us
  Pallas kernels  496 us (64%)
  waiting for transfers between devices  75.6 us (10%)
  matrix products  68.3 us (9%)
  starting transfers between devices  40.4 us (5%)
  local copies, waits for them, and re-layouts  34.5 us (4%)
  other arithmetic  30.9 us (4%)
  between operations  20.5 us (3%)
    pallas_call x2, Pallas kernels, attend_backward(): pl.pallas_call(partial(attend_backward_kernel, safe, chunk, (bits, narrow...  181 us
    all_to_all x8, waiting for transfers between devices, exchange(): lax.all_to_all(groups, 'narrow', split_axis=0, concat_axis=0, tiled=True)  69.3 us
    pallas_call x2, Pallas kernels, attend(): pl.pallas_call(partial(attend_kernel, safe, chunk), grid=(pairs, seq_len...  63.1 us
    pallas_call x1, Pallas kernels, renew_bases(): pl.pallas_call(partial(renew_kernel, rows), out_shape=jax.ShapeDtypeStruc...  54.7 us
    pallas_call x1, Pallas kernels, gather_bands(): pl.pallas_call(partial(gather_kernel, bits, narrow_bits, plans, tuple(chu...  52.8 us
    pallas_call x1, Pallas kernels, reduce_to_shards(): pl.pallas_call(partial(reduce_kernel, bits, narrow_bits, plans, chunks, l...  44.9 us
    pallas_call x4, Pallas kernels, weight_grad(): pl.pallas_call(partial(weight_grad_kernel, columns, band_rows), grid=(ban...  40.5 us
    all_to_all x8, starting transfers between devices, exchange(): lax.all_to_all(groups, 'narrow', split_axis=0, concat_axis=0, tiled=True)  33.4 us
  transfers between devices with their start and end apart: 13, of which 5 were waited for; matrix products, arithmetic and copies ran while one was open for 8% of the time, Pallas kernels for 53%

profile of v4, /device:TPU:0, one launch (start us, length us, event | category | flops | bytes accessed | tf_op | source)
XLA Modules:
  0.0 766.1 jit_solution(1830549586055935416)
XLA Ops:
  15.6 52.8 %shard_map.288 = (bf16[4,2,2,2,2,2,8,3072]{7,6,5,4,3,2,1,0:T(8,128)(2,1)}, bf16[1,2,2,2,2,2,8,128]{7,6,5,4,3,2,1,0:T(8,128)(2,1)}) custom-call(bf16[4,8,3072]{2,1,0:T(8,128)(2,1)} %convert_element_type.70.refs_0_, bf16[1,8,128]{2,1,0:T(8,128)(2,1)} %pad_bitcast_fusion.refs_1_), custom_call_target="tpu_custom_call" | custom-call | bytes 100000000 | tf_op jit(solution)/shard_map/pallas_call | solution.py:689
  70.9 8.6 %shard_map.289 = (bf16[4,768,384]{2,1,0:T(8,128)(2,1)S(1)}, bf16[4,768,384]{2,1,0:T(8,128)(2,1)}) custom-call(bf16[768,1024]{1,0:T(8,128)(2,1)S(1)} %fusion.13.acts_ref.left_ref, bf16[1024,3072]{1,0:T(8,128)(2,1)} %bitcast.142, bf16[1024,3072]{1,0:T(8,128)(2,1)} %bitcast.143, bf16[1024,3072]{1,0:T(8,128)(2,1)} %bitcast.144), custom_call_target="tpu_custom_call" | custom-call | flops 4831838208 | bytes 12582912 | tf_op jit(solution)/shard_map/pallas_call | solution.py:282
  85.2 33.8 %all-to-all-done = bf16[4,768,384]{2,1,0:T(8,128)(2,1)S(1)} async-done(((bf16[4,768,384]{2,1,0:T(8,128)(2,1)}), bf16[4,768,384]{2,1,0:T(8,128)(2,1)S(1)}, u32[]{:S(2)}, u32[]{:S(2)}) %all-to-all-start) | async-done | bytes 2359328 | tf_op jit(solution)/shard_map/all_to_all | solution.py:448
  123.6 31.0 %shard_map.290 = (bf16[3072,128]{1,0:T(8,128)(2,1)}, f32[1,2,3072]{2,1,0:T(2,128)S(1)}) custom-call(s32[1]{0:T(128)S(6)} %copy.114.length_ref, bf16[3072,384]{1,0:T(8,128)(2,1)S(1)} %bitcast.132, bf16[3072,384]{1,0:T(8,128)(2,1)S(1)} %bitcast.133, bf16[3072,384]{1,0:T(8,128)(2,1)S(1)} %bitcast.134), custom_call_target="tpu_custom_call" | custom-call | flops 19327352832 | bytes 3145728 | tf_op jit(solution)/shard_map/pallas_call | solution.py:118
  155.2 11.0 %all-to-all-done.2 = bf16[4,768,384]{2,1,0:T(8,128)(2,1)} async-done(((bf16[4,768,384]{2,1,0:T(8,128)(2,1)}), bf16[4,768,384]{2,1,0:T(8,128)(2,1)}, u32[]{:S(2)}, u32[]{:S(2)}) %all-to-all-start.2) | async-done | bytes 2359328 | tf_op jit(solution)/shard_map/all_to_all | solution.py:448
  170.0 32.1 %shard_map.291 = (bf16[3072,128]{1,0:T(8,128)(2,1)}, f32[1,2,3072]{2,1,0:T(2,128)S(1)}) custom-call(s32[1]{0:T(128)S(6)} %copy.114.length_ref, bf16[3072,384]{1,0:T(8,128)(2,1)} %bitcast.8.q_ref.k_ref.v_ref, bf16[3072,384]{1,0:T(8,128)(2,1)} %bitcast.8.q_ref.k_ref.v_ref, bf16[3072,384]{1,0:T(8,128)(2,1)} %bitcast.8.q_ref.k_ref.v_ref), custom_call_target="tpu_custom_call" | custom-call | flops 19327352832 | bytes 3145728 | tf_op jit(solution)/shard_map/pallas_call | solution.py:118
  209.8 9.3 %all-to-all-done.3 = bf16[4,768,128]{2,1,0:T(8,128)(2,1)} async-done(((bf16[4,768,128]{2,1,0:T(8,128)(2,1)}), bf16[4,768,128]{2,1,0:T(8,128)(2,1)}, u32[]{:S(2)}, u32[]{:S(2)}) %all-to-all-start.3) | async-done | bytes 786464 | tf_op jit(solution)/shard_map/all_to_all | solution.py:448
  232.8 12.5 %fusion.52 = f32[768,4096]{1,0:T(8,128)} fusion(bf16[768,1024]{1,0:T(8,128)(2,1)S(1)} %copy-done.5, bf16[4096,1024]{1,0:T(8,128)(2,1)} %bitcast.162), kind=kOutput, calls=%fused_computation.110 | convolution fusion | flops 6442450944 | bytes 22544384 | tf_op jit(solution)/shard_map/td,fd->tf/dot_general | solution.py:850
  245.3 6.2 all-gather.6.cloned.1.call-done
  251.5 22.4 %fusion.6 = (bf16[768,4096]{1,0:T(8,128)(2,1)}, bf16[768,4096]{1,0:T(8,128)(2,1)}) fusion(f32[768,4096]{1,0:T(8,128)} %fusion.52, bf16[768,1024]{1,0:T(8,128)(2,1)S(1)} %multiply_convert_fusion.1.left_ref, bf16[1024,4096]{1,0:T(8,128)(2,1)} %bitcast.164), kind=kOutput, calls=%fused_computation.8 | convolution fusion | flops 6511656960 | bytes 35127296 | tf_op jit(solution)/shard_map/dot_general | solution.py:843
  274.0 11.9 %multiply_reduce_fusion = (f32[1024]{0:T(1024)S(1)}, f32[768]{0:T(1024)S(1)}, f32[768]{0:T(1024)S(1)}, f32[768,1024]{1,0:T(8,128)S(1)}) fusion(f32[768,1024]{1,0:T(8,128)S(1)} %copy-done.18, f32[768]{0:T(1024)S(1)} %add_rsqrt_fusion, f32[768]{0:T(1024)S(1)} %broadcast_multiply_fusion.4, f32[1024]{0:T(1024)S(1)} %mul.238, ...), kind=kOutput, calls=%fused_computation.27 | convolution fusion | flops 6448739328 | bytes 20992000 | tf_op jit(solution)/shard_map/tf,df->td/dot_general | solution.py:854
  309.2 12.3 %shard_map.292 = bf16[32,512,256]{2,1,0:T(8,128)(2,1)} custom-call(bf16[768,1024]{1,0:T(8,128)(2,1)S(1)} %multiply_convert_fusion.1.left_ref, bf16[1,768,4096]{2,1,0:T(8,128)(2,1)} %bitcast.170), custom_call_target="tpu_custom_call" | custom-call | flops 6442450944 | bytes 16252928 | tf_op jit(solution)/shard_map/pallas_call | solution.py:769
  321.6 15.8 %shard_map.295 = bf16[32,512,256]{2,1,0:T(8,128)(2,1)} custom-call(bf16[768,4096]{1,0:T(8,128)(2,1)} %get-tuple-element.74.left_ref, bf16[1,768,1024]{2,1,0:T(8,128)(2,1)S(1)} %bitcast.138), custom_call_target="tpu_custom_call" | custom-call | flops 6442450944 | bytes 16252928 | tf_op jit(solution)/shard_map/pallas_call | solution.py:769
  341.2 78.5 %shard_map.296 = (bf16[3072,384]{1,0:T(8,128)(2,1)}, f32[512,256]{1,0:T(8,128)}) custom-call(s32[1]{0:T(128)S(6)} %copy.114.length_ref, bf16[3072,384]{1,0:T(8,128)(2,1)} %bitcast.8.q_ref.k_ref.v_ref, bf16[3072,384]{1,0:T(8,128)(2,1)} %bitcast.8.q_ref.k_ref.v_ref, bf16[3072,384]{1,0:T(8,128)(2,1)} %bitcast.8.q_ref.k_ref.v_ref, ...), custom_call_target="tpu_custom_call" | custom-call | flops 48318382080 | bytes 6291456 | tf_op jit(solution)/shard_map/pallas_call | solution.py:224
  423.8 102.6 %shard_map.294 = (bf16[3072,384]{1,0:T(8,128)(2,1)}, f32[512,256]{1,0:T(8,128)}, f32[128,256]{1,0:T(8,128)}) custom-call(s32[1]{0:T(128)S(6)} %copy.114.length_ref, bf16[3072,384]{1,0:T(8,128)(2,1)} %bitcast.135, bf16[3072,384]{1,0:T(8,128)(2,1)} %bitcast.136, bf16[3072,384]{1,0:T(8,128)(2,1)} %bitcast.137, bf16[3072,128]{1,0:T(8,128)(2,1)} %get-tuple-element.41.o_ref, ...), custom_call_target="tpu_custom_call" | custom-call | flops 48318382080 | bytes 6291456 | tf_op jit(solution)/shard_map/pallas_call | solution.py:224
  531.2 12.6 %add_convert_fusion = bf16[768,1024]{1,0:T(8,128)(2,1)} fusion(f32[768,1024]{1,0:T(8,128)} %copy-done.17, bf16[768,4096]{1,0:T(8,128)(2,1)} %get-tuple-element.74.left_ref, bf16[4096,1024]{1,0:T(8,128)(2,1)} %bitcast.163), kind=kOutput, calls=%fused_computation.30 | convolution fusion | flops 6444023808 | bytes 19398656 | tf_op jit(solution)/shard_map/dot_general | solution.py:845
  544.5 15.2 %all-to-all-done.5.refs_0_ = bf16[4,768,384]{2,1,0:T(8,128)(2,1)} async-done(((bf16[4,768,384]{2,1,0:T(8,128)(2,1)}), bf16[4,768,384]{2,1,0:T(8,128)(2,1)}, u32[]{:S(2)}, u32[]{:S(2)}) %all-to-all-start.5) | async-done | bytes 2359328 | tf_op jit(solution)/shard_map/all_to_all | solution.py:448
  559.7 10.1 %shard_map.297 = f32[768,1024]{1,0:T(8,128)} custom-call(bf16[4,768,384]{2,1,0:T(8,128)(2,1)} %all-to-all-done.5.refs_0_, bf16[4,768,384]{2,1,0:T(8,128)(2,1)S(1)} %all-to-all-done.7.refs_1_, bf16[1024,3072]{1,0:T(8,128)(2,1)} %bitcast.145, bf16[1024,3072]{1,0:T(8,128)(2,1)} %bitcast.146, bf16[1024,3072]{1,0:T(8,128)(2,1)} %bitcast.147), custom_call_target="tpu_custom_call" | custom-call | flops 4831838208 | bytes 14155776 | tf_op jit(solution)/shard_map/pallas_call | solution.py:322
  574.0 9.5 %shard_map.298 = bf16[32,384,256]{2,1,0:T(8,128)(2,1)} custom-call(bf16[768,1024]{1,0:T(8,128)(2,1)S(1)} %copy-done.2, bf16[4,768,384]{2,1,0:T(8,128)(2,1)} %all-to-all-done.5.refs_0_, bf16[4,768,384]{2,1,0:T(8,128)(2,1)} %copy-done), custom_call_target="tpu_custom_call" | custom-call | flops 4831838208 | bytes 12582912 | tf_op jit(solution)/shard_map/pallas_call | solution.py:769
  583.5 44.9 %shard_map.299 = (f32[384,256]{1,0:T(8,128)}, f32[8,128]{1,0:T(8,128)}) custom-call(bf16[2,2,2,2,2,384,256]{6,5,4,3,2,1,0:T(8,128)(2,1)} %bitcast.148, f32[2,2,2,2,2,8,128]{6,5,4,3,2,1,0:T(8,128)} %bitcast.158), custom_call_target="tpu_custom_call" | custom-call | flops 100000000 | bytes 400000000 | tf_op jit(solution)/shard_map/pallas_call | solution.py:615
  642.2 16.2 %shard_map.300 = f32[8,128]{1,0:T(8,128)} custom-call(f32[8,128]{1,0:T(8,128)} %broadcast_in_dim.14.own_ref), custom_call_target="tpu_custom_call" | custom-call | tf_op jit(solution)/shard_map/pallas_call | solution.py:732
  660.9 4.9 fusion.18
  667.1 23.8 %shard_map.301 = (bf16[6,256,256]{2,1,0:T(8,128)(2,1)S(1)}, f32[6,256,256]{2,1,0:T(8,128)}, f32[6,256,256]{2,1,0:T(8,128)}, f32[6,256,256]{2,1,0:T(8,128)}, f32[...) custom-call(f32[1,1]{1,0:T(1,128)} %bitcast.39.factor_ref, ...), custom_call_target="tpu_custom_call" | custom-call | flops 12079595520 | bytes 23592960 | tf_op jit(solution)/shard_map/pallas_call | solution.py:371
  695.4 54.7 %shard_map.302 = f32[12,256,256]{2,1,0:T(8,128)S(1)} custom-call(f32[12,256,256]{2,1,0:T(8,128)} %bitcast.171, f32[12,256,256]{2,1,0:T(8,128)} %bitcast.172), custom_call_target="tpu_custom_call" | custom-call | flops 40265318400 | bytes 9437184 | tf_op jit(solution)/shard_map/pallas_call | solution.py:431
  (189 shorter events, 112.6 us)
Async XLA Ops:
  7.2 62.2 %copy-start.14 = (bf16[768,1024]{1,0:T(8,128)(2,1)S(1)}, bf16[768,1024]{1,0:T(8,128)(2,1)}, u32[]{:S(2)}) copy-start(bf16[768,1024]{1,0:T(8,128)(2,1)} %param.17) | copy-start | bytes 4718596
  7.2 219.0 %all-gather.4.cloned.1.call-start = ((), (), s32[]{:S(2)}) async-start(), calls=%async_computation.10 | async-start | bytes 2162688 | tf_op jit(solution)/shard_map/all_gather | solution.py:823
  8.9 223.4 %all-gather.8.cloned.1.call-start = ((), (), s32[]{:S(2)}) async-start(), calls=%async_computation.12 | async-start | bytes 8650752 | tf_op jit(solution)/shard_map/all_gather | solution.py:823
  10.8 240.8 %all-gather.6.cloned.1.call-start = ((), (), s32[]{:S(2)}) async-start(), calls=%async_computation.11 | async-start | bytes 8650752 | tf_op jit(solution)/shard_map/all_gather | solution.py:823
  80.9 38.1 %all-to-all-start = ((bf16[4,768,384]{2,1,0:T(8,128)(2,1)}), bf16[4,768,384]{2,1,0:T(8,128)(2,1)S(1)}, u32[]{:S(2)}, u32[]{:S(2)}) async-start(bf16[4,768,384]{2,1,0:T(8,128)(2,1)} %copy-done.4), calls=%async_computation | async-start | bytes 4718592 | tf_op jit(solution)/shard_map/all_to_all | solution.py:448
  119.0 35.7 %copy-start.3 = (bf16[4,768,384]{2,1,0:T(8,128)(2,1)}, bf16[4,768,384]{2,1,0:T(8,128)(2,1)S(1)}, u32[]{:S(2)}) copy-start(bf16[4,768,384]{2,1,0:T(8,128)(2,1)S(1)} %all-to-all-done) | copy-start | bytes 7077892
  119.0 47.3 %all-to-all-start.2 = ((bf16[4,768,384]{2,1,0:T(8,128)(2,1)}), bf16[4,768,384]{2,1,0:T(8,128)(2,1)}, u32[]{:S(2)}, u32[]{:S(2)}) async-start(bf16[4,768,384]{2,1,0:T(8,128)(2,1)} %get-tuple-element.42), calls=%async_computation.2 | async-start | bytes 4718592 | tf_op jit(solution)/shard_map/all_to_all | solution.py:448
  166.2 36.4 %all-to-all-start.1 = ((bf16[4,768,128]{2,1,0:T(8,128)(2,1)}), bf16[4,768,128]{2,1,0:T(8,128)(2,1)S(1)}, u32[]{:S(2)}, u32[]{:S(2)}) async-start(bf16[4,768,128]{2,1,0:T(8,128)(2,1)} %bitcast.6), calls=%async_computation.1 | async-start | bytes 1572864 | tf_op jit(solution)/shard_map/all_to_all | solution.py:448
  169.9 38.1 %copy-start.38 = (s32[192]{0:T(256)S(1)}, s32[192]{0:T(256)}, u32[]{:S(2)}) copy-start(s32[192]{0:T(256)} %param.20) | copy-start | bytes 2308
  202.7 16.4 %all-to-all-start.3 = ((bf16[4,768,128]{2,1,0:T(8,128)(2,1)}), bf16[4,768,128]{2,1,0:T(8,128)(2,1)}, u32[]{:S(2)}, u32[]{:S(2)}) async-start(bf16[4,768,128]{2,1,0:T(8,128)(2,1)} %bitcast.9), calls=%async_computation.3 | async-start | bytes 1572864 | tf_op jit(solution)/shard_map/all_to_all | solution.py:448
  299.4 38.1 %all-to-all-start.6 = ((bf16[4,768,128]{2,1,0:T(8,128)(2,1)}), bf16[4,768,128]{2,1,0:T(8,128)(2,1)}, u32[]{:S(2)}, u32[]{:S(2)}) async-start(bf16[4,768,128]{2,1,0:T(8,128)(2,1)} %get-tuple-element.79), calls=%async_computation.6 | async-start | bytes 1572864 | tf_op jit(solution)/shard_map/all_to_all | solution.py:448
  337.4 82.3 %all-to-all-start.4 = ((bf16[4,768,128]{2,1,0:T(8,128)(2,1)}), bf16[4,768,128]{2,1,0:T(8,128)(2,1)S(1)}, u32[]{:S(2)}, u32[]{:S(2)}) async-start(bf16[4,768,128]{2,1,0:T(8,128)(2,1)} %get-tuple-element.80), calls=%async_computation.4 | async-start | bytes 1572864 | tf_op jit(solution)/shard_map/all_to_all | solution.py:448
  419.7 106.7 %all-to-all-start.7 = ((bf16[4,768,384]{2,1,0:T(8,128)(2,1)}), bf16[4,768,384]{2,1,0:T(8,128)(2,1)S(1)}, u32[]{:S(2)}, u32[]{:S(2)}) async-start(bf16[4,768,384]{2,1,0:T(8,128)(2,1)} %bitcast.150), calls=%async_computation.7 | async-start | bytes 4718592 | tf_op jit(solution)/shard_map/all_to_all | solution.py:448
  526.4 33.3 %copy-start = (bf16[4,768,384]{2,1,0:T(8,128)(2,1)}, bf16[4,768,384]{2,1,0:T(8,128)(2,1)S(1)}, u32[]{:S(2)}) copy-start(bf16[4,768,384]{2,1,0:T(8,128)(2,1)S(1)} %all-to-all-done.7.refs_1_) | copy-start | bytes 7077892
  526.4 33.2 %all-to-all-start.5 = ((bf16[4,768,384]{2,1,0:T(8,128)(2,1)}), bf16[4,768,384]{2,1,0:T(8,128)(2,1)}, u32[]{:S(2)}, u32[]{:S(2)}) async-start(bf16[4,768,384]{2,1,0:T(8,128)(2,1)} %bitcast.151), calls=%async_computation.5 | async-start | bytes 4718592 | tf_op jit(solution)/shard_map/all_to_all | solution.py:448
  544.5 25.4 %copy-start.34 = (f32[1024]{0:T(1024)S(1)}, f32[1024]{0:T(1024)}, u32[]{:S(2)}) copy-start(f32[1024]{0:T(1024)} %copy-done.33) | copy-start | bytes 12292
  544.5 25.4 %copy-start.36 = (f32[768]{0:T(1024)S(1)}, f32[768]{0:T(1024)}, u32[]{:S(2)}) copy-start(f32[768]{0:T(1024)} %copy-done.35) | copy-start | bytes 9220
  583.5 44.9 %copy-start.23 = (f32[512,256]{1,0:T(8,128)S(1)}, f32[512,256]{1,0:T(8,128)}, u32[]{:S(2)}) copy-start(f32[512,256]{1,0:T(8,128)} %get-tuple-element.52) | copy-start | bytes 1572868
  583.5 44.9 %copy-start.30 = (f32[128,256]{1,0:T(8,128)S(1)}, f32[128,256]{1,0:T(8,128)}, u32[]{:S(2)}) copy-start(f32[128,256]{1,0:T(8,128)} %get-tuple-element.50) | copy-start | bytes 393220
  629.6 30.7 %copy-start.40 = (f32[2,32]{1,0:T(2,128)S(1)}, f32[2,32]{1,0:T(2,128)}, u32[]{:S(2)}) copy-start(f32[2,32]{1,0:T(2,128)} %param.25) | copy-start | bytes 772
  629.6 30.7 %copy-start.41 = (f32[2,32]{1,0:T(2,128)S(1)}, f32[2,32]{1,0:T(2,128)}, u32[]{:S(2)}) copy-start(f32[2,32]{1,0:T(2,128)} %param.26) | copy-start | bytes 772
  629.6 30.7 %copy-start.42 = (f32[2,32]{1,0:T(2,128)S(1)}, f32[2,32]{1,0:T(2,128)}, u32[]{:S(2)}) copy-start(f32[2,32]{1,0:T(2,128)} %param.27) | copy-start | bytes 772
  632.3 33.6 %all-to-all-start.8 = ((bf16[6,32,8,256]{3,2,0,1:T(8,128)(2,1)}), bf16[6,32,8,256]{3,2,0,1:T(8,128)(2,1)}, u32[]{:S(2)}, u32[]{:S(2)}) async-start(bf16[6,32,8,256]{3,2,0,1:T(8,128)(2,1)} %copy.79), calls=%async_computation.8 | async-start | bytes 1572864 | tf_op jit(solution)/shard_map/all_to_all | solution.py:905
  691.8 60.2 %all-to-all-start.9 = ((bf16[6,32,8,256]{3,2,0,1:T(8,128)(2,1)}), bf16[6,32,8,256]{3,2,0,1:T(8,128)(2,1)S(1)}, u32[]{:S(2)}, u32[]{:S(2)}) async-start(bf16[6,32,8,256]{3,2,0,1:T(8,128)(2,1)} %copy.81), calls=%async_computation.9 | async-start | bytes 1572864 | tf_op jit(solution)/shard_map/all_to_all | solution.py:920
  (36 other events, 200.8 us)
Sparse Core Ops, SparseCore 0:
  11.5 62.3 all-gather.3
  77.4 94.2 all-gather.7
  175.2 76.2 all-gather.5

commit v5 on v4

--- a/solution.py
+++ b/solution.py
@@ -29,10 +29,13 @@
 TN = (((0,), (0,)), ((), ()))
 MESH = pl.DeviceIdType.MESH
 VMEM_LIMIT = 48 * 2**20
-AHEAD = 4
+AHEAD = 8
 SKEW = 3
-PACE = 0.9
-DELAY = 1.0
+ORDERS = ((0, 2, 1, None), (0, 1, 2, None), (0, 2, None, 1))
+PACE = 3.7
+DELAY = 12.0
+GATHER_PACE = 10.0
+GATHER_DELAY = 20.0
 
 
 def shortened(shard):
@@ -75,189 +78,6 @@
         return scores
     position = start + lax.broadcasted_iota(jnp.int32, scores.shape, 0)
     return jnp.where(position < length, scores, neg_large)
-
-
-def attend_kernel(safe, chunk, length_ref, q_ref, k_ref, v_ref, o_ref, log_ref, vt_ref, s_ref):
-    seq_len = k_ref.shape[0]
-    length = length_ref[0]
-
-    @pl.when(pl.program_id(1) == 0)
-    def _():
-        vt_ref[...] = v_ref[...].T
-
-    outs = []
-    for head in range(2):
-        queries = one_head(q_ref[...], head) * bfloat16(HEAD**-0.5)
-        topmost = None
-        for at in range(0, seq_len, chunk):
-            scores = lax.dot_general(
-                k_ref[at : at + chunk, :], queries, NT, preferred_element_type=float32
-            )
-            scores = hide(scores, at, safe, length)
-            s_ref[head, at : at + chunk, :] = scores
-            top = jnp.max(scores, 0, keepdims=True)
-            topmost = top if topmost is None else jnp.maximum(topmost, top)
-        totals = jnp.zeros_like(topmost)
-        mixed = jnp.zeros((HEAD, q_ref.shape[0]), float32)
-        for at in range(0, seq_len, chunk):
-            expo = jnp.exp(s_ref[head, at : at + chunk, :] - topmost)
-            totals += jnp.sum(expo, 0, keepdims=True)
-            mixed += jnp.dot(
-                vt_ref[head * HEAD : (head + 1) * HEAD, at : at + chunk],
-                expo.astype(bfloat16),
-                preferred_element_type=float32,
-            )
-        outs.append(mixed * (1.0 / totals))
-        log_ref[0, head : head + 1, :] = topmost + jnp.log(totals)
-    o_ref[...] = jnp.concatenate(outs, 0).T.astype(bfloat16)
-
-
-def attend(lengths, scene, safe, rows=1024, chunk=512):
-    seq_len, width = scene.shape[0], scene.shape[1] // 3
-    pairs = width // PAIR
-    return pl.pallas_call(
-        partial(attend_kernel, safe, chunk),
-        grid=(pairs, seq_len // rows),
-        in_specs=[
-            pl.BlockSpec(memory_space=pltpu.SMEM),
-            pl.BlockSpec((rows, PAIR), lambda p, i: (i, p)),
-            pl.BlockSpec((seq_len, PAIR), lambda p, i: (0, pairs + p)),
-            pl.BlockSpec((seq_len, PAIR), lambda p, i: (0, 2 * pairs + p)),
-        ],
-        out_specs=[
-            pl.BlockSpec((rows, PAIR), lambda p, i: (i, p)),
-            pl.BlockSpec((1, 2, rows), lambda p, i: (p, 0, i)),
-        ],
-        out_shape=[
-            jax.ShapeDtypeStruct((seq_len, width), bfloat16),
-            jax.ShapeDtypeStruct((pairs, 2, seq_len), float32),
-        ],
-        scratch_shapes=[
-            pltpu.VMEM((PAIR, seq_len), bfloat16),
-            pltpu.VMEM((2, seq_len, rows), float32),
-        ],
-        compiler_params=pltpu.CompilerParams(vmem_limit_bytes=VMEM_LIMIT),
-        cost_estimate=pl.CostEstimate(
-            flops=4 * pairs * 2 * 4 * seq_len * seq_len * HEAD,
-            bytes_accessed=8 * seq_len * width,
-            transcendentals=0,
-        ),
-    )(lengths, scene, scene, scene)
-
-
-def attend_backward_kernel(safe, chunk, plan, slots, length_ref, q_ref, k_ref, v_ref, o_ref, do_ref, log_ref, *refs):
-    count = plan[4]
-    sources, out_ref, outs = refs[:count], refs[count], refs[count + 1 : 2 * count + 1]
-    kt_ref, dk_sum, dv_sum = refs[2 * count + 1 : 2 * count + 4]
-    peers, begin, finish, drain = reduce_steps(*plan[:4], sources, outs, refs[2 * count + 4 :])
-    total = len(plan[3])
-    seq_len = k_ref.shape[0]
-    length = length_ref[0]
-    step = pl.program_id(0)
-
-    def move(chunk, stage):
-        finish(chunk, stage)
-        if stage == 0 and chunk + AHEAD < total:
-            begin(chunk + AHEAD)
-
-    def move_at(head):
-        for at in range(head, len(slots) - 1, 2):
-            if slots[at]:
-
-                @pl.when(step == at // 2)
-                def _(at=at):
-                    for chunk, stage in slots[at]:
-                        move(chunk, stage)
-
-    @pl.when(step == 0)
-    def _():
-        greet(peers)
-        for chunk in range(min(AHEAD, total)):
-            begin(chunk)
-        kt_ref[...] = k_ref[...].T
-        dk_sum[...] = jnp.zeros_like(dk_sum)
-        dv_sum[...] = jnp.zeros_like(dv_sum)
-
-    products = (o_ref[...].astype(float32) * do_ref[...].astype(float32)).T
-    turned = []
-    for head in range(2):
-        move_at(head)
-        lanes = slice(head * HEAD, (head + 1) * HEAD)
-        queries = one_head(q_ref[...], head) * bfloat16(HEAD**-0.5)
-        d_mixed = one_head(do_ref[...], head)
-        inner = jnp.sum(products[lanes, :], 0, keepdims=True)
-        log_total = log_ref[0, head : head + 1, :]
-        d_queries = jnp.zeros((HEAD, q_ref.shape[0]), float32)
-        for at in range(0, seq_len, chunk):
-            part = slice(at, at + chunk)
-            scores = lax.dot_general(k_ref[part, :], queries, NT, preferred_element_type=float32)
-            probs = jnp.exp(hide(scores, at, safe, length) - log_total)
-            d_probs = lax.dot_general(v_ref[part, :], d_mixed, NT, preferred_element_type=float32)
-            dv_sum[part, :] += jnp.dot(
-                probs.astype(bfloat16), d_mixed, preferred_element_type=float32
-            )
-            d_scores = (probs * (d_probs - inner)).astype(bfloat16)
-            dk_sum[part, :] += jnp.dot(d_scores, queries, preferred_element_type=float32)
-            d_queries += jnp.dot(kt_ref[lanes, part], d_scores, preferred_element_type=float32)
-        turned.append(d_queries * HEAD**-0.5)
-    rows = q_ref.shape[0]
-    here = pl.ds(pl.multiple_of(step * rows, rows), rows)
-    out_ref[here, :PAIR] = jnp.concatenate(turned, 0).T.astype(bfloat16)
-
-    @pl.when(step == pl.num_programs(0) - 1)
-    def _():
-        out_ref[:, PAIR : 2 * PAIR] = dk_sum[...].astype(bfloat16)
-        out_ref[:, 2 * PAIR :] = dv_sum[...].astype(bfloat16)
-        for chunk, stage in slots[-1]:
-            move(chunk, stage)
-        drain()
-
-
-def attend_backward(
-    lengths, scene, mixed, d_mixed, log_totals, safe, parts, pieces, collective_id, rows=512, chunk=1024
-):
-    seq_len = scene.shape[0]
-    bits, narrow_bits, plans, chunks, halved, outs, scratch = reduce_plan(parts, pieces)
-    steps = seq_len // rows
-    slots = reduce_slots(len(chunks), bits, 2 * steps, PACE, DELAY)
-    tile = pl.BlockSpec((rows, PAIR), lambda i: (i, 0))
-    return pl.pallas_call(
-        partial(
-            attend_backward_kernel,
-            safe,
-            chunk,
-            (bits, narrow_bits, plans, chunks, len(parts)),
-            slots,
-        ),
-        grid=(steps,),
-        in_specs=[
-            pl.BlockSpec(memory_space=pltpu.SMEM),
-            tile,
-            pl.BlockSpec((seq_len, PAIR), lambda i: (0, 1)),
-            pl.BlockSpec((seq_len, PAIR), lambda i: (0, 2)),
-            tile,
-            tile,
-            pl.BlockSpec((1, 2, rows), lambda i: (0, 0, i)),
-        ]
-        + [pl.BlockSpec(memory_space=pl.ANY)] * len(parts),
-        out_specs=[pl.BlockSpec((seq_len, 3 * PAIR), lambda i: (0, 0))]
-        + [pl.BlockSpec(out.shape, lambda i: (0, 0)) for out in outs],
-        out_shape=[jax.ShapeDtypeStruct((seq_len, 3 * PAIR), bfloat16)] + outs,
-        scratch_shapes=[
-            pltpu.VMEM((PAIR, seq_len), bfloat16),
-            pltpu.VMEM((seq_len, PAIR), float32),
-            pltpu.VMEM((seq_len, PAIR), float32),
-        ]
-        + scratch,
-        compiler_params=pltpu.CompilerParams(
-            collective_id=collective_id, has_side_effects=True, vmem_limit_bytes=58 * 2**20
-        ),
-        cost_estimate=pl.CostEstimate(
-            flops=4 * 2 * 10 * seq_len * seq_len * HEAD,
-            bytes_accessed=16 * seq_len * PAIR,
-            transcendentals=0,
-        ),
-    )(lengths, scene, scene, scene, mixed, d_mixed, log_totals, *halved)
 
 
 def project_kernel(acts_ref, wq_ref, wk_ref, wv_ref, *out_refs):
@@ -444,10 +264,6 @@
     )(gram, turn)
 
 
-def exchange(groups):
-    return lax.all_to_all(groups, "narrow", split_axis=0, concat_axis=0, tiled=True)
-
-
 def partner(bit, narrow_bits):
     axis, step = ("narrow", 1 << bit) if bit < narrow_bits else ("wide", 1 << (bit - narrow_bits))
     place = lax.axis_index(axis)
@@ -570,7 +386,7 @@
     drain()
 
 
-def reduce_slots(chunks, bits, slots, pace, delay):
+def slot_table(chunks, bits, slots, pace, delay):
     table = [[] for _ in range(slots + 1)]
     done = sorted(
         (chunk * pace + (stage + 1) * delay, -stage, chunk, stage)
@@ -590,9 +406,9 @@
     for at, (shape, cut) in enumerate(zip(shapes, pieces)):
         rows = shape[0] // cut
         for row in range(0, shape[0], rows):
-            chunks.append((at, row, rows, len(chunks) % 2))
+            chunks.append((at, row, rows, len(chunks) % len(ORDERS)))
     later = tuple(range(3, bits))
-    plans = ((0, 2, 1) + later, (0, 1, 2) + later)
+    plans = tuple(tuple(b for part in order for b in (later if part is None else (part,))) for order in ORDERS)
     sizes = [bits - 1] + [bits - 1 - stage for stage in range(bits)]
     scratch = [
         pltpu.VMEM((2,) * size + shape, kind)
@@ -625,11 +441,9 @@
     )(*halved)
 
 
-def gather_kernel(bits, narrow_bits, plans, chunks, count, *refs):
-    sources, outs = refs[:count], refs[count : 2 * count]
-    own_sem, send_sem, recv_sem = refs[2 * count :]
+def gather_steps(bits, narrow_bits, plans, chunks, sources, outs, scratch):
+    own_sem, send_sem, recv_sem = scratch
     peers = [partner(b, narrow_bits) for b in range(bits)]
-    greet(peers)
     dims = list(reversed(range(bits)))
 
     def place(chunk, stage):
@@ -657,25 +471,42 @@
     def keep(chunk):
         return pltpu.make_async_copy(own(chunk), place(chunk, 0), own_sem.at[chunk])
 
+    def begin(chunk):
+        send(chunk, 0).start()
+        keep(chunk).start()
+
+    def finish(chunk, stage):
+        if stage == 0:
+            keep(chunk).wait()
+        send(chunk, stage).wait_recv()
+        if stage + 1 < bits:
+            send(chunk, stage + 1).start()
+
+    def drain():
+        for chunk in range(len(chunks)):
+            for stage in range(bits):
+                send(chunk, stage).wait_send()
+
+    return peers, begin, finish, drain
+
+
+def gather_kernel(bits, narrow_bits, plans, chunks, count, *refs):
+    peers, begin, finish, drain = gather_steps(
+        bits, narrow_bits, plans, chunks, refs[:count], refs[count : 2 * count], refs[2 * count :]
+    )
+    greet(peers)
     total = len(chunks)
     for chunk in range(total):
-        send(chunk, 0).start()
-        keep(chunk).start()
+        begin(chunk)
     for step in range(total + SKEW * bits):
         for stage in reversed(range(bits)):
             chunk = step - SKEW * stage
             if 0 <= chunk < total:
-                if stage == 0:
-                    keep(chunk).wait()
-                send(chunk, stage).wait_recv()
-                if stage + 1 < bits:
-                    send(chunk, stage + 1).start()
-    for chunk in range(total):
-        for stage in range(bits):
-            send(chunk, stage).wait_send()
-
-
-def gather_bands(parts, pieces, collective_id):
+                finish(chunk, stage)
+    drain()
+
+
+def gather_plan(parts, pieces):
     bits, narrow_bits = mesh_bits()
     chunks = []
     for at, (part, (cut, cut_cols)) in enumerate(zip(parts, pieces)):
@@ -686,19 +517,26 @@
     later = tuple(reversed(range(3, bits)))
     plans = (later + (1, 2, 0), later + (2, 1, 0))
     total = len(chunks)
+    outs = [
+        jax.ShapeDtypeStruct(part.shape[:1] + (2,) * bits + part.shape[1:], part.dtype)
+        for part in parts
+    ]
+    scratch = [
+        pltpu.SemaphoreType.DMA((total,)),
+        pltpu.SemaphoreType.DMA((total, bits)),
+        pltpu.SemaphoreType.DMA((total, bits)),
+    ]
+    return bits, narrow_bits, plans, tuple(chunks), outs, scratch
+
+
+def gather_bands(parts, pieces, collective_id):
+    bits, narrow_bits, plans, chunks, outs, scratch = gather_plan(parts, pieces)
     results = pl.pallas_call(
-        partial(gather_kernel, bits, narrow_bits, plans, tuple(chunks), len(parts)),
-        out_shape=[
-            jax.ShapeDtypeStruct(part.shape[:1] + (2,) * bits + part.shape[1:], part.dtype)
-            for part in parts
-        ],
+        partial(gather_kernel, bits, narrow_bits, plans, chunks, len(parts)),
+        out_shape=outs,
         in_specs=[pl.BlockSpec(memory_space=pl.ANY)] * len(parts),
         out_specs=[pl.BlockSpec(memory_space=pl.ANY)] * len(parts),
-        scratch_shapes=[
-            pltpu.SemaphoreType.DMA((total,)),
-            pltpu.SemaphoreType.DMA((total, bits)),
-            pltpu.SemaphoreType.DMA((total, bits)),
-        ],
+        scratch_shapes=scratch,
         compiler_params=pltpu.CompilerParams(collective_id=collective_id, has_side_effects=True),
         cost_estimate=pl.CostEstimate(flops=0, bytes_accessed=10**8, transcendentals=0),
     )(*parts)
@@ -706,6 +544,422 @@
         result.reshape(part.shape[:1] + (1 << bits,) + part.shape[1:])
         for result, part in zip(results, parts)
     ]
+
+
+def group_peers():
+    count = lax.axis_size("narrow")
+    me = lax.axis_index("narrow")
+    return me, [({"narrow": lax.rem(me + d, count)}, lax.rem(me + d, count)) for d in range(count)]
+
+
+def rows_at(place, rows):
+    return pl.ds(pl.multiple_of(place * rows, rows), rows)
+
+
+def attend_kernel(safe, chunk, halves, plan, slots, length_ref, *refs):
+    count = plan[4]
+    packed, sources = refs[:halves], refs[halves : halves + count]
+    refs = refs[halves + count :]
+    scenes_out, merged, mixed_out, log_ref = refs[:4]
+    scene_ref, o_ref, vt_ref, s_ref, near_sem, in_sem, back_sem, out_sem = refs[4 + count : 12 + count]
+    others, begin, finish, drain = gather_steps(
+        *plan[:4], sources, refs[4 : 4 + count], refs[12 + count :]
+    )
+    seq_len = scene_ref.shape[1]
+    me, peers = group_peers()
+    devices = len(peers)
+    tok_rows = seq_len // devices
+    length = length_ref[0]
+    half, step = pl.program_id(0), pl.program_id(1)
+    last = pl.num_programs(1) - 1
+    own = rows_at(me, tok_rows)
+
+    def bring(h, d):
+        device, place = peers[d]
+        if d == 0:
+            return pltpu.make_async_copy(packed[h].at[me], scene_ref.at[h, own], in_sem.at[h, 0])
+        return pltpu.make_async_remote_copy(
+            src_ref=packed[h].at[place],
+            dst_ref=scene_ref.at[h, own],
+            send_sem=near_sem.at[h, d],
+            recv_sem=in_sem.at[h, d],
+            device_id=device,
+            device_id_type=MESH,
+        )
+
+    def give(h, d, at, to, sender):
+        column = pl.ds(pl.multiple_of((sender * halves + h) * PAIR, PAIR), PAIR)
+        target = merged.at[:, column]
+        source = o_ref.at[h, rows_at(to, tok_rows)]
+        if d == 0:
+            return pltpu.make_async_copy(source, target, out_sem.at[h, 0])
+        return pltpu.make_async_remote_copy(
+            src_ref=source,
+            dst_ref=target,
+            send_sem=back_sem.at[h, d],
+            recv_sem=out_sem.at[h, d],
+            device_id={"narrow": to},
+            device_id_type=MESH,
+        )
+
+    def save_scene(h):
+        return pltpu.make_async_copy(scene_ref.at[h], scenes_out.at[h], near_sem.at[h, 0])
+
+    def save_mixed(h):
+        return pltpu.make_async_copy(o_ref.at[h], mixed_out.at[h], back_sem.at[h, 0])
+
+    @pl.when((half == 0) & (step == 0))
+    def _():
+        greet(peers[1:] + others[plan[1] :])
+        for d in range(devices):
+            bring(0, d).start()
+        for which in range(len(plan[3])):
+            begin(which)
+
+    for h in range(halves):
+
+        @pl.when((half == h) & (step == 0))
+        def _(h=h):
+            for d in range(devices):
+                if d:
+                    bring(h, d).wait_recv()
+                else:
+                    bring(h, d).wait()
+            if h + 1 < halves:
+                for d in range(devices):
+                    bring(h + 1, d).start()
+            save_scene(h).start()
+            vt_ref[...] = scene_ref[h, :, 2 * PAIR :].T
+
+    points = 2 * seq_len // chunk
+
+    def move_at(point):
+        for h in range(halves):
+            for s in range(devices):
+                todo = slots[(h * devices + s) * 2 * points + point]
+                if todo:
+
+                    @pl.when((half == h) & (step == s))
+                    def _(todo=todo):
+                        for which, stage in todo:
+                            finish(which, stage)
+
+    to = lax.rem(me + 1 + step, devices)
+    here = rows_at(to, tok_rows)
+    outs = []
+    for head in range(2):
+        queries = one_head(scene_ref[half, here, :PAIR], head) * bfloat16(HEAD**-0.5)
+        topmost = None
+        for at in range(0, seq_len, chunk):
+            move_at(head * points + at // chunk)
+            scores = lax.dot_general(
+                scene_ref[half, at : at + chunk, PAIR : 2 * PAIR],
+                queries,
+                NT,
+                preferred_element_type=float32,
+            )
+            scores = hide(scores, at, safe, length)
+            s_ref[head, at : at + chunk, :] = scores
+            top = jnp.max(scores, 0, keepdims=True)
+            topmost = top if topmost is None else jnp.maximum(topmost, top)
+        totals = jnp.zeros_like(topmost)
+        mixed = jnp.zeros((HEAD, tok_rows), float32)
+        for at in range(0, seq_len, chunk):
+            move_at(head * points + points // 2 + at // chunk)
+            expo = jnp.exp(s_ref[head, at : at + chunk, :] - topmost)
+            totals += jnp.sum(expo, 0, keepdims=True)
+            mixed += jnp.dot(
+                vt_ref[head * HEAD : (head + 1) * HEAD, at : at + chunk],
+                expo.astype(bfloat16),
+                preferred_element_type=float32,
+            )
+        outs.append(mixed * (1.0 / totals))
+        log_ref[half, head : head + 1, here] = topmost + jnp.log(totals)
+    o_ref[half, here, :] = jnp.concatenate(outs, 0).T.astype(bfloat16)
+
+    for h in range(halves):
+        for s in range(devices):
+
+            @pl.when((half == h) & (step == s))
+            def _(h=h, s=s):
+                d = (s + 1) % devices
+                give(h, d, s, lax.rem(me + d, devices), me).start()
+                if s == devices - 1:
+                    save_mixed(h).start()
+
+    @pl.when((half == halves - 1) & (step == last))
+    def _():
+        for which, stage in slots[-1]:
+            finish(which, stage)
+        drain()
+        for h in range(halves):
+            for d in range(devices):
+                if d:
+                    bring(h, d).wait_send()
+                    sender = lax.rem(me + devices - d, devices)
+                    arriving = give(h, d, d, lax.rem(me + d, devices), sender)
+                    arriving.wait_recv()
+                    arriving.wait_send()
+                else:
+                    give(h, 0, 0, me, me).wait()
+            save_scene(h).wait()
+            save_mixed(h).wait()
+
+
+def attend(lengths, packed, safe, parts, pieces, collective_id, chunk=512):
+    devices, tok_rows, _ = packed[0].shape
+    halves, seq_len = len(packed), devices * tok_rows
+    width = devices * halves * PAIR
+    anywhere = pl.BlockSpec(memory_space=pl.ANY)
+    bits, narrow_bits, plans, chunks, outs, scratch = gather_plan(parts, pieces)
+    slots = slot_table(
+        len(chunks), bits, halves * devices * 4 * (seq_len // chunk), GATHER_PACE, GATHER_DELAY
+    )
+    plan = (bits, narrow_bits, plans, chunks, len(parts))
+    results = pl.pallas_call(
+        partial(attend_kernel, safe, chunk, halves, plan, slots),
+        grid=(halves, devices),
+        in_specs=[pl.BlockSpec(memory_space=pltpu.SMEM)] + [anywhere] * (halves + len(parts)),
+        out_specs=[anywhere] * 3
+        + [pl.BlockSpec((halves, 2, seq_len), lambda p, i: (0, 0, 0))]
+        + [anywhere] * len(parts),
+        out_shape=[
+            jax.ShapeDtypeStruct((halves, seq_len, 3 * PAIR), bfloat16),
+            jax.ShapeDtypeStruct((tok_rows, width), bfloat16),
+            jax.ShapeDtypeStruct((halves, seq_len, PAIR), bfloat16),
+            jax.ShapeDtypeStruct((halves, 2, seq_len), float32),
+        ]
+        + outs,
+        scratch_shapes=[
+            pltpu.VMEM((halves, seq_len, 3 * PAIR), bfloat16),
+            pltpu.VMEM((halves, seq_len, PAIR), bfloat16),
+            pltpu.VMEM((PAIR, seq_len), bfloat16),
+            pltpu.VMEM((2, seq_len, tok_rows), float32),
+        ]
+        + [pltpu.SemaphoreType.DMA((halves, devices))] * 4
+        + scratch,
+        compiler_params=pltpu.CompilerParams(
+            collective_id=collective_id, has_side_effects=True, vmem_limit_bytes=VMEM_LIMIT
+        ),
+        cost_estimate=pl.CostEstimate(
+            flops=4 * halves * 2 * 4 * seq_len * seq_len * HEAD,
+            bytes_accessed=16 * seq_len * PAIR * halves,
+            transcendentals=0,
+        ),
+    )(lengths, *packed, *parts)
+    gathered = [
+        result.reshape(part.shape[0], 1 << bits, *part.shape[1:])
+        for result, part in zip(results[4:], parts)
+    ]
+    return list(results[:4]) + gathered
+
+
+def attend_backward_kernel(
+    safe, chunk, halves, plan, slots, length_ref, scene_ref, o_ref, log_ref, d_merged, *refs
+):
+    count = plan[4]
+    sources, packed_out, outs = refs[:count], refs[count], refs[count + 1 : 2 * count + 1]
+    do_ref, stage_ref, kt_ref, dk_sum, dv_sum = refs[2 * count + 1 : 2 * count + 6]
+    near_sem, in_sem, q_send, q_recv, kv_send, kv_recv = refs[2 * count + 6 : 2 * count + 12]
+    others, begin, finish, drain = reduce_steps(*plan[:4], sources, outs, refs[2 * count + 12 :])
+    total = len(plan[3])
+    me, peers = group_peers()
+    devices = len(peers)
+    seq_len = scene_ref.shape[1]
+    tok_rows = seq_len // devices
+    length = length_ref[0]
+    half, step = pl.program_id(0), pl.program_id(1)
+    own = rows_at(me, tok_rows)
+    chunks = seq_len // chunk
+
+    def move(which, stage):
+        finish(which, stage)
+        if stage == 0 and which + AHEAD < total:
+            begin(which + AHEAD)
+
+    def move_at(head, part):
+        for h in range(halves):
+            for s in range(devices):
+                todo = slots[((h * devices + s) * 2 + head) * chunks + part]
+                if todo:
+
+                    @pl.when((half == h) & (step == s))
+                    def _(todo=todo):
+                        for which, stage in todo:
+                            move(which, stage)
+
+    def bring(h, d):
+        device, place = peers[d]
+        column = pl.ds(pl.multiple_of((place * halves + h) * PAIR, PAIR), PAIR)
+        source, target = d_merged.at[:, column], do_ref.at[h, own]
+        if d == 0:
+            return pltpu.make_async_copy(source, target, in_sem.at[h, 0])
+        return pltpu.make_async_remote_copy(
+            src_ref=source,
+            dst_ref=target,
+            send_sem=near_sem.at[h, d],
+            recv_sem=in_sem.at[h, d],
+            device_id=device,
+            device_id_type=MESH,
+        )
+
+    def give(h, d, columns, send_sem, recv_sem, sender):
+        device, place = peers[d]
+        source = stage_ref.at[h, rows_at(place, tok_rows), columns]
+        target = packed_out.at[h, sender, :, columns]
+        if d == 0:
+            return pltpu.make_async_copy(source, target, recv_sem.at[h, 0])
+        return pltpu.make_async_remote_copy(
+            src_ref=source,
+            dst_ref=target,
+            send_sem=send_sem.at[h, d],
+            recv_sem=recv_sem.at[h, d],
+            device_id=device,
+            device_id_type=MESH,
+        )
+
+    q_columns, kv_columns = pl.ds(0, PAIR), pl.ds(PAIR, 2 * PAIR)
+
+    @pl.when((half == 0) & (step == 0))
+    def _():
+        narrow_bits = plan[1]
+        greet(peers[1:] + others[narrow_bits:])
+        for h in range(halves):
+            for d in range(devices):
+                bring(h, d).start()
+        for which in range(min(AHEAD, total)):
+            begin(which)
+
+    for h in range(halves):
+
+        @pl.when((half == h) & (step == 0))
+        def _(h=h):
+            kt_ref[...] = scene_ref[0, :, PAIR : 2 * PAIR].T
+            dk_sum[...] = jnp.zeros_like(dk_sum)
+            dv_sum[...] = jnp.zeros_like(dv_sum)
+            for d in range(devices):
+                if d:
+                    bring(h, d).wait_recv()
+                else:
+                    bring(h, d).wait()
+
+    here = rows_at(lax.rem(me + 1 + step, devices), tok_rows)
+    products = (o_ref[0, here, :].astype(float32) * do_ref[half, here, :].astype(float32)).T
+    turned = []
+    for head in range(2):
+        lanes = slice(head * HEAD, (head + 1) * HEAD)
+        queries = one_head(scene_ref[0, here, :PAIR], head) * bfloat16(HEAD**-0.5)
+        d_mixed = one_head(do_ref[half, here, :], head)
+        inner = jnp.sum(products[lanes, :], 0, keepdims=True)
+        log_total = log_ref[0, head : head + 1, here]
+        d_queries = jnp.zeros((HEAD, tok_rows), float32)
+        for index in range(chunks):
+            move_at(head, index)
+            at = index * chunk
+            part = slice(at, at + chunk)
+            scores = lax.dot_general(
+                scene_ref[0, part, PAIR : 2 * PAIR], queries, NT, preferred_element_type=float32
+            )
+            probs = jnp.exp(hide(scores, at, safe, length) - log_total)
+            d_probs = lax.dot_general(
+                scene_ref[0, part, 2 * PAIR :], d_mixed, NT, preferred_element_type=float32
+            )
+            dv_sum[part, :] += jnp.dot(
+                probs.astype(bfloat16), d_mixed, preferred_element_type=float32
+            )
+            d_scores = (probs * (d_probs - inner)).astype(bfloat16)
+            dk_sum[part, :] += jnp.dot(d_scores, queries, preferred_element_type=float32)
+            d_queries += jnp.dot(kt_ref[lanes, part], d_scores, preferred_element_type=float32)
+        turned.append(d_queries * HEAD**-0.5)
+    stage_ref[half, here, :PAIR] = jnp.concatenate(turned, 0).T.astype(bfloat16)
+
+    for h in range(halves):
+        for s in range(devices):
+
+            @pl.when((half == h) & (step == s))
+            def _(h=h, s=s):
+                give(h, (s + 1) % devices, q_columns, q_send, q_recv, me).start()
+                if s == devices - 1:
+                    stage_ref[h, :, PAIR : 2 * PAIR] = dk_sum[...].astype(bfloat16)
+                    stage_ref[h, :, 2 * PAIR :] = dv_sum[...].astype(bfloat16)
+                    for d in range(devices):
+                        give(h, d, kv_columns, kv_send, kv_recv, me).start()
+
+    @pl.when((half == halves - 1) & (step == devices - 1))
+    def _():
+        for which, stage in slots[-1]:
+            move(which, stage)
+        drain()
+        for h in range(halves):
+            for d in range(devices):
+                for columns, send_sem, recv_sem in (
+                    (q_columns, q_send, q_recv),
+                    (kv_columns, kv_send, kv_recv),
+                ):
+                    sender = lax.rem(me + devices - d, devices)
+                    copy = give(h, d, columns, send_sem, recv_sem, sender)
+                    if d:
+                        copy.wait_recv()
+                        copy.wait_send()
+                    else:
+                        copy.wait()
+                if d:
+                    bring(h, d).wait_send()
+
+
+def attend_backward(
+    lengths, scenes, mixed, d_merged, log_totals, safe, parts, pieces, collective_id, chunk=512
+):
+    halves, seq_len, _ = scenes.shape
+    devices = lax.axis_size("narrow")
+    tok_rows = seq_len // devices
+    bits, narrow_bits, plans, chunks, halved, outs, scratch = reduce_plan(parts, pieces)
+    slots = slot_table(
+        len(chunks), bits, halves * devices * 2 * (seq_len // chunk), PACE, DELAY
+    )
+    anywhere = pl.BlockSpec(memory_space=pl.ANY)
+
+    def of_half(array):
+        return pl.BlockSpec((1,) + array.shape[1:], lambda p, i: (p, 0, 0))
+
+    return pl.pallas_call(
+        partial(
+            attend_backward_kernel,
+            safe,
+            chunk,
+            halves,
+            (bits, narrow_bits, plans, chunks, len(parts)),
+            slots,
+        ),
+        grid=(halves, devices),
+        in_specs=[
+            pl.BlockSpec(memory_space=pltpu.SMEM),
+            of_half(scenes),
+            of_half(mixed),
+            of_half(log_totals),
+            anywhere,
+        ]
+        + [anywhere] * len(parts),
+        out_specs=[anywhere] + [pl.BlockSpec(out.shape, lambda p, i: (0, 0)) for out in outs],
+        out_shape=[jax.ShapeDtypeStruct((halves, devices, tok_rows, 3 * PAIR), bfloat16)] + outs,
+        scratch_shapes=[
+            pltpu.VMEM((halves, seq_len, PAIR), bfloat16),
+            pltpu.VMEM((halves, seq_len, 3 * PAIR), bfloat16),
+            pltpu.VMEM((PAIR, seq_len), bfloat16),
+            pltpu.VMEM((seq_len, PAIR), float32),
+            pltpu.VMEM((seq_len, PAIR), float32),
+        ]
+        + [pltpu.SemaphoreType.DMA((halves, devices))] * 6
+        + scratch,
+        compiler_params=pltpu.CompilerParams(
+            collective_id=collective_id, has_side_effects=True, vmem_limit_bytes=60 * 2**20
+        ),
+        cost_estimate=pl.CostEstimate(
+            flops=4 * halves * 2 * 10 * seq_len * seq_len * HEAD,
+            bytes_accessed=32 * seq_len * PAIR,
+            transcendentals=0,
+        ),
+    )(lengths, scenes, mixed, log_totals, d_merged, *halved)
 
 
 def total_kernel(bits, narrow_bits, own_ref, sum_ref, arrived, send_sem, recv_sem):
@@ -818,25 +1072,21 @@
     w_attn = w_attn.reshape(width, 3 * width)
     gain_pair = gain_pair[0, :, :2, :share].transpose(1, 0, 2).reshape(2, width)
     gain_pair = gain_pair.astype(jnp.float32)
-    w_proj, w_hidden, w_back = (
-        gathered.reshape(-1, gathered.shape[2])
-        for gathered in lax.all_gather(lowered[1:4], ("wide", "narrow"), axis=1, tiled=True)
+    w_proj, w_back = (
+        gathered.reshape(-1, width)
+        for gathered in lax.all_gather(lowered[1:4:2], ("wide", "narrow"), axis=1, tiled=True)
     )
     inputs = tokens.astype(jnp.float32)
     normed_one, inverse_one = normalize(inputs)
     act_one = (normed_one * gain_pair[0]).astype(jnp.bfloat16)
     head_width = width // narrow_count
     safe = seq_len - tok_rows
-    halves = head_width // PAIR
-    scenes = [
-        exchange(part).reshape(seq_len, 3 * PAIR)
-        for part in project(act_one, w_attn, narrow_count)
-    ]
-    attended = [attend(lengths, scene, safe) for scene in scenes]
-    merged = [exchange(o.reshape(narrow_count, tok_rows, PAIR)) for o, _ in attended]
-    merged = jnp.concatenate(
-        [merged[half][group] for group in range(narrow_count) for half in range(halves)], 1
-    )
+    packed = project(act_one, w_attn, narrow_count)
+    halves = len(packed)
+    scenes, merged, mixed, log_totals, w_hidden = attend(
+        lengths, packed, safe, (lowered[2],), ((4, 2),), 4
+    )
+    w_hidden = w_hidden.reshape(width, FF)
     middle = inputs + jnp.dot(merged, w_proj, preferred_element_type=jnp.float32)
     normed_two, inverse_two = normalize(middle)
     act_two = (normed_two * gain_pair[1]).astype(jnp.bfloat16)
@@ -859,19 +1109,11 @@
     d_merged = jnp.einsum("te,de->td", d_branch, w_proj, preferred_element_type=jnp.float32).astype(
         jnp.bfloat16
     )
-    d_mixed = d_merged.reshape(tok_rows, narrow_count, halves, PAIR).transpose(2, 1, 0, 3)
-    d_mixed = [exchange(d_mixed[half]).reshape(seq_len, PAIR) for half in range(halves)]
-    ready = (((d_w_hidden, d_proj), (8, 2)), ((d_back,), (8,)))
-    d_scenes, summed = [], []
-    for half in range(halves):
-        mixed, log_total = attended[half]
-        parts, cuts = ready[half]
-        d_scene, *sums = attend_backward(
-            lengths, scenes[half], mixed, d_mixed[half], log_total, safe, parts, cuts, 4 + half
-        )
-        d_scenes.append(d_scene)
-        summed.append(sums)
-    d_packed = [exchange(d.reshape(narrow_count, tok_rows, 3 * PAIR)) for d in d_scenes]
+    ready = (d_w_hidden, d_back, d_proj)
+    d_packed, hidden_sum, back_sum, proj_sum = attend_backward(
+        lengths, scenes, mixed, d_merged, log_totals, safe, ready, (8, 8, 2), 5
+    )
+    d_packed = [d_packed[half] for half in range(halves)]
     grouped = tuple(
         tuple((half, group, third * PAIR, PAIR) for half in range(halves))
         for third in range(3)
@@ -884,7 +1126,6 @@
     gain_parts = jnp.stack([d_gain_one, d_gain_two]).reshape(2, device_count, share)
     gain_parts = jnp.pad(gain_parts.transpose(1, 0, 2), ((0, 0), (0, 6), (0, 128 - share)))
     attn_sum, gain_grad = reduce_to_shards((d_attn, gain_parts), (6, 1), 1)
-    (hidden_sum, proj_sum), (back_sum,) = summed
     grad_shards = (attn_sum, proj_sum, hidden_sum, back_sum)
     gain_grad = gain_grad[:2, :share]
     band_rows = BLOCK // device_count

time: 772 us -> 693 us (0.90)
  waiting for transfers between devices: 75.6 us -> 0.06 us
  Pallas kernels: 496 us -> 549 us
  starting transfers between devices: 40.4 us -> 7.68 us
  local copies, waits for them, and re-layouts: 34.5 us -> 17.4 us
    all_to_all x8 -> x0, waiting for transfers between devices: 69.3 us -> none  [exchange(): lax.all_to_all(groups, 'narrow', split_axis=0, concat_axis=0, tiled=True)]
    pallas_call x5 -> x3, Pallas kernels: 297 us -> 343 us  [the longest x1 160 us: attend_backward(): pl.pallas_call(partial(attend_backward_kernel, safe, chunk, halves, (bits...]
    all_to_all x8 -> x0, starting transfers between devices: 33.4 us -> none  [exchange(): lax.all_to_all(groups, 'narrow', split_axis=0, concat_axis=0, tiled=True)]
    unnamed x97 -> x82, local copies, waits for them, and re-layouts: 16.9 us -> 4.57 us
  transfers between devices with their start and end apart: 13 -> 4, of which waited for: 5 -> 0; matrix products, arithmetic and copies ran while one was open for 8% -> 5% of each run, Pallas kernels for 53% -> 38%
where the time goes in v5:
time: 693 us; the launch traced here: 689 us
  Pallas kernels  549 us (79%)
  matrix products  65.3 us (9%)
  other arithmetic  28.6 us (4%)
  between operations  20.7 us (3%)
  local copies, waits for them, and re-layouts  17.4 us (3%)
  starting transfers between devices  7.68 us (1%)
    pallas_call x1, Pallas kernels, attend_backward(): pl.pallas_call(partial(attend_backward_kernel, safe, chunk, halves, (bits...  160 us
    pallas_call x1, Pallas kernels, attend(): pl.pallas_call(partial(attend_kernel, safe, chunk, halves, plan, slots),...  133 us
    pallas_call x1, Pallas kernels, renew_bases(): pl.pallas_call(partial(renew_kernel, rows), out_shape=jax.ShapeDtypeStruc...  54.8 us
    pallas_call x1, Pallas kernels, reduce_to_shards(): pl.pallas_call(partial(reduce_kernel, bits, narrow_bits, plans, chunks, l...  51.3 us
    pallas_call x1, Pallas kernels, gather_bands(): pl.pallas_call(partial(gather_kernel, bits, narrow_bits, plans, chunks, l...  49.5 us
    pallas_call x4, Pallas kernels, weight_grad(): pl.pallas_call(partial(weight_grad_kernel, columns, band_rows), grid=(ban...  40 us
    pallas_call x1, Pallas kernels, soap_update(): pl.pallas_call(soap_kernel, grid=(slots,), in_specs=[pl.BlockSpec(memory_...  23.8 us
    dot_general x1, matrix products, body(): hidden = jnp.dot(act_two, w_hidden, preferred_element_type=jnp.float32)  19.2 us
  transfers between devices with their start and end apart: 4, of which 0 were waited for; matrix products, arithmetic and copies ran while one was open for 5% of the time, Pallas kernels for 38%

profile of v5, /device:TPU:0, one launch (start us, length us, event | category | flops | bytes accessed | tf_op | source)
XLA Modules:
  0.0 688.6 jit_solution(17258795862060391967)
XLA Ops:
  13.7 49.5 %shard_map.288 = (bf16[4,2,2,2,2,2,8,3072]{7,6,5,4,3,2,1,0:T(8,128)(2,1)}, bf16[1,2,2,2,2,2,8,128]{7,6,5,4,3,2,1,0:T(8,128)(2,1)}) custom-call(bf16[4,8,3072]{2,1,0:T(8,128)(2,1)} %convert_element_type.70.refs_0_, bf16[1,8,128]{2,1,0:T(8,128)(2,1)} %pad_bitcast_fusion.refs_1_), custom_call_target="tpu_custom_call" | custom-call | bytes 100000000 | tf_op jit(solution)/shard_map/pallas_call | solution.py:534
  69.6 8.6 %shard_map.289 = (bf16[4,768,384]{2,1,0:T(8,128)(2,1)S(1)}, bf16[4,768,384]{2,1,0:T(8,128)(2,1)}) custom-call(bf16[768,1024]{1,0:T(8,128)(2,1)S(1)} %fusion.13.acts_ref.left_ref, bf16[1024,3072]{1,0:T(8,128)(2,1)} %bitcast.93, bf16[1024,3072]{1,0:T(8,128)(2,1)} %bitcast.94, bf16[1024,3072]{1,0:T(8,128)(2,1)} %bitcast.95), custom_call_target="tpu_custom_call" | custom-call | flops 4831838208 | bytes 12582912 | tf_op jit(solution)/shard_map/pallas_call | solution.py:102
  78.2 133.5 %shard_map.290 = (bf16[2,3072,384]{2,1,0:T(8,128)(2,1)}, bf16[768,1024]{1,0:T(8,128)(2,1)S(1)}, bf16[2,3072,128]{2,1,0:T(8,128)(2,1)S(1)}, f32[2,2,3072]{2,1,0:T...) custom-call(s32[1]{0:T(128)S(6)} %copy.100.length_ref, bf16[4,768,384]{2,1,0:T(8,128)(2,1)S(1)} %get-tuple-element.40.refs_0_, ...), custom_call_target="tpu_custom_call" | custom-call | flops 38654705664 | bytes 12582912 | tf_op jit(solution)/shard_map/pallas_call | solution.py:719
  213.5 4.0 fusion.43
  220.0 13.0 %fusion.44 = f32[768,4096]{1,0:T(8,128)} fusion(bf16[768,1024]{1,0:T(8,128)(2,1)S(1)} %copy-done.3, bf16[4096,1024]{1,0:T(8,128)(2,1)} %bitcast.109), kind=kOutput, calls=%fused_computation.93 | convolution fusion | flops 6442450944 | bytes 22544384 | tf_op jit(solution)/shard_map/td,fd->tf/dot_general | solution.py:1100
  233.0 19.2 %fusion.6 = (bf16[768,4096]{1,0:T(8,128)(2,1)S(1)}, bf16[768,4096]{1,0:T(8,128)(2,1)}) fusion(f32[768,4096]{1,0:T(8,128)} %fusion.44, bf16[768,1024]{1,0:T(8,128)(2,1)S(1)} %multiply_convert_fusion.1.left_ref, bf16[1024,4096]{1,0:T(8,128)(2,1)} %bitcast.113), kind=kOutput, calls=%fused_computation.8 | convolution fusion | flops 6511656960 | bytes 35127296 | tf_op jit(solution)/shard_map/dot_general | solution.py:1093
  252.2 12.1 %multiply_reduce_fusion = (f32[1024]{0:T(1024)S(1)}, f32[768]{0:T(1024)S(1)}, f32[768]{0:T(1024)S(1)}, f32[768,1024]{1,0:T(8,128)S(1)}) fusion(f32[768,1024]{1,0:T(8,128)S(1)} %copy-done.15, f32[768]{0:T(1024)S(1)} %add_rsqrt_fusion, f32[768]{0:T(1024)S(1)} %broadcast_multiply_fusion.4, f32[1024]{0:T(1024)S(1)} %mul.238, ...), kind=kOutput, calls=%fused_computation.27 | convolution fusion | flops 6448739328 | bytes 20992000 | tf_op jit(solution)/shard_map/tf,df->td/dot_general | solution.py:1104
  265.7 2.8 shard_map.293
  268.5 12.5 %shard_map.291 = bf16[32,512,256]{2,1,0:T(8,128)(2,1)} custom-call(bf16[768,1024]{1,0:T(8,128)(2,1)S(1)} %multiply_convert_fusion.1.left_ref, bf16[1,768,4096]{2,1,0:T(8,128)(2,1)} %bitcast.117), custom_call_target="tpu_custom_call" | custom-call | flops 6442450944 | bytes 16252928 | tf_op jit(solution)/shard_map/pallas_call | solution.py:1023
  281.0 3.0 convolution_convert_fusion.d_merged
  283.9 15.8 %shard_map.292 = bf16[32,512,256]{2,1,0:T(8,128)(2,1)} custom-call(bf16[768,4096]{1,0:T(8,128)(2,1)} %get-tuple-element.74.left_ref, bf16[1,768,1024]{2,1,0:T(8,128)(2,1)S(1)} %bitcast.89), custom_call_target="tpu_custom_call" | custom-call | flops 6442450944 | bytes 16252928 | tf_op jit(solution)/shard_map/pallas_call | solution.py:1023
  299.7 159.8 %shard_map.294 = (bf16[2,4,768,384]{3,2,1,0:T(8,128)(2,1)}, f32[512,256]{1,0:T(8,128)}, f32[512,256]{1,0:T(8,128)}, f32[128,256]{1,0:T(8,128)}) custom-call(s32[1]{0:T(128)S(6)} %copy.100.length_ref, bf16[2,3072,384]{2,1,0:T(8,128)(2,1)} %get-tuple-element.44.scene_ref, bf16[2,3072,128]{2,1,0:T(8,128)(2,1)} %copy-done.9, f32[2,2,3072]{2,1,0:T(2,128)} %copy-done.10, ...), custom_call_target="tpu_custom_call" | custom-call | flops 96636764160 | bytes 12582912 | tf_op jit(solution)/shard_map/pallas_call | solution.py:925
  459.6 2.9 slice_bitcast_fusion
  462.4 10.8 %shard_map.295 = f32[768,1024]{1,0:T(8,128)} custom-call(bf16[4,768,384]{2,1,0:T(8,128)(2,1)S(1)} %get-tuple-element.76.refs_0_, bf16[4,768,384]{2,1,0:T(8,128)(2,1)S(1)} %get-tuple-element.75.refs_1_, bf16[1024,3072]{1,0:T(8,128)(2,1)} %bitcast.96, bf16[1024,3072]{1,0:T(8,128)(2,1)} %bitcast.97, bf16[1024,3072]{1,0:T(8,128)(2,1)} %bitcast.98), custom_call_target="tpu_custom_call" | custom-call | flops 4831838208 | bytes 14155776 | tf_op jit(solution)/shard_map/pallas_call | solution.py:142
  473.3 8.9 %shard_map.296 = bf16[32,384,256]{2,1,0:T(8,128)(2,1)} custom-call(bf16[768,1024]{1,0:T(8,128)(2,1)S(1)} %copy-done.2, bf16[4,768,384]{2,1,0:T(8,128)(2,1)S(1)} %get-tuple-element.76.refs_0_, bf16[4,768,384]{2,1,0:T(8,128)(2,1)} %copy-done), custom_call_target="tpu_custom_call" | custom-call | flops 4831838208 | bytes 12582912 | tf_op jit(solution)/shard_map/pallas_call | solution.py:1023
  484.4 51.3 %shard_map.297 = (f32[384,256]{1,0:T(8,128)}, f32[8,128]{1,0:T(8,128)}) custom-call(bf16[2,2,2,2,2,384,256]{6,5,4,3,2,1,0:T(8,128)(2,1)} %bitcast.99, f32[2,2,2,2,2,8,128]{6,5,4,3,2,1,0:T(8,128)} %bitcast.105), custom_call_target="tpu_custom_call" | custom-call | flops 100000000 | bytes 400000000 | tf_op jit(solution)/shard_map/pallas_call | solution.py:431
  543.4 3.8 all-to-all-start
  551.6 16.9 %shard_map.298 = f32[8,128]{1,0:T(8,128)} custom-call(f32[8,128]{1,0:T(8,128)} %broadcast_in_dim.14.own_ref), custom_call_target="tpu_custom_call" | custom-call | tf_op jit(solution)/shard_map/pallas_call | solution.py:986
  570.5 4.5 fusion.18
  575.6 12.2 %add_convert_fusion = bf16[768,1024]{1,0:T(8,128)(2,1)} fusion(f32[768,1024]{1,0:T(8,128)S(1)} %copy-done.16, bf16[768,4096]{1,0:T(8,128)(2,1)} %get-tuple-element.74.left_ref, bf16[4096,1024]{1,0:T(8,128)(2,1)} %bitcast.110), kind=kOutput, calls=%fused_computation.30 | convolution fusion | flops 6444023808 | bytes 19398656 | tf_op jit(solution)/shard_map/dot_general | solution.py:1095
  589.0 23.8 %shard_map.299 = (bf16[6,256,256]{2,1,0:T(8,128)(2,1)S(1)}, f32[6,256,256]{2,1,0:T(8,128)}, f32[6,256,256]{2,1,0:T(8,128)}, f32[6,256,256]{2,1,0:T(8,128)}, f32[...) custom-call(f32[1,1]{1,0:T(1,128)} %bitcast.22.factor_ref, ...), custom_call_target="tpu_custom_call" | custom-call | flops 12079595520 | bytes 23592960 | tf_op jit(solution)/shard_map/pallas_call | solution.py:191
  613.8 3.8 all-to-all-start.1
  617.7 54.8 %shard_map.300 = f32[12,256,256]{2,1,0:T(8,128)S(1)} custom-call(f32[12,256,256]{2,1,0:T(8,128)} %bitcast.118, f32[12,256,256]{2,1,0:T(8,128)} %bitcast.119), custom_call_target="tpu_custom_call" | custom-call | flops 40265318400 | bytes 9437184 | tf_op jit(solution)/shard_map/pallas_call | solution.py:251
  672.4 1.9 slice_bitcast_fusion.2
  (150 shorter events, 38.8 us)
Async XLA Ops:
  7.2 60.7 %copy-start.33 = (s32[192]{0:T(256)S(1)}, s32[192]{0:T(256)}, u32[]{:S(2)}) copy-start(s32[192]{0:T(256)} %param.20) | copy-start | bytes 2308
  7.2 60.4 %copy-start.11 = (bf16[768,1024]{1,0:T(8,128)(2,1)S(1)}, bf16[768,1024]{1,0:T(8,128)(2,1)}, u32[]{:S(2)}) copy-start(bf16[768,1024]{1,0:T(8,128)(2,1)} %param.17) | copy-start | bytes 4718596
  7.2 206.2 %all-gather.3.cloned.1.call-start = ((), (), s32[]{:S(2)}) async-start(), calls=%async_computation.2 | async-start | bytes 2162688 | tf_op jit(solution)/shard_map/all_gather | solution.py:1077
  8.9 210.7 %all-gather.5.cloned.1.call-start = ((), (), s32[]{:S(2)}) async-start(), calls=%async_computation.3 | async-start | bytes 8650752 | tf_op jit(solution)/shard_map/all_gather | solution.py:1077
  69.6 8.6 %copy-start.1 = (bf16[768,1024]{1,0:T(8,128)(2,1)}, bf16[768,1024]{1,0:T(8,128)(2,1)S(1)}, u32[]{:S(2)}) copy-start(bf16[768,1024]{1,0:T(8,128)(2,1)S(1)} %fusion.13.acts_ref.left_ref) | copy-start | bytes 4718596
  233.0 19.2 %copy-start.15 = (f32[768,1024]{1,0:T(8,128)S(1)}, f32[768,1024]{1,0:T(8,128)}, u32[]{:S(2)}) copy-start(f32[768,1024]{1,0:T(8,128)} %copy-done.14) | copy-start | bytes 9437188
  252.2 12.1 %copy-start.40 = (bf16[768,4096]{1,0:T(8,128)(2,1)}, bf16[768,4096]{1,0:T(8,128)(2,1)S(1)}, u32[]{:S(2)}) copy-start(bf16[768,4096]{1,0:T(8,128)(2,1)S(1)} %get-tuple-element.73) | copy-start | bytes 18874372
  265.6 15.3 %copy-start.17 = (f32[768,1024]{1,0:T(8,128)}, f32[768,1024]{1,0:T(8,128)S(1)}, u32[]{:S(2)}) copy-start(f32[768,1024]{1,0:T(8,128)S(1)} %get-tuple-element.72) | copy-start | bytes 9437188
  268.5 12.5 %copy-start.6 = (bf16[32,128,256]{2,1,0:T(8,128)(2,1)}, bf16[32,128,256]{2,1,0:T(8,128)(2,1)S(1)}, u32[]{:S(2)}) copy-start(bf16[32,128,256]{2,1,0:T(8,128)(2,1)S(1)} %shard_map.293) | copy-start | bytes 6291460
  268.5 12.5 %copy-start.39 = (bf16[4,256,1024]{2,1,0:T(8,128)(2,1)S(1)}, bf16[4,256,1024]{2,1,0:T(8,128)(2,1)}, u32[]{:S(2)}) copy-start(bf16[4,256,1024]{2,1,0:T(8,128)(2,1)} %all-gather.3.cloned.1.call-done) | copy-start | bytes 6291460
  462.4 10.8 %copy-start = (bf16[4,768,384]{2,1,0:T(8,128)(2,1)}, bf16[4,768,384]{2,1,0:T(8,128)(2,1)S(1)}, u32[]{:S(2)}) copy-start(bf16[4,768,384]{2,1,0:T(8,128)(2,1)S(1)} %get-tuple-element.75.refs_1_) | copy-start | bytes 7077892
  462.4 10.8 %copy-start.2 = (bf16[768,1024]{1,0:T(8,128)(2,1)S(1)}, bf16[768,1024]{1,0:T(8,128)(2,1)}, u32[]{:S(2)}) copy-start(bf16[768,1024]{1,0:T(8,128)(2,1)} %copy-done.1) | copy-start | bytes 4718596
  473.3 9.0 %copy-start.12 = (bf16[768,1024]{1,0:T(8,128)(2,1)S(1)}, bf16[768,1024]{1,0:T(8,128)(2,1)}, u32[]{:S(2)}) copy-start(bf16[768,1024]{1,0:T(8,128)(2,1)} %param.17) | copy-start | bytes 4718596
  473.3 9.0 %copy-start.13 = (f32[768,1024]{1,0:T(8,128)S(1)}, f32[768,1024]{1,0:T(8,128)}, u32[]{:S(2)}) copy-start(f32[768,1024]{1,0:T(8,128)} %shard_map.295) | copy-start | bytes 9437188
  473.3 9.0 %copy-start.27 = (f32[768]{0:T(1024)S(1)}, f32[768]{0:T(1024)}, u32[]{:S(2)}) copy-start(f32[768]{0:T(1024)} %copy-done.26) | copy-start | bytes 9220
  473.3 9.0 %copy-start.29 = (f32[1024]{0:T(1024)S(1)}, f32[1024]{0:T(1024)}, u32[]{:S(2)}) copy-start(f32[1024]{0:T(1024)} %copy-done.28) | copy-start | bytes 12292
  473.3 9.0 %copy-start.31 = (f32[768]{0:T(1024)S(1)}, f32[768]{0:T(1024)}, u32[]{:S(2)}) copy-start(f32[768]{0:T(1024)} %copy-done.30) | copy-start | bytes 9220
  484.4 53.1 %copy-start.25 = (f32[128,256]{1,0:T(8,128)S(1)}, f32[128,256]{1,0:T(8,128)}, u32[]{:S(2)}) copy-start(f32[128,256]{1,0:T(8,128)} %get-tuple-element.50) | copy-start | bytes 393220
  484.4 53.7 %copy-start.21 = (f32[512,256]{1,0:T(8,128)S(1)}, f32[512,256]{1,0:T(8,128)}, u32[]{:S(2)}) copy-start(f32[512,256]{1,0:T(8,128)} %get-tuple-element.51) | copy-start | bytes 1572868
  484.4 54.4 %copy-start.20 = (f32[512,256]{1,0:T(8,128)S(1)}, f32[512,256]{1,0:T(8,128)}, u32[]{:S(2)}) copy-start(f32[512,256]{1,0:T(8,128)} %get-tuple-element.52) | copy-start | bytes 1572868
  543.4 44.4 %all-to-all-start = ((bf16[6,32,8,256]{3,2,0,1:T(8,128)(2,1)}), bf16[6,32,8,256]{3,2,0,1:T(8,128)(2,1)}, u32[]{:S(2)}, u32[]{:S(2)}) async-start(bf16[6,32,8,256]{3,2,0,1:T(8,128)(2,1)} %copy.74), calls=%async_computation | async-start | bytes 1572864 | tf_op jit(solution)/shard_map/all_to_all | solution.py:1146
  575.6 13.4 %copy-start.4 = (f32[6,256,256]{2,1,0:T(8,128)S(1)}, f32[6,256,256]{2,1,0:T(8,128)}, u32[]{:S(2)}) copy-start(f32[6,256,256]{2,1,0:T(8,128)} %first_ref.1) | copy-start | bytes 4718596
  575.6 13.4 %copy-start.5 = (f32[6,256,256]{2,1,0:T(8,128)S(1)}, f32[6,256,256]{2,1,0:T(8,128)}, u32[]{:S(2)}) copy-start(f32[6,256,256]{2,1,0:T(8,128)} %second_ref.1) | copy-start | bytes 4718596
  613.8 60.5 %all-to-all-start.1 = ((bf16[6,32,8,256]{3,2,0,1:T(8,128)(2,1)}), bf16[6,32,8,256]{3,2,0,1:T(8,128)(2,1)S(1)}, u32[]{:S(2)}, u32[]{:S(2)}) async-start(bf16[6,32,8,256]{3,2,0,1:T(8,128)(2,1)} %copy.76), calls=%async_computation.1 | async-start | bytes 1572864 | tf_op jit(solution)/shard_map/all_to_all | solution.py:1161
  (23 other events, 71.0 us)
Sparse Core Ops, SparseCore 0:
  11.5 62.9 all-gather.2
  78.1 96.3 all-gather.4

commit v6 on v5

--- a/solution.py
+++ b/solution.py
@@ -34,8 +34,10 @@
 ORDERS = ((0, 2, 1, None), (0, 1, 2, None), (0, 2, None, 1))
 PACE = 3.7
 DELAY = 12.0
-GATHER_PACE = 10.0
-GATHER_DELAY = 20.0
+GATHER_PACE = 6.0
+GATHER_DELAY = 30.0
+GELU = 0.7978845608
+CUBIC = 0.044715
 
 
 def shortened(shard):
@@ -57,15 +59,6 @@
         - normed * jnp.mean(scaled * normed, -1, keepdims=True)
     )
     return (d_input, d_gain)
-
-
-def from_pieces(pieces, band_count, col_count):
-    band_rows = pieces.shape[1]
-    return (
-        pieces.reshape(band_count, col_count // BLOCK, band_rows, BLOCK)
-        .transpose(0, 2, 1, 3)
-        .reshape(band_count, band_rows, col_count)
-    )
 
 
 def one_head(matrix, head):
@@ -962,39 +955,240 @@
     )(lengths, scenes, mixed, log_totals, d_merged, *halved)
 
 
-def total_kernel(bits, narrow_bits, own_ref, sum_ref, arrived, send_sem, recv_sem):
-    peers = [partner(b, narrow_bits) for b in range(bits)]
-    greet(peers)
-    sum_ref[...] = own_ref[...]
-    for stage in range(bits):
-        copy = pltpu.make_async_remote_copy(
-            src_ref=sum_ref,
-            dst_ref=arrived.at[stage],
-            send_sem=send_sem.at[stage],
-            recv_sem=recv_sem.at[stage],
-            device_id=peers[stage][0],
+def feed_kernel(deal, acts_ref, grad_ref, middle_ref, up_ref, down_ref, out_ref, back_ref, one_ref, two_ref, turned_ref, sum_ref):
+    at, last = pl.program_id(0), pl.num_programs(0) - 1
+
+    @pl.when(at == 0)
+    def _():
+        sum_ref[...] = middle_ref[...]
+        back_ref[...] = jnp.zeros_like(back_ref)
+        turned_ref[...] = acts_ref[...].T
+
+    acts, grad = acts_ref[...], grad_ref[...]
+    hidden = jnp.dot(acts, up_ref[...], preferred_element_type=float32)
+    square = hidden * hidden
+    bend = jnp.tanh(GELU * hidden * (1.0 + CUBIC * square))
+    share = 0.5 + 0.5 * bend
+    active = (hidden * share).astype(bfloat16)
+    slope = share + hidden * (0.5 - 0.5 * bend * bend) * (GELU + 3.0 * GELU * CUBIC * square)
+    d_active = lax.dot_general(grad, down_ref[...], NT, preferred_element_type=float32)
+    d_hidden = (d_active * slope).astype(bfloat16)
+    sum_ref[...] += jnp.dot(active, down_ref[...], preferred_element_type=float32)
+    back_ref[...] += lax.dot_general(d_hidden, up_ref[...], NT, preferred_element_type=float32)
+    if deal:
+        rows = BLOCK // one_ref.shape[0]
+        d_up = jnp.dot(turned_ref[...], d_hidden, preferred_element_type=float32)
+        d_up = d_up.astype(bfloat16)
+        d_down = jnp.dot(active.T, grad, preferred_element_type=float32).astype(bfloat16)
+        for band in range(d_up.shape[0] // BLOCK):
+            blocks = [
+                d_up[band * BLOCK : (band + 1) * BLOCK, start : start + BLOCK].reshape(-1, rows, BLOCK)
+                for start in range(0, d_up.shape[1], BLOCK)
+            ]
+            one_ref[:, band] = jnp.concatenate(blocks, 1)
+        blocks = [
+            d_down[low : low + BLOCK, start : start + BLOCK].reshape(-1, rows, BLOCK)
+            for low in range(0, d_down.shape[0], BLOCK)
+            for start in range(0, d_down.shape[1], BLOCK)
+        ]
+        two_ref[...] = jnp.concatenate(blocks, 1)
+    else:
+        one_ref[...] = active
+        two_ref[...] = d_hidden
+
+    @pl.when(at == last)
+    def _():
+        out_ref[...] = sum_ref[...].astype(bfloat16)
+
+
+def feed_forward(acts, grad, middle, w_up, w_down, device_count, tile=2 * BLOCK):
+    tok_rows, width = acts.shape
+    hidden = w_up.shape[1]
+    rows = BLOCK // device_count
+    deal = rows % 8 == 0
+    full = pl.BlockSpec((tok_rows, width), lambda j: (0, 0))
+    if deal:
+        bands, blocks = width // BLOCK, hidden // BLOCK
+        kinds = [(device_count, bands, blocks * rows, BLOCK), (device_count, blocks * bands * rows, BLOCK)]
+        part = tile // BLOCK * rows
+        specs = [
+            pl.BlockSpec((device_count, bands, part, BLOCK), lambda j: (0, 0, j, 0)),
+            pl.BlockSpec((device_count, bands * part, BLOCK), lambda j: (0, j, 0)),
+        ]
+    else:
+        kinds = [(tok_rows, hidden)] * 2
+        specs = [pl.BlockSpec((tok_rows, tile), lambda j: (0, j))] * 2
+    out, back, one, two = pl.pallas_call(
+        partial(feed_kernel, deal),
+        grid=(hidden // tile,),
+        in_specs=[full, full, full]
+        + [
+            pl.BlockSpec((width, tile), lambda j: (0, j)),
+            pl.BlockSpec((tile, width), lambda j: (j, 0)),
+        ],
+        out_specs=[full, full] + specs,
+        out_shape=[
+            jax.ShapeDtypeStruct((tok_rows, width), bfloat16),
+            jax.ShapeDtypeStruct((tok_rows, width), float32),
+        ]
+        + [jax.ShapeDtypeStruct(kind, bfloat16) for kind in kinds],
+        scratch_shapes=[pltpu.VMEM((width, tok_rows), bfloat16), pltpu.VMEM((tok_rows, width), float32)],
+        compiler_params=pltpu.CompilerParams(vmem_limit_bytes=58 * 2**20),
+        cost_estimate=pl.CostEstimate(
+            flops=12 * tok_rows * width * hidden, bytes_accessed=8 * width * hidden, transcendentals=0
+        ),
+    )(acts, grad, middle, w_up, w_down)
+    if deal:
+        return out, back, one.reshape(device_count, -1, BLOCK), two
+    columns = lambda size: tuple(((0, 0, start, BLOCK),) for start in range(0, size, BLOCK))
+    return (
+        out,
+        back,
+        weight_grad(acts, [two[None]], columns(hidden), device_count),
+        weight_grad(one, [grad[None]], columns(width), device_count),
+    )
+
+
+def ship_kernel(narrow_count, held_ref, *refs):
+    shards, gain_ref = refs[:4], refs[4]
+    arrived, total_ref = refs[5:7]
+    pieces, outgoing, squares, send_sem, recv_sem, tile_send, tile_recv = refs[7:]
+    devices, slots = outgoing.shape[:2]
+    me = lax.axis_index("wide") * narrow_count + lax.axis_index("narrow")
+
+    def device(d):
+        place = lax.rem(me + d, devices)
+        return place, {"wide": place // narrow_count, "narrow": lax.rem(place, narrow_count)}
+
+    barrier = pltpu.get_barrier_semaphore()
+
+    def announce(d, carry):
+        pl.semaphore_signal(barrier, inc=1, device_id=device(d)[1], device_id_type=MESH)
+        return carry
+
+    lax.fori_loop(1, devices, announce, 0)
+    at, own = 0, jnp.sum(gain_ref[...] * gain_ref[...])
+    for shard in shards:
+        values = shard[...]
+        own += jnp.sum(values * values)
+        pieces[at : at + values.shape[0]] = values
+        at += values.shape[0]
+    squares[me] = jnp.full(squares.shape[1:], own, float32)
+
+    def pack(place, carry):
+        for slot in range(slots):
+            block = held_ref[place * slots + slot]
+            piece = pieces[jnp.maximum(block, 0)]
+            outgoing[place, slot] = jnp.where(block >= 0, piece, 0.0).astype(bfloat16)
+        return carry
+
+    lax.fori_loop(0, devices, pack, 0)
+    pl.semaphore_wait(barrier, devices - 1)
+
+    def copies(d):
+        place, target = device(d)
+        return (
+            pltpu.make_async_remote_copy(
+                src_ref=outgoing.at[place],
+                dst_ref=arrived.at[:, me],
+                send_sem=send_sem.at[d],
+                recv_sem=recv_sem.at[d],
+                device_id=target,
+                device_id_type=MESH,
+            ),
+            pltpu.make_async_remote_copy(
+                src_ref=squares.at[me],
+                dst_ref=squares.at[me],
+                send_sem=tile_send.at[d],
+                recv_sem=tile_recv.at[d],
+                device_id=target,
+                device_id_type=MESH,
+            ),
+        )
+
+    def start(d, carry):
+        for copy in copies(d):
+            copy.start()
+        return carry
+
+    lax.fori_loop(1, devices, start, 0)
+    arrived[:, me] = outgoing[me]
+
+    def arrive(d, carry):
+        sender = lax.rem(me + devices - d, devices)
+        pltpu.make_async_remote_copy(
+            src_ref=outgoing.at[sender],
+            dst_ref=arrived.at[:, sender],
+            send_sem=send_sem.at[d],
+            recv_sem=recv_sem.at[d],
+            device_id=device(d)[1],
             device_id_type=MESH,
-        )
-        copy.start()
-        copy.wait()
-        sum_ref[...] = sum_ref[...] + arrived[stage]
-
-
-def total_of(value, collective_id):
-    bits, narrow_bits = mesh_bits()
+        ).wait_recv()
+        pltpu.make_async_remote_copy(
+            src_ref=squares.at[sender],
+            dst_ref=squares.at[sender],
+            send_sem=tile_send.at[d],
+            recv_sem=tile_recv.at[d],
+            device_id=device(d)[1],
+            device_id_type=MESH,
+        ).wait_recv()
+        for copy in copies(d):
+            copy.wait_send()
+        return carry
+
+    lax.fori_loop(1, devices, arrive, 0)
+    total_ref[...] = jnp.sum(squares[...], 0)
+
+
+def ship(shards, gain_grad, held, cap_slots, collective_id):
+    devices = held.shape[0] // cap_slots
+    rows = shards[0].shape[1]
+    blocks = sum(shard.shape[0] for shard in shards)
     tile = (8, 128)
+    vmem = pl.BlockSpec(memory_space=pltpu.VMEM)
     return pl.pallas_call(
-        partial(total_kernel, bits, narrow_bits),
-        out_shape=jax.ShapeDtypeStruct(tile, float32),
-        in_specs=[pl.BlockSpec(memory_space=pltpu.VMEM)],
-        out_specs=pl.BlockSpec(memory_space=pltpu.VMEM),
+        partial(ship_kernel, lax.axis_size("narrow")),
+        in_specs=[pl.BlockSpec(memory_space=pltpu.SMEM)] + [vmem] * (len(shards) + 1),
+        out_specs=[vmem, vmem],
+        out_shape=[
+            jax.ShapeDtypeStruct((cap_slots, devices, rows, BLOCK), bfloat16),
+            jax.ShapeDtypeStruct(tile, float32),
+        ],
         scratch_shapes=[
-            pltpu.VMEM((bits,) + tile, float32),
-            pltpu.SemaphoreType.DMA((bits,)),
-            pltpu.SemaphoreType.DMA((bits,)),
-        ],
-        compiler_params=pltpu.CompilerParams(collective_id=collective_id, has_side_effects=True),
-    )(jnp.broadcast_to(value, tile))[0, 0]
+            pltpu.VMEM((blocks, rows, BLOCK), float32),
+            pltpu.VMEM((devices, cap_slots, rows, BLOCK), bfloat16),
+            pltpu.VMEM((devices,) + tile, float32),
+        ]
+        + [pltpu.SemaphoreType.DMA((devices,))] * 4,
+        compiler_params=pltpu.CompilerParams(
+            collective_id=collective_id, has_side_effects=True, vmem_limit_bytes=VMEM_LIMIT
+        ),
+    )(held, *shards, gain_grad)
+
+
+def update_kernel(rates, slot_ref, back_ref, *refs):
+    masters, outs = refs[: len(rates)], refs[len(rates) :]
+    block = 0
+    for rate, master, out in zip(rates, masters, outs):
+        bands, _, columns = master.shape
+        for band in range(bands):
+            for start in range(0, columns, BLOCK):
+                here = slice(start, start + BLOCK)
+                old = master[band, :, here]
+                step = back_ref[slot_ref[block]].astype(float32)
+                out[band, :, here] = old - rate * (step + weight_decay * old)
+                block += 1
+
+
+def update(masters, rates, places, back):
+    vmem = pl.BlockSpec(memory_space=pltpu.VMEM)
+    return pl.pallas_call(
+        partial(update_kernel, rates),
+        in_specs=[pl.BlockSpec(memory_space=pltpu.SMEM)] + [vmem] * (len(masters) + 1),
+        out_specs=[vmem] * len(masters),
+        out_shape=[jax.ShapeDtypeStruct(master.shape, float32) for master in masters],
+        compiler_params=pltpu.CompilerParams(vmem_limit_bytes=VMEM_LIMIT),
+    )(places, back, *masters)
 
 
 def weight_grad_kernel(columns, band_rows, left_ref, *refs):
@@ -1090,21 +1284,13 @@
     middle = inputs + jnp.dot(merged, w_proj, preferred_element_type=jnp.float32)
     normed_two, inverse_two = normalize(middle)
     act_two = (normed_two * gain_pair[1]).astype(jnp.bfloat16)
-    hidden = jnp.dot(act_two, w_hidden, preferred_element_type=jnp.float32)
-    active = jax.nn.gelu(hidden, approximate=True).astype(jnp.bfloat16)
-    block_out = (middle + jnp.dot(active, w_back, preferred_element_type=jnp.float32)).astype(
-        jnp.bfloat16
-    )
-    plain = lambda size: tuple(((0, 0, start, BLOCK),) for start in range(0, size, BLOCK))
-    d_back = weight_grad(active, [cotangent[None]], plain(width), device_count)
-    d_active = jnp.einsum("td,fd->tf", cotangent, w_back, preferred_element_type=jnp.float32)
-    _, gelu_pull = jax.vjp(partial(jax.nn.gelu, approximate=True), hidden)
-    d_hidden = gelu_pull(d_active)[0].astype(jnp.bfloat16)
-    d_w_hidden = weight_grad(act_two, [d_hidden[None]], plain(FF), device_count)
-    d_act_two = jnp.einsum("tf,df->td", d_hidden, w_hidden, preferred_element_type=jnp.float32)
+    block_out, d_act_two, d_w_hidden, d_back = feed_forward(
+        act_two, cotangent, middle, w_hidden, w_back, device_count
+    )
     d_norm_two, d_gain_two = norm_backward(d_act_two, normed_two, inverse_two, gain_pair[1])
     d_middle = cotangent.astype(jnp.float32) + d_norm_two
     d_branch = d_middle.astype(jnp.bfloat16)
+    plain = lambda size: tuple(((0, 0, start, BLOCK),) for start in range(0, size, BLOCK))
     d_proj = weight_grad(merged, [d_branch[None]], plain(width), device_count)
     d_merged = jnp.einsum("te,de->td", d_branch, w_proj, preferred_element_type=jnp.float32).astype(
         jnp.bfloat16
@@ -1126,31 +1312,23 @@
     gain_parts = jnp.stack([d_gain_one, d_gain_two]).reshape(2, device_count, share)
     gain_parts = jnp.pad(gain_parts.transpose(1, 0, 2), ((0, 0), (0, 6), (0, 128 - share)))
     attn_sum, gain_grad = reduce_to_shards((d_attn, gain_parts), (6, 1), 1)
-    grad_shards = (attn_sum, proj_sum, hidden_sum, back_sum)
-    gain_grad = gain_grad[:2, :share]
     band_rows = BLOCK // device_count
-    local_squares = jnp.sum(gain_grad * gain_grad) + sum(
-        (jnp.sum(shard * shard) for shard in grad_shards)
-    )
-    pieces = jnp.concatenate(grad_shards, 0).reshape(-1, band_rows, BLOCK)
-    block_count = pieces.shape[0]
+    block_count = owners.shape[0]
     order = lax.iota(jnp.int32, block_count)
     earlier = (owners[None, :] == owners[:, None]) & (order[None, :] < order[:, None])
-    slots = owners * cap_slots + jnp.sum(earlier.astype(jnp.int32), 1)
-    routing = (slots[None, :] == lax.iota(jnp.int32, device_count * cap_slots)[:, None]).astype(
-        jnp.float32
-    )
-    routing = routing.reshape(device_count, cap_slots, block_count)
-    grad_norm = jnp.sqrt(total_of(local_squares, 2))
+    rank = jnp.sum(earlier.astype(jnp.int32), 1)
+    slots = owners * cap_slots + rank
+    every = lax.iota(jnp.int32, device_count * cap_slots)
+    held = jnp.max(jnp.where(slots[None, :] == every[:, None], order[None, :], -1), 1)
+    shards = [
+        shard.reshape(-1, band_rows, BLOCK)
+        for shard in (attn_sum, proj_sum, hidden_sum, back_sum)
+    ]
+    slot_grads, squares = ship(shards, gain_grad, held, cap_slots, 2)
+    gain_grad = gain_grad[:2, :share]
+    grad_norm = jnp.sqrt(squares[0, 0])
     factor = jnp.minimum(1.0, clip_bound / grad_norm)
-    arrived = lax.all_to_all(
-        jnp.einsum("okb,bxy->koxy", routing, pieces, precision=highest).astype(jnp.bfloat16),
-        ("wide", "narrow"),
-        split_axis=1,
-        concat_axis=1,
-        tiled=True,
-    )
-    slot_grads = arrived.reshape(cap_slots, BLOCK, BLOCK)
+    slot_grads = slot_grads.reshape(cap_slots, BLOCK, BLOCK)
     restored, first_new, second_new, left_new, right_new, gram, turn = soap_update(
         factor, slot_grads, moment_first, moment_second, left_stat, right_stat, left_basis, right_basis
     )
@@ -1165,16 +1343,10 @@
         concat_axis=1,
         tiled=True,
     )
-    back_pieces = jnp.einsum("okb,koxy->bxy", routing, returned, precision=highest)
     fan_list = (2 * width, max(1, width * 16 // seq_len), width, FF)
-    updated = []
-    offset = 0
-    for master, fan_in in zip(masters, fan_list):
-        band_count, band_rows, col_count = master.shape
-        piece_count = band_count * (col_count // BLOCK)
-        direction = from_pieces(back_pieces[offset : offset + piece_count], band_count, col_count)
-        updated.append(master - fan_in ** (-0.5) * (direction + weight_decay * master))
-        offset += piece_count
+    rates = tuple(fan_in ** (-0.5) for fan_in in fan_list)
+    places = rank * device_count + owners
+    updated = update(masters, rates, places, returned.reshape(-1, band_rows, BLOCK))
     clipped = gain_grad * factor
     gain_one_new = decay_rate * gain_first + (1.0 - decay_rate) * clipped
     gain_two_new = decay_rate * gain_second + (1.0 - decay_rate) * clipped * clipped

time: 693 us -> 654 us (0.944)
  matrix products: 65.3 us -> 6.5 us
  Pallas kernels: 549 us -> 577 us
    dot_general x6 -> x0, matrix products: 58.3 us -> none  [the longest x1 19.2 us: body(): hidden = jnp.dot(act_two, w_hidden, preferred_element_type=jnp.float32)]
    pallas_call x1 -> x3, Pallas kernels: 16.9 us -> 74.5 us  [the longest x1 51.7 us: feed_forward(): pl.pallas_call(partial(feed_kernel, deal), grid=(hidden // tile,), in_spe...]
    pallas_call x4 -> x2, Pallas kernels: 40 us -> 11.9 us  [weight_grad(): pl.pallas_call(partial(weight_grad_kernel, columns, band_rows), grid=(ban...]
    all_to_all x1, starting transfers between devices: 3.83 us -> 11.2 us  [body(): lax.all_to_all(shortened(restored.reshape(cap_slots, device_count, -1, BL...]
  transfers between devices with their start and end apart: 4 -> 3, of which waited for: 0 -> 0; matrix products, arithmetic and copies ran while one was open for 5% -> 3% of each run, Pallas kernels for 38% -> 37%
where the time goes in v6:
time: 654 us; the launch traced here: 651 us
  Pallas kernels  577 us (88%)
  other arithmetic  23.3 us (4%)
  between operations  17.3 us (3%)
  local copies, waits for them, and re-layouts  15.6 us (2%)
  starting transfers between devices  11.3 us (2%)
    pallas_call x1, Pallas kernels, attend_backward(): pl.pallas_call(partial(attend_backward_kernel, safe, chunk, halves, (bits...  165 us
    pallas_call x1, Pallas kernels, attend(): pl.pallas_call(partial(attend_kernel, safe, chunk, halves, plan, slots),...  127 us
    pallas_call x1, Pallas kernels, renew_bases(): pl.pallas_call(partial(renew_kernel, rows), out_shape=jax.ShapeDtypeStruc...  54.9 us
    pallas_call x1, Pallas kernels, feed_forward(): pl.pallas_call(partial(feed_kernel, deal), grid=(hidden // tile,), in_spe...  51.7 us
    pallas_call x1, Pallas kernels, reduce_to_shards(): pl.pallas_call(partial(reduce_kernel, bits, narrow_bits, plans, chunks, l...  51.3 us
    pallas_call x1, Pallas kernels, gather_bands(): pl.pallas_call(partial(gather_kernel, bits, narrow_bits, plans, chunks, l...  49.5 us
    pallas_call x1, Pallas kernels, soap_update(): pl.pallas_call(soap_kernel, grid=(slots,), in_specs=[pl.BlockSpec(memory_...  23.8 us
    pallas_call x1, Pallas kernels, ship(): pl.pallas_call(partial(ship_kernel, lax.axis_size('narrow')), in_specs=[p...  20.9 us
  transfers between devices with their start and end apart: 3, of which 0 were waited for; matrix products, arithmetic and copies ran while one was open for 3% of the time, Pallas kernels for 37%

profile of v6, /device:TPU:0, one launch (start us, length us, event | category | flops | bytes accessed | tf_op | source)
XLA Modules:
  0.0 650.8 jit_solution(18442242119170090746)
XLA Ops:
  7.2 1.7 convert_element_type.61
  9.0 1.8 convert_element_type.63
  10.8 1.7 convert_element_type.54.refs_0_
  13.7 49.5 %shard_map.288 = (bf16[4,2,2,2,2,2,8,3072]{7,6,5,4,3,2,1,0:T(8,128)(2,1)}, bf16[1,2,2,2,2,2,8,128]{7,6,5,4,3,2,1,0:T(8,128)(2,1)}) custom-call(bf16[4,8,3072]{2,1,0:T(8,128)(2,1)} %convert_element_type.54.refs_0_, bf16[1,8,128]{2,1,0:T(8,128)(2,1)} %pad_bitcast_fusion.refs_1_), custom_call_target="tpu_custom_call" | custom-call | bytes 100000000 | tf_op jit(solution)/shard_map/pallas_call | solution.py:527
  69.2 8.6 %shard_map.289 = (bf16[4,768,384]{2,1,0:T(8,128)(2,1)S(1)}, bf16[4,768,384]{2,1,0:T(8,128)(2,1)}) custom-call(bf16[768,1024]{1,0:T(8,128)(2,1)S(1)} %fusion.6.acts_ref.left_ref, bf16[1024,3072]{1,0:T(8,128)(2,1)} %bitcast.59, bf16[1024,3072]{1,0:T(8,128)(2,1)} %bitcast.60, bf16[1024,3072]{1,0:T(8,128)(2,1)} %bitcast.61), custom_call_target="tpu_custom_call" | custom-call | flops 4831838208 | bytes 12582912 | tf_op jit(solution)/shard_map/pallas_call | solution.py:95
  77.8 126.8 %shard_map.290 = (bf16[2,3072,384]{2,1,0:T(8,128)(2,1)}, bf16[768,1024]{1,0:T(8,128)(2,1)S(1)}, bf16[2,3072,128]{2,1,0:T(8,128)(2,1)S(1)}, f32[2,2,3072]{2,1,0:T...) custom-call(s32[1]{0:T(128)S(6)} %copy.45.length_ref, bf16[4,768,384]{2,1,0:T(8,128)(2,1)S(1)} %get-tuple-element.50.refs_0_, ...), custom_call_target="tpu_custom_call" | custom-call | flops 38654705664 | bytes 12582912 | tf_op jit(solution)/shard_map/pallas_call | solution.py:712
  205.8 3.5 fusion.18
  211.1 1.6 multiply_convert_fusion.acts_ref
  212.7 51.7 %shard_map.291 = (bf16[768,1024]{1,0:T(8,128)(2,1)}, f32[768,1024]{1,0:T(8,128)}, bf16[32,4,128,256]{3,2,1,0:T(8,128)(2,1)}, bf16[32,512,256]{2,1,0:T(8,128)(2,1)}) custom-call(bf16[768,1024]{1,0:T(8,128)(2,1)} %multiply_convert_fusion.acts_ref, bf16[768,1024]{1,0:T(8,128)(2,1)} %grad_ref.1, f32[768,1024]{1,0:T(8,128)} %copy-done.17, ...), custom_call_target="tpu_custom_call" | custom-call | flops 38654705664 | bytes 33554432 | tf_op jit(solution)/shard_map/pallas_call | solution.py:1021
  264.4 4.2 multiply_reduce_fusion
  270.4 2.8 shard_map.292
  273.3 3.0 convolution_convert_fusion.d_merged
  276.2 164.7 %shard_map.293 = (bf16[2,4,768,384]{3,2,1,0:T(8,128)(2,1)}, f32[512,256]{1,0:T(8,128)}, f32[512,256]{1,0:T(8,128)}, f32[128,256]{1,0:T(8,128)}) custom-call(s32[1]{0:T(128)S(6)} %copy.45.length_ref, bf16[2,3072,384]{2,1,0:T(8,128)(2,1)} %get-tuple-element.56.scene_ref, bf16[2,3072,128]{2,1,0:T(8,128)(2,1)} %copy-done.15, f32[2,2,3072]{2,1,0:T(2,128)} %copy-done.16, ...), custom_call_target="tpu_custom_call" | custom-call | flops 96636764160 | bytes 12582912 | tf_op jit(solution)/shard_map/pallas_call | solution.py:918
  441.0 2.9 slice_bitcast_fusion
  443.8 10.8 %shard_map.294 = f32[768,1024]{1,0:T(8,128)} custom-call(bf16[4,768,384]{2,1,0:T(8,128)(2,1)S(1)} %get-tuple-element.94.refs_0_, bf16[4,768,384]{2,1,0:T(8,128)(2,1)S(1)} %get-tuple-element.93.refs_1_, bf16[1024,3072]{1,0:T(8,128)(2,1)} %bitcast.62, bf16[1024,3072]{1,0:T(8,128)(2,1)} %bitcast.63, bf16[1024,3072]{1,0:T(8,128)(2,1)} %bitcast.64), custom_call_target="tpu_custom_call" | custom-call | flops 4831838208 | bytes 14155776 | tf_op jit(solution)/shard_map/pallas_call | solution.py:135
  454.7 9.1 %shard_map.295 = bf16[32,384,256]{2,1,0:T(8,128)(2,1)} custom-call(bf16[768,1024]{1,0:T(8,128)(2,1)S(1)} %copy-done.2, bf16[4,768,384]{2,1,0:T(8,128)(2,1)S(1)} %get-tuple-element.94.refs_0_, bf16[4,768,384]{2,1,0:T(8,128)(2,1)} %copy-done), custom_call_target="tpu_custom_call" | custom-call | flops 4831838208 | bytes 12582912 | tf_op jit(solution)/shard_map/pallas_call | solution.py:1217
  466.2 51.3 %shard_map.296 = (f32[384,256]{1,0:T(8,128)}, f32[8,128]{1,0:T(8,128)}) custom-call(bf16[2,2,2,2,2,384,256]{6,5,4,3,2,1,0:T(8,128)(2,1)} %bitcast.65, f32[2,2,2,2,2,8,128]{6,5,4,3,2,1,0:T(8,128)} %bitcast.66), custom_call_target="tpu_custom_call" | custom-call | flops 100000000 | bytes 400000000 | tf_op jit(solution)/shard_map/pallas_call | solution.py:424
  519.2 20.9 %shard_map.297 = (bf16[6,32,8,256]{3,2,1,0:T(8,128)(2,1)S(1)}, f32[8,128]{1,0:T(8,128)S(1)}) custom-call(s32[192]{0:T(256)S(1)} %select_reduce_fusion.held_ref, f32[48,8,256]{2,1,0:T(8,128)S(1)} %bitcast.55, f32[16,8,256]{2,1,0:T(8,128)S(1)} %bitcast.56, f32[64,8,256]{2,1,0:T(8,128)S(1)} %bitcast.53, f32[64,8,256]{2,1,0:T(8,128)S(1)} %bitcast.54, ...), custom_call_target="tpu_custom_call" | custom-call | tf_op jit(solution)/shard_map/pallas_call | solution.py:1149
  542.8 23.8 %shard_map.298 = (bf16[6,256,256]{2,1,0:T(8,128)(2,1)S(1)}, f32[6,256,256]{2,1,0:T(8,128)}, f32[6,256,256]{2,1,0:T(8,128)}, f32[6,256,256]{2,1,0:T(8,128)}, f32[...) custom-call(f32[1,1]{1,0:T(1,128)} %bitcast.23.factor_ref, ...), custom_call_target="tpu_custom_call" | custom-call | flops 12079595520 | bytes 23592960 | tf_op jit(solution)/shard_map/pallas_call | solution.py:184
  567.5 11.2 %all-to-all-start = ((bf16[6,32,8,256]{3,2,0,1:T(8,128)(2,1)}), bf16[6,32,8,256]{3,2,0,1:T(8,128)(2,1)S(1)}, u32[]{:S(2)}, u32[]{:S(2)}) async-start(bf16[6,32,8,256]{3,2,0,1:T(8,128)(2,1)} %copy.39), calls=%async_computation | async-start | bytes 1572864 | tf_op jit(solution)/shard_map/all_to_all | solution.py:1339
  578.7 54.9 %shard_map.300 = f32[12,256,256]{2,1,0:T(8,128)S(1)} custom-call(f32[12,256,256]{2,1,0:T(8,128)} %bitcast.74, f32[12,256,256]{2,1,0:T(8,128)} %bitcast.75), custom_call_target="tpu_custom_call" | custom-call | flops 40265318400 | bytes 9437184 | tf_op jit(solution)/shard_map/pallas_call | solution.py:244
  635.0 1.9 slice_bitcast_fusion.2
  638.5 2.1 fusion.11
  640.7 1.9 shard_map.299
  (114 shorter events, 21.3 us)
Async XLA Ops:
  7.2 60.6 %copy-start.19 = (bf16[768,1024]{1,0:T(8,128)(2,1)S(1)}, bf16[768,1024]{1,0:T(8,128)(2,1)}, u32[]{:S(2)}) copy-start(bf16[768,1024]{1,0:T(8,128)(2,1)} %param.17) | copy-start | bytes 4718596
  7.2 198.6 %all-gather.3.cloned.1.call-start = ((), (), s32[]{:S(2)}) async-start(), calls=%async_computation.1 | async-start | bytes 2162688 | tf_op jit(solution)/shard_map/all_gather | solution.py:1271
  8.9 203.8 %all-gather.5.cloned.1.call-start = ((), (), s32[]{:S(2)}) async-start(), calls=%async_computation.2 | async-start | bytes 8650752 | tf_op jit(solution)/shard_map/all_gather | solution.py:1271
  64.2 5.0 copy-start.30
  68.7 9.2 %copy-start.32 = (f32[768]{0:T(1024)}, f32[768]{0:T(1024)S(1)}, u32[]{:S(2)}) copy-start(f32[768]{0:T(1024)S(1)} %add_rsqrt_fusion.1) | copy-start | bytes 9220
  69.2 8.6 %copy-start.1 = (bf16[768,1024]{1,0:T(8,128)(2,1)}, bf16[768,1024]{1,0:T(8,128)(2,1)S(1)}, u32[]{:S(2)}) copy-start(bf16[768,1024]{1,0:T(8,128)(2,1)S(1)} %fusion.6.acts_ref.left_ref) | copy-start | bytes 4718596
  212.7 55.9 %copy-start.27 = (bf16[768,1024]{1,0:T(8,128)(2,1)S(1)}, bf16[768,1024]{1,0:T(8,128)(2,1)}, u32[]{:S(2)}) copy-start(bf16[768,1024]{1,0:T(8,128)(2,1)} %grad_ref.1) | copy-start | bytes 4718596
  270.4 5.8 copy-start.25
  443.8 10.8 %copy-start = (bf16[4,768,384]{2,1,0:T(8,128)(2,1)}, bf16[4,768,384]{2,1,0:T(8,128)(2,1)S(1)}, u32[]{:S(2)}) copy-start(bf16[4,768,384]{2,1,0:T(8,128)(2,1)S(1)} %get-tuple-element.93.refs_1_) | copy-start | bytes 7077892
  443.8 10.8 %copy-start.2 = (bf16[768,1024]{1,0:T(8,128)(2,1)S(1)}, bf16[768,1024]{1,0:T(8,128)(2,1)}, u32[]{:S(2)}) copy-start(bf16[768,1024]{1,0:T(8,128)(2,1)} %copy-done.1) | copy-start | bytes 4718596
  454.6 9.2 %copy-start.20 = (bf16[768,1024]{1,0:T(8,128)(2,1)S(1)}, bf16[768,1024]{1,0:T(8,128)(2,1)}, u32[]{:S(2)}) copy-start(bf16[768,1024]{1,0:T(8,128)(2,1)} %param.17) | copy-start | bytes 4718596
  454.6 9.2 %copy-start.22 = (f32[768,1024]{1,0:T(8,128)S(1)}, f32[768,1024]{1,0:T(8,128)}, u32[]{:S(2)}) copy-start(f32[768,1024]{1,0:T(8,128)} %shard_map.294) | copy-start | bytes 9437188
  454.7 9.2 %copy-start.29 = (f32[768]{0:T(1024)S(1)}, f32[768]{0:T(1024)}, u32[]{:S(2)}) copy-start(f32[768]{0:T(1024)} %copy-done.28) | copy-start | bytes 9220
  454.7 9.1 %copy-start.31 = (f32[1024]{0:T(1024)S(1)}, f32[1024]{0:T(1024)}, u32[]{:S(2)}) copy-start(f32[1024]{0:T(1024)} %copy-done.30) | copy-start | bytes 12292
  454.7 9.1 %copy-start.33 = (f32[768]{0:T(1024)S(1)}, f32[768]{0:T(1024)}, u32[]{:S(2)}) copy-start(f32[768]{0:T(1024)} %copy-done.32) | copy-start | bytes 9220
  466.2 51.3 %copy-start.7 = (f32[512,256]{1,0:T(8,128)S(1)}, f32[512,256]{1,0:T(8,128)}, u32[]{:S(2)}) copy-start(f32[512,256]{1,0:T(8,128)} %get-tuple-element.64) | copy-start | bytes 1572868
  466.2 51.3 %copy-start.8 = (f32[512,256]{1,0:T(8,128)S(1)}, f32[512,256]{1,0:T(8,128)}, u32[]{:S(2)}) copy-start(f32[512,256]{1,0:T(8,128)} %get-tuple-element.65) | copy-start | bytes 1572868
  466.2 51.3 %copy-start.10 = (f32[128,256]{1,0:T(8,128)S(1)}, f32[128,256]{1,0:T(8,128)}, u32[]{:S(2)}) copy-start(f32[128,256]{1,0:T(8,128)} %get-tuple-element.63) | copy-start | bytes 393220
  466.2 75.2 %copy-start.12 = (f32[6,256,256]{2,1,0:T(8,128)S(1)}, f32[6,256,256]{2,1,0:T(8,128)}, u32[]{:S(2)}) copy-start(f32[6,256,256]{2,1,0:T(8,128)} %first_ref.1) | copy-start | bytes 4718596
  567.5 73.1 %all-to-all-start = ((bf16[6,32,8,256]{3,2,0,1:T(8,128)(2,1)}), bf16[6,32,8,256]{3,2,0,1:T(8,128)(2,1)S(1)}, u32[]{:S(2)}, u32[]{:S(2)}) async-start(bf16[6,32,8,256]{3,2,0,1:T(8,128)(2,1)} %copy.39), calls=%async_computation | async-start | bytes 1572864 | tf_op jit(solution)/shard_map/all_to_all | solution.py:1339
  578.7 55.0 %copy-start.34 = (f32[2,32]{1,0:T(2,128)S(1)}, f32[2,32]{1,0:T(2,128)}, u32[]{:S(2)}) copy-start(f32[2,32]{1,0:T(2,128)} %param.25) | copy-start | bytes 772
  578.7 55.0 %copy-start.35 = (f32[2,32]{1,0:T(2,128)S(1)}, f32[2,32]{1,0:T(2,128)}, u32[]{:S(2)}) copy-start(f32[2,32]{1,0:T(2,128)} %param.26) | copy-start | bytes 772
  578.7 55.0 %copy-start.36 = (f32[2,32]{1,0:T(2,128)S(1)}, f32[2,32]{1,0:T(2,128)}, u32[]{:S(2)}) copy-start(f32[2,32]{1,0:T(2,128)} %param.27) | copy-start | bytes 772
  578.7 58.1 %copy-start.26 = (f32[768,1024]{1,0:T(8,128)S(1)}, f32[768,1024]{1,0:T(8,128)}, u32[]{:S(2)}) copy-start(f32[768,1024]{1,0:T(8,128)} %copy-done.25) | copy-start | bytes 9437188
  (17 other events, 39.9 us)
Sparse Core Ops, SparseCore 0:
  11.5 62.9 all-gather.2
  78.0 95.9 all-gather.4

commit v7 on v6

--- a/solution.py
+++ b/solution.py
@@ -36,6 +36,7 @@
 DELAY = 12.0
 GATHER_PACE = 6.0
 GATHER_DELAY = 30.0
+SETTLE_DELAY = 6.0
 GELU = 0.7978845608
 CUBIC = 0.044715
 
@@ -155,10 +156,15 @@
     factor_ref, g_ref, first_ref, second_ref, ls_ref, rs_ref, lb_ref, rb_ref,
     back_ref, first_out, second_out, ls_out, rs_out, gram_ref, turn_ref,
 ):
-    gradient = factor_ref[0, 0] * g_ref[0].astype(float32)
+    factor = factor_ref[0, 0]
+    rough = g_ref[0]
+    gradient = factor * rough.astype(float32)
+    half_square = (1.0 - decay_rate) * factor * factor
     left_base, right_base = lb_ref[0], rb_ref[0]
-    left_new = decay_rate * ls_ref[0] + (1.0 - decay_rate) * exact(gradient, gradient, NT)
-    right_new = decay_rate * rs_ref[0] + (1.0 - decay_rate) * exact(gradient, gradient, TN)
+    left_square = lax.dot_general(rough, rough, NT, preferred_element_type=float32)
+    right_square = jnp.dot(rough.T, rough, preferred_element_type=float32)
+    left_new = decay_rate * ls_ref[0] + half_square * left_square
+    right_new = decay_rate * rs_ref[0] + half_square * right_square
     ls_out[0] = left_new
     rs_out[0] = right_new
     turned = exact(left_base, exact(gradient, right_base), TN)
@@ -194,7 +200,7 @@
     )(factor.reshape(1, 1), gradient, first_old, second_old, left_old, right_old, left_base, right_base)
 
 
-def renew_kernel(rows, gram_ref, turn_ref, q_ref, x_ref, u_ref):
+def renew_kernel(rows, gram_ref, turn_ref, left_ref, right_ref, x_ref, u_ref):
     count, order = gram_ref.shape[0], gram_ref.shape[1]
     eye = (
         lax.broadcasted_iota(jnp.int32, (rows, rows), 0)
@@ -233,19 +239,20 @@
         lax.fori_loop(0, count, solve, 0, unroll=2)
 
     def turn_back(at, carry):
-        q_ref[at] = u_ref[at, :, order:].T
+        left_ref[at] = u_ref[2 * at, :, order:].T
+        right_ref[at] = u_ref[2 * at + 1, :, order:].T
         return carry
 
-    lax.fori_loop(0, count, turn_back, 0)
+    lax.fori_loop(0, count // 2, turn_back, 0)
 
 
 def renew_bases(gram, turn, rows=64):
     count, order, _ = gram.shape
     return pl.pallas_call(
         partial(renew_kernel, rows),
-        out_shape=jax.ShapeDtypeStruct(gram.shape, float32),
+        out_shape=[jax.ShapeDtypeStruct((count // 2, order, order), float32)] * 2,
         in_specs=[pl.BlockSpec(memory_space=pltpu.VMEM)] * 2,
-        out_specs=pl.BlockSpec(memory_space=pltpu.VMEM),
+        out_specs=[pl.BlockSpec(memory_space=pltpu.VMEM)] * 2,
         scratch_shapes=[
             pltpu.VMEM((count, rows, 2 * rows), float32),
             pltpu.VMEM((count, order, 2 * order), float32),
@@ -391,7 +398,8 @@
     return table
 
 
-def reduce_plan(parts, pieces):
+def reduce_plan(parts, pieces, orders=None):
+    orders = ORDERS if orders is None else orders
     bits, narrow_bits = mesh_bits()
     shapes = [part.shape[1:] for part in parts]
     kinds = [part.dtype for part in parts]
@@ -399,9 +407,9 @@
     for at, (shape, cut) in enumerate(zip(shapes, pieces)):
         rows = shape[0] // cut
         for row in range(0, shape[0], rows):
-            chunks.append((at, row, rows, len(chunks) % len(ORDERS)))
+            chunks.append((at, row, rows, len(chunks) % len(orders)))
     later = tuple(range(3, bits))
-    plans = tuple(tuple(b for part in order for b in (later if part is None else (part,))) for order in ORDERS)
+    plans = tuple(tuple(b for part in order for b in (later if part is None else (part,))) for order in orders)
     sizes = [bits - 1] + [bits - 1 - stage for stage in range(bits)]
     scratch = [
         pltpu.VMEM((2,) * size + shape, kind)
@@ -415,7 +423,10 @@
         pltpu.SemaphoreType.DMA((total, bits)),
     ]
     outs = [jax.ShapeDtypeStruct(shape, float32) for shape in shapes]
-    halved = [part.reshape((2,) * bits + shape) for part, shape in zip(parts, shapes)]
+    halved = [
+        part.reshape((2,) * bits + shape) if hasattr(part, "reshape") else part
+        for part, shape in zip(parts, shapes)
+    ]
     return bits, narrow_bits, plans, tuple(chunks), halved, outs, scratch
 
 
@@ -953,6 +964,91 @@
             transcendentals=0,
         ),
     )(lengths, scenes, mixed, log_totals, d_merged, *halved)
+
+
+def settle_kernel(plan, acts_ref, grads_ref, weights_ref, sum_ref, back_ref, right_ref, left_ref, dealt, *scratch):
+    bits = plan[0]
+    halves, groups, tok_rows, _ = grads_ref.shape
+    width = acts_ref.shape[1]
+    bands = width // BLOCK
+    chunks = plan[3]
+    peers, begin, finish, drain = reduce_steps(*plan[:4], [dealt], [sum_ref], scratch)
+    left_ref[...] = acts_ref[...].T
+    blocks = 3 * width // BLOCK
+    for half in range(halves):
+        for group in range(groups):
+            for third in range(3):
+                start = third * width + (group * halves + half) * PAIR
+                right_ref[:, start : start + PAIR] = grads_ref[
+                    half, group, :, third * PAIR : (third + 1) * PAIR
+                ]
+    rows = BLOCK >> bits
+
+    def band_product(band):
+        left = left_ref[band * BLOCK : (band + 1) * BLOCK, :]
+        for at in range(0, blocks, 2):
+            pair = jnp.dot(
+                left, right_ref[:, at * BLOCK : (at + 2) * BLOCK], preferred_element_type=float32
+            ).astype(bfloat16)
+            pair = [pair[:, h * BLOCK : (h + 1) * BLOCK].reshape(-1, rows, BLOCK) for h in range(2)]
+            low = (band * blocks + at) * rows
+            both = jnp.concatenate(pair, 1)
+            dealt[(slice(None),) * bits + (slice(low, low + 2 * rows),)] = both.reshape(
+                (2,) * bits + both.shape[1:]
+            )
+
+    def back_product(band):
+        here = slice(band * BLOCK, (band + 1) * BLOCK)
+        back_ref[:, here] = lax.dot_general(
+            right_ref[...], weights_ref[here, :], NT, preferred_element_type=float32
+        )
+
+    each = len(chunks) // bands
+    work = [(2.5 * band, -1, band, -1) for band in range(2 * bands)]
+    for chunk in range(len(chunks)):
+        for stage in range(bits):
+            ready = max(2.5 * (chunk // each + 1), 3.5 * chunk)
+            work.append((ready + SETTLE_DELAY * (stage + 1), -stage, chunk, stage))
+    for _, _, which, stage in sorted(work):
+        if stage >= 0:
+            finish(which, stage)
+        elif which < bands:
+            band_product(which)
+            if which == 0:
+                greet(peers)
+            for chunk in range(which * each, (which + 1) * each):
+                begin(chunk)
+        else:
+            back_product(which - bands)
+    drain()
+
+
+def settle(acts, grads, weights, device_count, collective_id):
+    tok_rows, width = acts.shape
+    rows = 3 * width * width // BLOCK // device_count
+    dealt = jax.ShapeDtypeStruct((device_count, rows, BLOCK), bfloat16)
+    bits, narrow_bits, plans, chunks, _, outs, scratch = reduce_plan(
+        [dealt], (2 * width // BLOCK,), ORDERS[:2]
+    )
+    vmem = pl.BlockSpec(memory_space=pltpu.VMEM)
+    return pl.pallas_call(
+        partial(settle_kernel, (bits, narrow_bits, plans, chunks)),
+        in_specs=[vmem] * 3,
+        out_specs=[vmem] * 2,
+        out_shape=outs + [jax.ShapeDtypeStruct((tok_rows, width), float32)],
+        scratch_shapes=[
+            pltpu.VMEM((tok_rows, 3 * width), bfloat16),
+            pltpu.VMEM((width, tok_rows), bfloat16),
+            pltpu.VMEM((2,) * bits + (rows, BLOCK), bfloat16),
+        ]
+        + scratch,
+        compiler_params=pltpu.CompilerParams(
+            collective_id=collective_id, has_side_effects=True, vmem_limit_bytes=60 * 2**20
+        ),
+        cost_estimate=pl.CostEstimate(
+            flops=12 * tok_rows * width**2, bytes_accessed=10**8, transcendentals=0
+        ),
+    )(acts, grads, weights)
 
 
 def feed_kernel(deal, acts_ref, grad_ref, middle_ref, up_ref, down_ref, out_ref, back_ref, one_ref, two_ref, turned_ref, sum_ref):
@@ -1067,13 +1163,14 @@
         return carry
 
     lax.fori_loop(1, devices, announce, 0)
-    at, own = 0, jnp.sum(gain_ref[...] * gain_ref[...])
+    at, own = 0, jnp.zeros((), float32)
     for shard in shards:
         values = shard[...]
         own += jnp.sum(values * values)
         pieces[at : at + values.shape[0]] = values
         at += values.shape[0]
-    squares[me] = jnp.full(squares.shape[1:], own, float32)
+    squares[me, : gain_ref.shape[0]] = gain_ref[...]
+    squares[me, gain_ref.shape[0] :] = jnp.full((8, 128), own, float32)
 
     def pack(place, carry):
         for slot in range(slots):
@@ -1144,7 +1241,7 @@
     devices = held.shape[0] // cap_slots
     rows = shards[0].shape[1]
     blocks = sum(shard.shape[0] for shard in shards)
-    tile = (8, 128)
+    tile = (gain_grad.shape[0] + 8, 128)
     vmem = pl.BlockSpec(memory_space=pltpu.VMEM)
     return pl.pallas_call(
         partial(ship_kernel, lax.axis_size("narrow")),
@@ -1299,19 +1396,21 @@
     d_packed, hidden_sum, back_sum, proj_sum = attend_backward(
         lengths, scenes, mixed, d_merged, log_totals, safe, ready, (8, 8, 2), 5
     )
-    d_packed = [d_packed[half] for half in range(halves)]
-    grouped = tuple(
-        tuple((half, group, third * PAIR, PAIR) for half in range(halves))
-        for third in range(3)
-        for group in range(narrow_count)
-    )
-    d_attn = weight_grad(act_one, d_packed, grouped, device_count)
-    d_act_one = project_back(d_packed, w_attn)
+    if BLOCK // device_count % 8:
+        d_packed = [d_packed[half] for half in range(halves)]
+        grouped = tuple(
+            tuple((half, group, third * PAIR, PAIR) for half in range(halves))
+            for third in range(3)
+            for group in range(narrow_count)
+        )
+        d_attn = weight_grad(act_one, d_packed, grouped, device_count)
+        (attn_sum,) = reduce_to_shards((d_attn,), (6,), 1)
+        d_act_one = project_back(d_packed, w_attn)
+    else:
+        attn_sum, d_act_one = settle(act_one, d_packed, w_attn, device_count, 1)
     d_norm_one, d_gain_one = norm_backward(d_act_one, normed_one, inverse_one, gain_pair[0])
     grad_tokens = (d_middle + d_norm_one).astype(jnp.bfloat16)
-    gain_parts = jnp.stack([d_gain_one, d_gain_two]).reshape(2, device_count, share)
-    gain_parts = jnp.pad(gain_parts.transpose(1, 0, 2), ((0, 0), (0, 6), (0, 128 - share)))
-    attn_sum, gain_grad = reduce_to_shards((d_attn, gain_parts), (6, 1), 1)
+    gain_parts = jnp.stack([d_gain_one, d_gain_two]).reshape(-1, 128)
     band_rows = BLOCK // device_count
     block_count = owners.shape[0]
     order = lax.iota(jnp.int32, block_count)
@@ -1324,18 +1423,18 @@
         shard.reshape(-1, band_rows, BLOCK)
         for shard in (attn_sum, proj_sum, hidden_sum, back_sum)
     ]
-    slot_grads, squares = ship(shards, gain_grad, held, cap_slots, 2)
-    gain_grad = gain_grad[:2, :share]
-    grad_norm = jnp.sqrt(squares[0, 0])
+    slot_grads, totals = ship(shards, gain_parts, held, cap_slots, 2)
+    place = lax.axis_index(("wide", "narrow"))
+    gain_grad = totals[:-8].reshape(2, width)
+    grad_norm = jnp.sqrt(totals[-1, 0] + jnp.sum(gain_grad * gain_grad))
+    gain_grad = lax.dynamic_slice_in_dim(gain_grad, place * share, share, 1)
     factor = jnp.minimum(1.0, clip_bound / grad_norm)
     slot_grads = slot_grads.reshape(cap_slots, BLOCK, BLOCK)
     restored, first_new, second_new, left_new, right_new, gram, turn = soap_update(
         factor, slot_grads, moment_first, moment_second, left_stat, right_stat, left_basis, right_basis
     )
     square = (-1, BLOCK, BLOCK)
-    bases = renew_bases(gram.reshape(square), turn.reshape(square))
-    bases = bases.reshape(cap_slots, 2, BLOCK, BLOCK)
-    left_turn, right_turn = bases[:, 0], bases[:, 1]
+    left_turn, right_turn = renew_bases(gram.reshape(square), turn.reshape(square))
     returned = lax.all_to_all(
         shortened(restored.reshape(cap_slots, device_count, -1, BLOCK)),
         ("wide", "narrow"),

time: 654 us -> 645 us (0.986)
  Pallas kernels: 577 us -> 565 us
    pallas_call x2 -> x1, Pallas kernels: 11.9 us -> 2.81 us  [weight_grad(): pl.pallas_call(partial(weight_grad_kernel, columns, band_rows), grid=(ban...]
    pallas_call x3 -> x2, Pallas kernels: 117 us -> 113 us  [the longest x1 58.1 us: settle(): pl.pallas_call(partial(settle_kernel, (bits, narrow_bits, plans, chunks))...]
where the time goes in v7:
time: 645 us; the launch traced here: 642 us
  Pallas kernels  565 us (88%)
  other arithmetic  26.8 us (4%)
  between operations  18 us (3%)
  starting transfers between devices  12.9 us (2%)
  local copies, waits for them, and re-layouts  11.4 us (2%)
  matrix products  6.89 us (1%)
    pallas_call x1, Pallas kernels, attend_backward(): pl.pallas_call(partial(attend_backward_kernel, safe, chunk, halves, (bits...  164 us
    pallas_call x1, Pallas kernels, attend(): pl.pallas_call(partial(attend_kernel, safe, chunk, halves, plan, slots),...  127 us
    pallas_call x1, Pallas kernels, settle(): pl.pallas_call(partial(settle_kernel, (bits, narrow_bits, plans, chunks))...  58.1 us
    pallas_call x1, Pallas kernels, renew_bases(): pl.pallas_call(partial(renew_kernel, rows), out_shape=[jax.ShapeDtypeStru...  55.1 us
    pallas_call x1, Pallas kernels, feed_forward(): pl.pallas_call(partial(feed_kernel, deal), grid=(hidden // tile,), in_spe...  52.4 us
    pallas_call x1, Pallas kernels, gather_bands(): pl.pallas_call(partial(gather_kernel, bits, narrow_bits, plans, chunks, l...  49.5 us
    pallas_call x1, Pallas kernels, ship(): pl.pallas_call(partial(ship_kernel, lax.axis_size('narrow')), in_specs=[p...  24.4 us
    pallas_call x1, Pallas kernels, soap_update(): pl.pallas_call(soap_kernel, grid=(slots,), in_specs=[pl.BlockSpec(memory_...  21.7 us
  transfers between devices with their start and end apart: 3, of which 0 were waited for; matrix products, arithmetic and copies ran while one was open for 3% of the time, Pallas kernels for 37%

profile of v7, /device:TPU:0, one launch (start us, length us, event | category | flops | bytes accessed | tf_op | source)
XLA Modules:
  0.0 641.5 jit_solution(9924274684202277550)
XLA Ops:
  7.2 1.7 convert_element_type.59
  9.0 1.8 convert_element_type.61
  10.8 1.7 convert_element_type.52.refs_0_
  13.7 49.5 %shard_map.288 = (bf16[4,2,2,2,2,2,8,3072]{7,6,5,4,3,2,1,0:T(8,128)(2,1)}, bf16[1,2,2,2,2,2,8,128]{7,6,5,4,3,2,1,0:T(8,128)(2,1)}) custom-call(bf16[4,8,3072]{2,1,0:T(8,128)(2,1)} %convert_element_type.52.refs_0_, bf16[1,8,128]{2,1,0:T(8,128)(2,1)} %pad_bitcast_fusion.refs_1_), custom_call_target="tpu_custom_call" | custom-call | bytes 100000000 | tf_op jit(solution)/shard_map/pallas_call | solution.py:538
  69.2 8.6 %shard_map.289 = (bf16[4,768,384]{2,1,0:T(8,128)(2,1)S(1)}, bf16[4,768,384]{2,1,0:T(8,128)(2,1)}) custom-call(bf16[768,1024]{1,0:T(8,128)(2,1)S(1)} %fusion.6.acts_ref, bf16[1024,3072]{1,0:T(8,128)(2,1)} %bitcast.44, bf16[1024,3072]{1,0:T(8,128)(2,1)} %bitcast.45, bf16[1024,3072]{1,0:T(8,128)(2,1)} %bitcast.46), custom_call_target="tpu_custom_call" | custom-call | flops 4831838208 | bytes 12582912 | tf_op jit(solution)/shard_map/pallas_call | solution.py:96
  77.8 126.8 %shard_map.290 = (bf16[2,3072,384]{2,1,0:T(8,128)(2,1)}, bf16[768,1024]{1,0:T(8,128)(2,1)S(1)}, bf16[2,3072,128]{2,1,0:T(8,128)(2,1)S(1)}, f32[2,2,3072]{2,1,0:T...) custom-call(s32[1]{0:T(128)S(6)} %copy.37.length_ref, bf16[4,768,384]{2,1,0:T(8,128)(2,1)S(1)} %get-tuple-element.52.refs_0_, ...), custom_call_target="tpu_custom_call" | custom-call | flops 38654705664 | bytes 12582912 | tf_op jit(solution)/shard_map/pallas_call | solution.py:723
  205.8 3.9 fusion.19
  210.2 1.3 copy-done.17
  211.5 1.6 multiply_convert_fusion.acts_ref
  213.1 52.4 %shard_map.291 = (bf16[768,1024]{1,0:T(8,128)(2,1)}, f32[768,1024]{1,0:T(8,128)}, bf16[32,4,128,256]{3,2,1,0:T(8,128)(2,1)}, bf16[32,512,256]{2,1,0:T(8,128)(2,1)}) custom-call(bf16[768,1024]{1,0:T(8,128)(2,1)} %multiply_convert_fusion.acts_ref, bf16[768,1024]{1,0:T(8,128)(2,1)} %grad_ref.1, f32[768,1024]{1,0:T(8,128)} %copy-done.17, ...), custom_call_target="tpu_custom_call" | custom-call | flops 38654705664 | bytes 33554432 | tf_op jit(solution)/shard_map/pallas_call | solution.py:1117
  265.5 3.2 multiply_reduce_fusion
  270.1 2.8 shard_map.292
  272.9 3.0 convolution_convert_fusion.d_merged
  275.9 164.3 %shard_map.293 = (bf16[2,4,768,384]{3,2,1,0:T(8,128)(2,1)}, f32[512,256]{1,0:T(8,128)}, f32[512,256]{1,0:T(8,128)}, f32[128,256]{1,0:T(8,128)}) custom-call(s32[1]{0:T(128)S(6)} %copy.37.length_ref, bf16[2,3072,384]{2,1,0:T(8,128)(2,1)} %get-tuple-element.58.scene_ref, bf16[2,3072,128]{2,1,0:T(8,128)(2,1)} %copy-done.15, f32[2,2,3072]{2,1,0:T(2,128)} %copy-done.16, ...), custom_call_target="tpu_custom_call" | custom-call | flops 96636764160 | bytes 12582912 | tf_op jit(solution)/shard_map/pallas_call | solution.py:929
  440.2 58.1 %shard_map.294 = (f32[384,256]{1,0:T(8,128)}, f32[768,1024]{1,0:T(8,128)}) custom-call(bf16[768,1024]{1,0:T(8,128)(2,1)} %copy-done, bf16[2,4,768,384]{3,2,1,0:T(8,128)(2,1)} %get-tuple-element.63.grads_ref, bf16[1024,3072]{1,0:T(8,128)(2,1)} %bitcast.47), custom_call_target="tpu_custom_call" | custom-call | flops 9663676416 | bytes 100000000 | tf_op jit(solution)/shard_map/pallas_call | solution.py:1034
  498.4 3.8 fusion.12
  502.2 24.4 %shard_map.295 = (bf16[6,32,8,256]{3,2,1,0:T(8,128)(2,1)S(1)}, f32[24,128]{1,0:T(8,128)S(1)}) custom-call(s32[192]{0:T(256)S(1)} %select_reduce_fusion.held_ref, f32[48,8,256]{2,1,0:T(8,128)S(1)} %bitcast.39, f32[16,8,256]{2,1,0:T(8,128)S(1)} %bitcast.40, f32[64,8,256]{2,1,0:T(8,128)S(1)} %bitcast.37, f32[64,8,256]{2,1,0:T(8,128)S(1)} %bitcast.38, ...), custom_call_target="tpu_custom_call" | custom-call | tf_op jit(solution)/shard_map/pallas_call | solution.py:1246
  530.0 1.4 copy-done.10
  532.5 21.7 %shard_map.296 = (bf16[6,256,256]{2,1,0:T(8,128)(2,1)S(1)}, f32[6,256,256]{2,1,0:T(8,128)}, f32[6,256,256]{2,1,0:T(8,128)}, f32[6,256,256]{2,1,0:T(8,128)}, f32[...) custom-call(f32[1,1]{1,0:T(1,128)} %bitcast.20.factor_ref, ...), custom_call_target="tpu_custom_call" | custom-call | flops 12079595520 | bytes 23592960 | tf_op jit(solution)/shard_map/pallas_call | solution.py:190
  555.2 12.8 %all-to-all-start = ((bf16[6,32,8,256]{3,2,0,1:T(8,128)(2,1)}), bf16[6,32,8,256]{3,2,0,1:T(8,128)(2,1)}, u32[]{:S(2)}, u32[]{:S(2)}) async-start(bf16[6,32,8,256]{3,2,0,1:T(8,128)(2,1)} %copy.35), calls=%async_computation | async-start | bytes 1572864 | tf_op jit(solution)/shard_map/all_to_all | solution.py:1438
  568.0 1.9 copy-done.13
  569.9 55.1 %shard_map.298 = (f32[6,256,256]{2,1,0:T(8,128)}, f32[6,256,256]{2,1,0:T(8,128)}) custom-call(f32[12,256,256]{2,1,0:T(8,128)S(1)} %bitcast.42, f32[12,256,256]{2,1,0:T(8,128)} %bitcast.57), custom_call_target="tpu_custom_call" | custom-call | flops 40265318400 | bytes 9437184 | tf_op jit(solution)/shard_map/pallas_call | solution.py:251
  625.8 4.4 fusion.11
  631.4 1.9 shard_map.297
  (102 shorter events, 15.7 us)
Async XLA Ops:
  7.2 60.6 %copy-start.19 = (bf16[768,1024]{1,0:T(8,128)(2,1)S(1)}, bf16[768,1024]{1,0:T(8,128)(2,1)}, u32[]{:S(2)}) copy-start(bf16[768,1024]{1,0:T(8,128)(2,1)} %param.17) | copy-start | bytes 4718596
  7.2 198.6 %all-gather.3.cloned.1.call-start = ((), (), s32[]{:S(2)}) async-start(), calls=%async_computation.1 | async-start | bytes 2162688 | tf_op jit(solution)/shard_map/all_gather | solution.py:1368
  8.9 204.2 %all-gather.5.cloned.1.call-start = ((), (), s32[]{:S(2)}) async-start(), calls=%async_computation.2 | async-start | bytes 8650752 | tf_op jit(solution)/shard_map/all_gather | solution.py:1368
  64.2 5.0 copy-start.26
  68.1 9.8 %copy-start.24 = (f32[768]{0:T(1024)}, f32[768]{0:T(1024)S(1)}, u32[]{:S(2)}) copy-start(f32[768]{0:T(1024)S(1)} %broadcast_multiply_fusion.5) | copy-start | bytes 9220
  68.7 9.2 %copy-start.28 = (f32[768]{0:T(1024)}, f32[768]{0:T(1024)S(1)}, u32[]{:S(2)}) copy-start(f32[768]{0:T(1024)S(1)} %add_rsqrt_fusion.1) | copy-start | bytes 9220
  69.2 8.6 %copy-start = (bf16[768,1024]{1,0:T(8,128)(2,1)}, bf16[768,1024]{1,0:T(8,128)(2,1)S(1)}, u32[]{:S(2)}) copy-start(bf16[768,1024]{1,0:T(8,128)(2,1)S(1)} %fusion.6.acts_ref) | copy-start | bytes 4718596
  205.8 3.9 copy-start.16
  213.1 52.4 %copy-start.18 = (f32[768,1024]{1,0:T(8,128)S(1)}, f32[768,1024]{1,0:T(8,128)}, u32[]{:S(2)}) copy-start(f32[768,1024]{1,0:T(8,128)} %copy-done.17) | copy-start | bytes 9437188
  270.0 5.8 copy-start.22
  440.2 58.2 %copy-start.25 = (f32[768]{0:T(1024)S(1)}, f32[768]{0:T(1024)}, u32[]{:S(2)}) copy-start(f32[768]{0:T(1024)} %copy-done.24) | copy-start | bytes 9220
  440.2 58.2 %copy-start.27 = (f32[1024]{0:T(1024)S(1)}, f32[1024]{0:T(1024)}, u32[]{:S(2)}) copy-start(f32[1024]{0:T(1024)} %copy-done.26) | copy-start | bytes 12292
  440.2 58.2 %copy-start.29 = (f32[768]{0:T(1024)S(1)}, f32[768]{0:T(1024)}, u32[]{:S(2)}) copy-start(f32[768]{0:T(1024)} %copy-done.28) | copy-start | bytes 9220
  498.3 3.9 copy-start.5
  498.4 31.6 %copy-start.9 = (f32[6,256,256]{2,1,0:T(8,128)S(1)}, f32[6,256,256]{2,1,0:T(8,128)}, u32[]{:S(2)}) copy-start(f32[6,256,256]{2,1,0:T(8,128)} %first_ref.1) | copy-start | bytes 4718596
  555.2 75.0 %all-to-all-start = ((bf16[6,32,8,256]{3,2,0,1:T(8,128)(2,1)}), bf16[6,32,8,256]{3,2,0,1:T(8,128)(2,1)}, u32[]{:S(2)}, u32[]{:S(2)}) async-start(bf16[6,32,8,256]{3,2,0,1:T(8,128)(2,1)} %copy.35), calls=%async_computation | async-start | bytes 1572864 | tf_op jit(solution)/shard_map/all_to_all | solution.py:1438
  569.9 55.2 %copy-start.30 = (f32[2,32]{1,0:T(2,128)S(1)}, f32[2,32]{1,0:T(2,128)}, u32[]{:S(2)}) copy-start(f32[2,32]{1,0:T(2,128)} %param.25) | copy-start | bytes 772
  569.9 55.2 %copy-start.31 = (f32[2,32]{1,0:T(2,128)S(1)}, f32[2,32]{1,0:T(2,128)}, u32[]{:S(2)}) copy-start(f32[2,32]{1,0:T(2,128)} %param.26) | copy-start | bytes 772
  569.9 55.2 %copy-start.32 = (f32[2,32]{1,0:T(2,128)S(1)}, f32[2,32]{1,0:T(2,128)}, u32[]{:S(2)}) copy-start(f32[2,32]{1,0:T(2,128)} %param.27) | copy-start | bytes 772
  569.9 55.9 %copy-start.20 = (bf16[768,1024]{1,0:T(8,128)(2,1)S(1)}, bf16[768,1024]{1,0:T(8,128)(2,1)}, u32[]{:S(2)}) copy-start(bf16[768,1024]{1,0:T(8,128)(2,1)} %param.17) | copy-start | bytes 4718596
  625.7 5.7 copy-start.1
  625.7 5.7 copy-start.2
  625.8 5.7 copy-start.3
  625.8 5.7 copy-start.4
  (13 other events, 32.3 us)
Sparse Core Ops, SparseCore 0:
  11.5 62.9 all-gather.2
  78.0 95.9 all-gather.4

commit v8 on v7

--- a/solution.py
+++ b/solution.py
@@ -37,6 +37,7 @@
 GATHER_PACE = 6.0
 GATHER_DELAY = 30.0
 SETTLE_DELAY = 6.0
+TOGETHER = 2
 GELU = 0.7978845608
 CUBIC = 0.044715
 
@@ -200,6 +201,45 @@
     )(factor.reshape(1, 1), gradient, first_old, second_old, left_old, right_old, left_base, right_base)
 
 
+def eliminate(x_ref, j):
+    count, rows, lanes = x_ref.shape
+    tile = j // 8 * 8
+    sublane = lax.broadcasted_iota(jnp.int32, (1, 8, 1), 1)
+    spread = lambda column: jnp.broadcast_to(column, (count, 1, lanes))
+    pivots = [x_ref[:, j + k : j + k + 1, :] for k in range(TOGETHER)]
+    corner = [
+        [spread(pivots[k][:, :, j + q : j + q + 1]) for q in range(TOGETHER)]
+        for k in range(TOGETHER)
+    ]
+    scaled, factors = [], []
+    for k in range(TOGETHER):
+        inverse = 1.0 / corner[k][k]
+        scaled.append(pivots[k] * inverse)
+        factors.append({})
+        for q in range(k + 1, TOGETHER):
+            factor = corner[k][q] * inverse
+            factors[k][q] = factor
+            pivots[q] = pivots[q] - factor * pivots[k]
+            for t in range(q, TOGETHER):
+                corner[q][t] = corner[q][t] - factor * corner[k][t]
+
+    def below(old, masked):
+        parts = [old[:, :, j + k : j + k + 1] for k in range(TOGETHER)]
+        new = old
+        for k in range(TOGETHER):
+            part = jnp.broadcast_to(parts[k], old.shape)
+            for q in range(k):
+                part = part - parts[q] * factors[q][k]
+            parts[k] = part
+            kept = jnp.where(sublane > j + k - tile, part, 0.0) if masked else part
+            new = new - kept * scaled[k]
+        return new
+
+    x_ref[:, tile : tile + 8, :] = below(x_ref[:, tile : tile + 8, :], True)
+    for start in range(tile + 8, rows, 8):
+        x_ref[:, start : start + 8, :] = below(x_ref[:, start : start + 8, :], False)
+
+
 def renew_kernel(rows, gram_ref, turn_ref, left_ref, right_ref, x_ref, u_ref):
     count, order = gram_ref.shape[0], gram_ref.shape[1]
     eye = (
@@ -209,31 +249,25 @@
     sublane = lax.broadcasted_iota(jnp.int32, (1, 8, 1), 1)
     for low in range(0, order, rows):
         part = slice(low, low + rows)
-
-        def panel(at, carry, low=low, part=part):
-            row = jnp.concatenate([gram_ref[at, part, :], turn_ref[at, part, :]], 1)
+        edge = low // 128 * 128
+
+        def panel(at, carry, low=low, part=part, edge=edge):
+            row = jnp.concatenate([gram_ref[at, part, edge:], turn_ref[at, part, :]], 1)
             if low:
-                row = row - exact(u_ref[at, :low, part], u_ref[at, :low, :], TN)
-            u_ref[at, part, :] = row
-            x_ref[at] = jnp.concatenate([row[:, part], eye], 1)
+                row = row - exact(u_ref[at, :low, part], u_ref[at, :low, edge:], TN)
+            u_ref[at, part, edge:] = row
+            x_ref[at] = jnp.concatenate([row[:, low - edge : low - edge + rows], eye], 1)
             return carry
 
         lax.fori_loop(0, count, panel, 0, unroll=2)
-        for j in range(rows):
-            tile = j // 8 * 8
-            row = x_ref[:, j : j + 1, :]
-            row = row * (1.0 / row[:, :, j : j + 1])
-            top = x_ref[:, tile : tile + 8, :]
-            below = jnp.where(sublane > j - tile, top[:, :, j : j + 1], 0.0)
-            x_ref[:, tile : tile + 8, :] = top - below * row
-            if tile + 8 < rows:
-                rest = x_ref[:, tile + 8 :, :]
-                x_ref[:, tile + 8 :, :] = rest - rest[:, :, j : j + 1] * row
-
-        def solve(at, carry, part=part):
+        for j in range(0, rows, TOGETHER):
+            eliminate(x_ref, j)
+
+        def solve(at, carry, part=part, edge=edge):
             both = x_ref[at]
             diagonal = jnp.sum(both[:, :rows] * eye, 1, keepdims=True)
-            u_ref[at, part, :] = exact(both[:, rows:] * lax.rsqrt(diagonal), u_ref[at, part, :])
+            inverse = both[:, rows:] * lax.rsqrt(diagonal)
+            u_ref[at, part, edge:] = exact(inverse, u_ref[at, part, edge:])
             return carry
 
         lax.fori_loop(0, count, solve, 0, unroll=2)

time: 645 us -> 642 us (level)
  no operation moved by 1% of the time
where the time goes in v8:
time: 642 us; the launch traced here: 638 us
  Pallas kernels  562 us (88%)
  other arithmetic  26.8 us (4%)
  between operations  17.9 us (3%)
  starting transfers between devices  13.2 us (2%)
  local copies, waits for them, and re-layouts  11.4 us (2%)
  matrix products  6.9 us (1%)
    pallas_call x1, Pallas kernels, attend_backward(): pl.pallas_call(partial(attend_backward_kernel, safe, chunk, halves, (bits...  164 us
    pallas_call x1, Pallas kernels, attend(): pl.pallas_call(partial(attend_kernel, safe, chunk, halves, plan, slots),...  127 us
    pallas_call x1, Pallas kernels, settle(): pl.pallas_call(partial(settle_kernel, (bits, narrow_bits, plans, chunks))...  57.5 us
    pallas_call x1, Pallas kernels, feed_forward(): pl.pallas_call(partial(feed_kernel, deal), grid=(hidden // tile,), in_spe...  52 us
    pallas_call x1, Pallas kernels, renew_bases(): pl.pallas_call(partial(renew_kernel, rows), out_shape=[jax.ShapeDtypeStru...  51.9 us
    pallas_call x1, Pallas kernels, gather_bands(): pl.pallas_call(partial(gather_kernel, bits, narrow_bits, plans, chunks, l...  49.5 us
    pallas_call x1, Pallas kernels, ship(): pl.pallas_call(partial(ship_kernel, lax.axis_size('narrow')), in_specs=[p...  25.1 us
    pallas_call x1, Pallas kernels, soap_update(): pl.pallas_call(soap_kernel, grid=(slots,), in_specs=[pl.BlockSpec(memory_...  21.7 us
  transfers between devices with their start and end apart: 3, of which 0 were waited for; matrix products, arithmetic and copies ran while one was open for 3% of the time, Pallas kernels for 37%

profile of v8, /device:TPU:0, one launch (start us, length us, event | category | flops | bytes accessed | tf_op | source)
XLA Modules:
  0.0 638.4 jit_solution(17481441925347709728)
XLA Ops:
  7.2 1.7 convert_element_type.59
  9.0 1.8 convert_element_type.61
  10.8 1.7 convert_element_type.52.refs_0_
  13.7 49.5 %shard_map.288 = (bf16[4,2,2,2,2,2,8,3072]{7,6,5,4,3,2,1,0:T(8,128)(2,1)}, bf16[1,2,2,2,2,2,8,128]{7,6,5,4,3,2,1,0:T(8,128)(2,1)}) custom-call(bf16[4,8,3072]{2,1,0:T(8,128)(2,1)} %convert_element_type.52.refs_0_, bf16[1,8,128]{2,1,0:T(8,128)(2,1)} %pad_bitcast_fusion.refs_1_), custom_call_target="tpu_custom_call" | custom-call | bytes 100000000 | tf_op jit(solution)/shard_map/pallas_call | solution.py:572
  69.2 8.6 %shard_map.289 = (bf16[4,768,384]{2,1,0:T(8,128)(2,1)S(1)}, bf16[4,768,384]{2,1,0:T(8,128)(2,1)}) custom-call(bf16[768,1024]{1,0:T(8,128)(2,1)S(1)} %fusion.6.acts_ref, bf16[1024,3072]{1,0:T(8,128)(2,1)} %bitcast.44, bf16[1024,3072]{1,0:T(8,128)(2,1)} %bitcast.45, bf16[1024,3072]{1,0:T(8,128)(2,1)} %bitcast.46), custom_call_target="tpu_custom_call" | custom-call | flops 4831838208 | bytes 12582912 | tf_op jit(solution)/shard_map/pallas_call | solution.py:97
  77.8 126.9 %shard_map.290 = (bf16[2,3072,384]{2,1,0:T(8,128)(2,1)}, bf16[768,1024]{1,0:T(8,128)(2,1)S(1)}, bf16[2,3072,128]{2,1,0:T(8,128)(2,1)S(1)}, f32[2,2,3072]{2,1,0:T...) custom-call(s32[1]{0:T(128)S(6)} %copy.37.length_ref, bf16[4,768,384]{2,1,0:T(8,128)(2,1)S(1)} %get-tuple-element.52.refs_0_, ...), custom_call_target="tpu_custom_call" | custom-call | flops 38654705664 | bytes 12582912 | tf_op jit(solution)/shard_map/pallas_call | solution.py:757
  205.8 3.9 fusion.19
  210.3 1.3 copy-done.17
  211.6 1.6 multiply_convert_fusion.acts_ref
  213.2 52.0 %shard_map.291 = (bf16[768,1024]{1,0:T(8,128)(2,1)}, f32[768,1024]{1,0:T(8,128)}, bf16[32,4,128,256]{3,2,1,0:T(8,128)(2,1)}, bf16[32,512,256]{2,1,0:T(8,128)(2,1)}) custom-call(bf16[768,1024]{1,0:T(8,128)(2,1)} %multiply_convert_fusion.acts_ref, bf16[768,1024]{1,0:T(8,128)(2,1)} %grad_ref.1, f32[768,1024]{1,0:T(8,128)} %copy-done.17, ...), custom_call_target="tpu_custom_call" | custom-call | flops 38654705664 | bytes 33554432 | tf_op jit(solution)/shard_map/pallas_call | solution.py:1151
  265.2 3.2 multiply_reduce_fusion
  269.8 2.8 shard_map.292
  272.6 3.0 convolution_convert_fusion.d_merged
  275.6 164.3 %shard_map.293 = (bf16[2,4,768,384]{3,2,1,0:T(8,128)(2,1)}, f32[512,256]{1,0:T(8,128)}, f32[512,256]{1,0:T(8,128)}, f32[128,256]{1,0:T(8,128)}) custom-call(s32[1]{0:T(128)S(6)} %copy.37.length_ref, bf16[2,3072,384]{2,1,0:T(8,128)(2,1)} %get-tuple-element.58.scene_ref, bf16[2,3072,128]{2,1,0:T(8,128)(2,1)} %copy-done.15, f32[2,2,3072]{2,1,0:T(2,128)} %copy-done.16, ...), custom_call_target="tpu_custom_call" | custom-call | flops 96636764160 | bytes 12582912 | tf_op jit(solution)/shard_map/pallas_call | solution.py:963
  439.9 57.5 %shard_map.294 = (f32[384,256]{1,0:T(8,128)}, f32[768,1024]{1,0:T(8,128)}) custom-call(bf16[768,1024]{1,0:T(8,128)(2,1)} %copy-done, bf16[2,4,768,384]{3,2,1,0:T(8,128)(2,1)} %get-tuple-element.63.grads_ref, bf16[1024,3072]{1,0:T(8,128)(2,1)} %bitcast.47), custom_call_target="tpu_custom_call" | custom-call | flops 9663676416 | bytes 100000000 | tf_op jit(solution)/shard_map/pallas_call | solution.py:1068
  497.5 3.8 fusion.12
  501.3 25.1 %shard_map.295 = (bf16[6,32,8,256]{3,2,1,0:T(8,128)(2,1)S(1)}, f32[24,128]{1,0:T(8,128)S(1)}) custom-call(s32[192]{0:T(256)S(1)} %select_reduce_fusion.held_ref, f32[48,8,256]{2,1,0:T(8,128)S(1)} %bitcast.39, f32[16,8,256]{2,1,0:T(8,128)S(1)} %bitcast.40, f32[64,8,256]{2,1,0:T(8,128)S(1)} %bitcast.37, f32[64,8,256]{2,1,0:T(8,128)S(1)} %bitcast.38, ...), custom_call_target="tpu_custom_call" | custom-call | tf_op jit(solution)/shard_map/pallas_call | solution.py:1280
  529.9 1.4 copy-done.10
  532.4 21.7 %shard_map.296 = (bf16[6,256,256]{2,1,0:T(8,128)(2,1)S(1)}, f32[6,256,256]{2,1,0:T(8,128)}, f32[6,256,256]{2,1,0:T(8,128)}, f32[6,256,256]{2,1,0:T(8,128)}, f32[...) custom-call(f32[1,1]{1,0:T(1,128)} %bitcast.20.factor_ref, ...), custom_call_target="tpu_custom_call" | custom-call | flops 12079595520 | bytes 23592960 | tf_op jit(solution)/shard_map/pallas_call | solution.py:191
  555.0 13.1 %all-to-all-start = ((bf16[6,32,8,256]{3,2,0,1:T(8,128)(2,1)}), bf16[6,32,8,256]{3,2,0,1:T(8,128)(2,1)}, u32[]{:S(2)}, u32[]{:S(2)}) async-start(bf16[6,32,8,256]{3,2,0,1:T(8,128)(2,1)} %copy.35), calls=%async_computation | async-start | bytes 1572864 | tf_op jit(solution)/shard_map/all_to_all | solution.py:1472
  568.2 1.9 copy-done.13
  570.0 51.9 %shard_map.298 = (f32[6,256,256]{2,1,0:T(8,128)}, f32[6,256,256]{2,1,0:T(8,128)}) custom-call(f32[12,256,256]{2,1,0:T(8,128)S(1)} %bitcast.42, f32[12,256,256]{2,1,0:T(8,128)} %bitcast.57), custom_call_target="tpu_custom_call" | custom-call | flops 40265318400 | bytes 9437184 | tf_op jit(solution)/shard_map/pallas_call | solution.py:285
  622.7 4.4 fusion.11
  628.3 1.9 shard_map.297
  (102 shorter events, 15.7 us)
Async XLA Ops:
  7.2 60.6 %copy-start.19 = (bf16[768,1024]{1,0:T(8,128)(2,1)S(1)}, bf16[768,1024]{1,0:T(8,128)(2,1)}, u32[]{:S(2)}) copy-start(bf16[768,1024]{1,0:T(8,128)(2,1)} %param.17) | copy-start | bytes 4718596
  7.2 198.6 %all-gather.3.cloned.1.call-start = ((), (), s32[]{:S(2)}) async-start(), calls=%async_computation.1 | async-start | bytes 2162688 | tf_op jit(solution)/shard_map/all_gather | solution.py:1402
  8.9 204.2 %all-gather.5.cloned.1.call-start = ((), (), s32[]{:S(2)}) async-start(), calls=%async_computation.2 | async-start | bytes 8650752 | tf_op jit(solution)/shard_map/all_gather | solution.py:1402
  64.2 5.0 copy-start.26
  68.1 9.7 %copy-start.24 = (f32[768]{0:T(1024)}, f32[768]{0:T(1024)S(1)}, u32[]{:S(2)}) copy-start(f32[768]{0:T(1024)S(1)} %broadcast_multiply_fusion.5) | copy-start | bytes 9220
  68.7 9.2 %copy-start.28 = (f32[768]{0:T(1024)}, f32[768]{0:T(1024)S(1)}, u32[]{:S(2)}) copy-start(f32[768]{0:T(1024)S(1)} %add_rsqrt_fusion.1) | copy-start | bytes 9220
  69.2 8.6 %copy-start = (bf16[768,1024]{1,0:T(8,128)(2,1)}, bf16[768,1024]{1,0:T(8,128)(2,1)S(1)}, u32[]{:S(2)}) copy-start(bf16[768,1024]{1,0:T(8,128)(2,1)S(1)} %fusion.6.acts_ref) | copy-start | bytes 4718596
  205.8 3.9 copy-start.16
  213.2 52.0 %copy-start.18 = (f32[768,1024]{1,0:T(8,128)S(1)}, f32[768,1024]{1,0:T(8,128)}, u32[]{:S(2)}) copy-start(f32[768,1024]{1,0:T(8,128)} %copy-done.17) | copy-start | bytes 9437188
  269.8 5.8 copy-start.22
  439.9 57.6 %copy-start.25 = (f32[768]{0:T(1024)S(1)}, f32[768]{0:T(1024)}, u32[]{:S(2)}) copy-start(f32[768]{0:T(1024)} %copy-done.24) | copy-start | bytes 9220
  439.9 57.6 %copy-start.27 = (f32[1024]{0:T(1024)S(1)}, f32[1024]{0:T(1024)}, u32[]{:S(2)}) copy-start(f32[1024]{0:T(1024)} %copy-done.26) | copy-start | bytes 12292
  439.9 57.6 %copy-start.29 = (f32[768]{0:T(1024)S(1)}, f32[768]{0:T(1024)}, u32[]{:S(2)}) copy-start(f32[768]{0:T(1024)} %copy-done.28) | copy-start | bytes 9220
  497.4 3.9 copy-start.5
  497.5 32.4 %copy-start.9 = (f32[6,256,256]{2,1,0:T(8,128)S(1)}, f32[6,256,256]{2,1,0:T(8,128)}, u32[]{:S(2)}) copy-start(f32[6,256,256]{2,1,0:T(8,128)} %first_ref.1) | copy-start | bytes 4718596
  555.0 72.1 %all-to-all-start = ((bf16[6,32,8,256]{3,2,0,1:T(8,128)(2,1)}), bf16[6,32,8,256]{3,2,0,1:T(8,128)(2,1)}, u32[]{:S(2)}, u32[]{:S(2)}) async-start(bf16[6,32,8,256]{3,2,0,1:T(8,128)(2,1)} %copy.35), calls=%async_computation | async-start | bytes 1572864 | tf_op jit(solution)/shard_map/all_to_all | solution.py:1472
  570.0 51.9 %copy-start.30 = (f32[2,32]{1,0:T(2,128)S(1)}, f32[2,32]{1,0:T(2,128)}, u32[]{:S(2)}) copy-start(f32[2,32]{1,0:T(2,128)} %param.25) | copy-start | bytes 772
  570.0 51.9 %copy-start.31 = (f32[2,32]{1,0:T(2,128)S(1)}, f32[2,32]{1,0:T(2,128)}, u32[]{:S(2)}) copy-start(f32[2,32]{1,0:T(2,128)} %param.26) | copy-start | bytes 772
  570.0 51.9 %copy-start.32 = (f32[2,32]{1,0:T(2,128)S(1)}, f32[2,32]{1,0:T(2,128)}, u32[]{:S(2)}) copy-start(f32[2,32]{1,0:T(2,128)} %param.27) | copy-start | bytes 772
  570.0 52.6 %copy-start.20 = (bf16[768,1024]{1,0:T(8,128)(2,1)S(1)}, bf16[768,1024]{1,0:T(8,128)(2,1)}, u32[]{:S(2)}) copy-start(bf16[768,1024]{1,0:T(8,128)(2,1)} %param.17) | copy-start | bytes 4718596
  622.6 5.7 copy-start.1
  622.6 5.7 copy-start.2
  622.6 5.7 copy-start.3
  622.7 5.7 copy-start.4
  (13 other events, 32.3 us)
Sparse Core Ops, SparseCore 0:
  11.5 62.9 all-gather.2
  78.0 95.9 all-gather.4
